TPU v7x, 512 devices: a whole 4x4x16 slice. The times are simulated.
512 devices in a mesh: rows: 128 (over z, x, core), cols: 4 (over y).
Axes of the slice: x: 4, y: 4, z: 16, core: 2. Of those that a mesh axis runs over, the one named last changes fastest.
Arguments:
- gradients: bfloat16 [98304, 8192], P('rows', 'cols'), may hold values from -60 to 60, as said below
- projection: bfloat16 [8192, 256], P('cols'), may hold values from -0.0625 to 0.0625
Outputs:
- basis: float32 [98304, 256], P('rows')
- reduced: float32 [256, 8192], P('rows', 'cols')
Inputs may be any that keep to these rules, and one draw needn't show every extreme that they name: Real-valued gradients; entries independent given per-example and per-feature scales.
All inputs are finite; a program needn't handle non-finite values.
Results may differ from a plain program's by a relative error of at most 0.0012.
Values sent between devices are 32-bit elements; how exact they have to be, the bound alone decides.
No kernel may reach another device: no remote copies, remote signals or barrier semaphores. Data moves between devices by JAX's collectives and lax.ppermute only.
A program may use at most 64 MiB of HBM per device.

v0:
```python
import jax
import jax.numpy as jnp
from jax import lax
from jax.sharding import PartitionSpec as P


def on_device(gradients, projection):
    partial_value = jnp.dot(gradients, projection, preferred_element_type=jnp.float32)
    total_rows = gradients.shape[0] * lax.axis_size("rows")
    factor = float(total_rows) ** 0.5
    sketch = lax.psum(partial_value, "cols")
    local_gram = jnp.dot(sketch.T, sketch, precision=lax.Precision.HIGHEST)
    gram = lax.psum(local_gram, "rows")
    lower = jnp.linalg.cholesky(gram)
    basis = jax.scipy.linalg.solve_triangular(lower, sketch.T, lower=True).T * factor
    half = sketch.astype(jnp.bfloat16)
    groups = lax.axis_size("rows")
    width = half.shape[1] // groups
    moment_part = lax.psum_scatter(
        jnp.einsum("rk,rf->kf", half, gradients, preferred_element_type=jnp.float32),
        "rows",
        scatter_dimension=0,
        tiled=True,
    )
    moment = lax.all_gather(moment_part, "rows", axis=0, tiled=True)
    solved = jax.scipy.linalg.solve_triangular(lower, moment, lower=True)
    reduced = lax.dynamic_slice_in_dim(solved, lax.axis_index("rows") * width, width, 0)
    return (basis, reduced)


def solution(mesh):
    in_specs = (P("rows", "cols"), P("cols", None))
    out_specs = (P("rows", None), P("rows", "cols"))
    return jax.shard_map(
        on_device, mesh=mesh, in_specs=in_specs, out_specs=out_specs, check_vma=False
    )
```

profile of v0, /device:TPU:1, one launch (start us, length us, event | category | flops | bytes accessed | tf_op | source)
XLA Modules:
  0.0 599.2 jit_solution(13653765618705803354)
XLA Ops:
  7.2 1.8 copy-done
  9.1 3.1 fusion.17
  12.2 63.4 %all-reduce.6.cloned.1.call-done = f32[768,256]{1,0:T(8,128)} async-done(((f32[768,256]{1,0:T(8,128)}), f32[768,256]{1,0:T(8,128)}) %all-reduce.6.cloned.1.call-update) | async-done | bytes 786448 | tf_op jit(solution)/shard_map/psum | solution.py:11
  75.7 3.5 fusion.3
  79.2 2.2 fusion.18
  81.6 1.3 dynamic-slice.3
  83.5 350.2 %all-reduce.8.cloned.1.call-done = (f32[256,256]{0,1:T(8,128)}, f32[256,2048]{1,0:T(8,128)}) async-done(((f32[256,256]{0,1:T(8,128)}, f32[256,2048]{1,0:T(8,128)}), (f32[256,256]{0,1:T(8,128)}, f32[256,2048]{1,0:T(8,128)})) %all-reduce.8.cloned.1.call-update) | async-done | bytes 2359312 | tf_op jit(solution)/shard_map/psum | solution.py:13
  433.7 1.5 dynamic-slice_bitcast_fusion
  435.2 1.1 copy.8
  436.3 1.0 fusion.5
  437.3 0.7 copy-done.4
  438.0 11.7 %cholesky.50 = f32[128,128]{1,0:T(8,128)S(1)} custom-call(f32[128,128]{1,0:T(8,128)S(1)} %cholesky.118), custom_call_target="Cholesky" | custom-call | tf_op jit(solution)/shard_map/jit(cholesky)/cholesky | solution.py:14
  449.7 9.8 %custom-call.18 = f32[1,128,128]{1,2,0:T(8,128)S(1)} custom-call(f32[1,128,128]{2,1,0:T(8,128)S(1)} %get-tuple-element.31), custom_call_target="InvertDiagBlocksLowerTriangular" | custom-call | tf_op jit(solution)/shard_map/jit(cholesky)/cholesky | solution.py:14
  459.6 1.0 constant_dynamic-update-slice_fusion
  460.6 1.1 convolution_subtract_fusion.2
  461.7 11.7 %cholesky.105 = f32[128,128]{1,0:T(8,128)S(1)} custom-call(f32[128,128]{1,0:T(8,128)S(1)} %convolution_subtract_fusion.2), custom_call_target="Cholesky" | custom-call | tf_op jit(solution)/shard_map/jit(cholesky)/cholesky | solution.py:14
  475.3 1.0 select_select_fusion
  476.4 5.3 while.1
  477.2 2.0 bitcast_dynamic-update-slice_fusion.2
  479.7 2.0 bitcast_dynamic-update-slice_fusion.2
  481.7 20.5 %custom-call.19 = f32[2,128,128]{1,2,0:T(8,128)S(1)} custom-call(f32[2,128,128]{2,1,0:T(8,128)} %get-tuple-element.9), custom_call_target="InvertDiagBlocksLowerTriangular" | custom-call | tf_op jit(solution)/shard_map/jit(_solve_triangular)/triangular_solve | solution.py:15
  502.2 1.5 fusion.1
  503.7 1.8 convolution_subtract_fusion.1
  506.0 1.0 fusion
  507.0 2.3 copy.9
  509.3 66.9 %all-gather.3.cloned.1.call-done = f32[128,2,2048]{2,1,0:T(2,128)} async-done(((f32[1,2,2048]{2,1,0:T(2,128)}), f32[128,2,2048]{2,1,0:T(2,128)}) %all-gather.3.cloned.1.call-update) | async-done | bytes 2097168 | tf_op jit(solution)/shard_map/all_gather | solution.py:25
  576.2 3.0 fusion.16
  579.2 3.0 reshape.50
  582.1 3.2 fusion.9
  585.4 3.0 reshape.51
  588.3 2.6 convolution_subtract_fusion
  591.0 1.0 fusion.10
  (28 shorter events, 3.5 us)
Async XLA Ops:
  7.2 1.9 copy-start
  7.2 68.5 %all-reduce.6.cloned.1.call-start = ((), (), s32[]{:S(2)}) async-start(), calls=%async_computation | async-start | bytes 1572864 | tf_op jit(solution)/shard_map/psum | solution.py:11
  12.2 421.5 %all-reduce.8.cloned.1.call-start = ((), (), s32[]{:S(2)}) async-start(), calls=%async_computation.2 | async-start | bytes 4718592 | tf_op jit(solution)/shard_map/psum | solution.py:13
  75.7 3.5 copy-start.1
  81.4 494.8 %all-gather.3.cloned.1.call-start = ((), (), s32[]{:S(2)}) async-start(), calls=%async_computation.1 | async-start | bytes 2113536 | tf_op jit(solution)/shard_map/all_gather | solution.py:25
  437.3 0.7 copy-start.4
  473.5 1.8 copy-start.3
  588.3 3.7 copy-start.2
Sparse Core Ops, SparseCore 0:
  12.3 63.3 all-reduce.5
  81.5 352.1 all-reduce.7
  437.4 138.6 all-gather.2
where the time goes:
time: 600 us; the launch traced here: 599 us
  waiting for transfers between devices  481 us (80%)
  other arithmetic  58 us (10%)
  local copies, waits for them, and re-layouts  22.8 us (4%)
  matrix products  21.6 us (4%)
  between operations  15.7 us (3%)
    psum x1, waiting for transfers between devices, on_device(): gram = lax.psum(local_gram, 'rows')  350 us
    all_gather x1, waiting for transfers between devices, on_device(): moment = lax.all_gather(moment_part, 'rows', axis=0, tiled=True)  66.9 us
    psum x1, waiting for transfers between devices, on_device(): sketch = lax.psum(partial_value, 'cols')  63.4 us
    another operation x6, other arithmetic, on_device(): lower = jnp.linalg.cholesky(gram)  34 us
    another operation x3, other arithmetic, on_device(): jax.scipy.linalg.solve_triangular(lower, sketch.T, lower=True).T * factor  21.5 us
  transfers between devices with their start and end apart: 3, of which 3 were waited for; matrix products, arithmetic and copies ran while one was open for 12% of the time, Pallas kernels for 0%

commit v1 on v0

v1 whole, which is shorter than its diff:
```python
import jax
import jax.numpy as jnp
from jax import lax
from jax.sharding import Mesh
from jax.sharding import PartitionSpec as P

HIGHEST = lax.Precision.HIGHEST
ROWS = ("z", "x", "core")
NEAR = ("x", "core", "y")


def exchange(blocks, axes):
    return lax.all_to_all(blocks, axes, 0, 0)


def spread(block, axes):
    count = lax.axis_size(axes)
    return exchange(jnp.broadcast_to(block[None], (count, *block.shape)), axes)


def on_device(gradients, projection):
    rows, feats = gradients.shape
    rank = projection.shape[1]
    total_rows = rows * lax.axis_size(ROWS)
    factor = float(total_rows) ** 0.5

    with jax.named_scope("sketch"):
        partial = jnp.dot(gradients, projection, preferred_element_type=jnp.float32)
        groups = lax.axis_size("y")
        own = exchange(partial.reshape(groups, rows // groups, rank), "y").sum(0)
        sketch = spread(own, "y").reshape(rows, rank)

    with jax.named_scope("gram"):
        local = jnp.dot(own.T, own, precision=HIGHEST)
        near = lax.axis_size(NEAR)
        share = exchange(local.reshape(near, rank // near, rank), NEAR).sum(0)
        share = spread(share, "z").sum(0)
        gram = spread(share, NEAR).reshape(rank, rank)

    with jax.named_scope("factor"):
        lower = jnp.linalg.cholesky(gram)
        inverse = jax.scipy.linalg.solve_triangular(
            lower, jnp.eye(rank, dtype=jnp.float32), lower=True
        )

    with jax.named_scope("moment"):
        half = sketch.astype(jnp.bfloat16)
        cores, xs = lax.axis_size("core"), lax.axis_size("x")
        width = feats // (cores * xs)
        moment = jnp.stack(
            [
                jnp.einsum(
                    "rk,rf->kf",
                    half,
                    gradients[:, i * width : (i + 1) * width],
                    preferred_element_type=jnp.float32,
                )
                for i in range(cores * xs)
            ]
        ).reshape(cores, xs, rank, width)
        core = lax.axis_index("core")
        away = lax.dynamic_index_in_dim(moment, 1 - core, 0, keepdims=False)
        here = lax.dynamic_index_in_dim(moment, core, 0, keepdims=False)
        moment = here + lax.ppermute(away, "core", [(0, 1), (1, 0)])
        moment = exchange(moment, "x").sum(0)

    with jax.named_scope("reduced"):
        solved = jnp.dot(inverse, moment, precision=HIGHEST)
        members = lax.axis_size(ROWS)
        parts = exchange(solved.reshape(members, rank // members, width), ROWS)
        parts = parts.reshape(lax.axis_size("z"), xs, cores, rank // members, width).sum(0)
        reduced = parts.transpose(2, 1, 0, 3).reshape(rank // members, feats)

    with jax.named_scope("basis"):
        basis = jnp.dot(sketch, inverse.T, precision=HIGHEST) * factor
    return (basis, reduced)


def solution(mesh):
    devices = mesh.devices.reshape(16, 4, 2, 4)
    fine = Mesh(devices, ("z", "x", "core", "y"))
    in_specs = (P(ROWS, "y"), P("y", None))
    out_specs = (P(ROWS, None), P(ROWS, "y"))
    return jax.shard_map(
        on_device, mesh=fine, in_specs=in_specs, out_specs=out_specs, check_vma=False
    )
```

time: 600 us -> 220 us (0.37)
  waiting for transfers between devices: 481 us -> 48.1 us
  starting transfers between devices: 0.3 us -> 42.3 us
  blocking collectives: 0 us -> 31.7 us
  between operations: 15.7 us -> 2.1 us
  local copies, waits for them, and re-layouts: 22.8 us -> 14.4 us
    psum x2 -> x0, waiting for transfers between devices: 414 us -> none  [the longest x1 350 us: on_device(): gram = lax.psum(local_gram, 'rows')]
    all_gather x1 -> x0, waiting for transfers between devices: 66.9 us -> none  [on_device(): moment = lax.all_gather(moment_part, 'rows', axis=0, tiled=True)]
    all_to_all x0 -> x5, waiting for transfers between devices: none -> 48.1 us  [exchange(): return lax.all_to_all(blocks, axes, 0, 0)]
    all_to_all x0 -> x5, starting transfers between devices: none -> 39.9 us  [exchange(): return lax.all_to_all(blocks, axes, 0, 0)]
    all_to_all x0 -> x2, blocking collectives: none -> 31.7 us  [exchange(): return lax.all_to_all(blocks, axes, 0, 0)]
    another operation x6 -> x3, matrix products: 10.7 us -> 0.83 us  [on_device(): jax.scipy.linalg.solve_triangular(lower, jnp.eye(rank, dtype=jnp.float32)...]
    another operation x10 -> x7, local copies, waits for them, and re-layouts: 14.1 us -> 5.09 us  [the longest x3 8.94 us: on_device(): solved = jax.scipy.linalg.solve_triangular(lower, moment, lower=True)]
    dot_general x3 -> x12, matrix products: 8.75 us -> 17.5 us  [the longest x8 11.2 us: on_device(): jnp.einsum('rk,rf->kf', half, gradients[:, i * width:(i + 1) * width], pr...]
  transfers between devices with their start and end apart: 3 -> 6, of which waited for: 3 -> 5; matrix products, arithmetic and copies ran while one was open for 12% -> 37% of each run, Pallas kernels for 0% -> 0%
where the time goes in v1:
time: 220 us; the launch traced here: 218 us
  other arithmetic  58.5 us (27%)
  waiting for transfers between devices  48.1 us (22%)
  starting transfers between devices  42.3 us (19%)
  blocking collectives  31.7 us (14%)
  matrix products  20.5 us (9%)
  local copies, waits for them, and re-layouts  14.4 us (7%)
    all_to_all x5, waiting for transfers between devices, exchange(): return lax.all_to_all(blocks, axes, 0, 0)  48.1 us
    all_to_all x5, starting transfers between devices, exchange(): return lax.all_to_all(blocks, axes, 0, 0)  39.9 us
    another operation x6, other arithmetic, on_device(): lower = jnp.linalg.cholesky(gram)  34 us
    all_to_all x2, blocking collectives, exchange(): return lax.all_to_all(blocks, axes, 0, 0)  31.7 us
    another operation x4, other arithmetic, on_device(): jax.scipy.linalg.solve_triangular(lower, jnp.eye(rank, dtype=jnp.float32)...  21.2 us
    dot_general x8, matrix products, on_device(): jnp.einsum('rk,rf->kf', half, gradients[:, i * width:(i + 1) * width], pr...  11.2 us
    another operation x6, local copies, waits for them, and re-layouts  5.02 us
  transfers between devices with their start and end apart: 6, of which 5 were waited for; matrix products, arithmetic and copies ran while one was open for 37% of the time, Pallas kernels for 0%

profile of v1, /device:TPU:1, one launch (start us, length us, event | category | flops | bytes accessed | tf_op | source)
XLA Modules:
  0.0 217.9 jit_solution(13019680662848022511)
XLA Ops:
  0.6 1.2 copy-done
  1.9 2.9 %fusion.31 = f32[768,256]{1,0:T(8,128)S(1)} fusion(bf16[768,2048]{1,0:T(8,128)(2,1)} %param.2, bf16[2048,256]{1,0:T(8,128)(2,1)S(1)} %copy-done), kind=kOutput, calls=%fused_computation.64 | convolution fusion | flops 805306368 | bytes 4980736 | tf_op jit(solution)/shard_map/sketch/dot_general | solution.py:28
  4.7 13.2 %all_to_all.35 = f32[4,192,256]{2,1,0:T(8,128)S(1)} all-to-all(f32[4,192,256]{2,1,0:T(8,128)S(1)} %bitcast.101), channel_id=1, replica_groups=mesh['z'=16,'x'=4,'core'=2,'y'=4] {'y'}, dimensions={0} | all-to-all | bytes 1572864 | tf_op jit(solution)/shard_map/sketch/all_to_all | solution.py:13
  18.5 18.6 %all_to_all.36 = f32[32,8,256]{2,1,0:T(8,128)S(1)} all-to-all(f32[32,8,256]{2,1,0:T(8,128)S(1)} %fusion.19), channel_id=1, replica_groups=mesh['z'=16,'x'=4,'core'=2,'y'=4] {'x','core','y'}, dimensions={0} | all-to-all | bytes 524288 | tf_op jit(solution)/shard_map/gram/all_to_all | solution.py:13
  38.0 3.5 %all-to-all-start.1 = ((f32[4,192,256]{2,1,0:T(8,128)}), f32[4,192,256]{2,1,0:T(8,128)S(1)}, u32[]{:S(2)}, u32[]{:S(2)}) async-start(f32[4,192,256]{2,1,0:T(8,128)} %broadcast_in_dim.7), calls=%async_computation.1 | async-start | bytes 1572864 | tf_op jit(solution)/shard_map/sketch/all_to_all | solution.py:13
  41.6 11.7 %all-to-all-done.1 = f32[4,192,256]{2,1,0:T(8,128)S(1)} async-done(((f32[4,192,256]{2,1,0:T(8,128)}), f32[4,192,256]{2,1,0:T(8,128)S(1)}, u32[]{:S(2)}, u32[]{:S(2)}) %all-to-all-start.1) | async-done | bytes 786464 | tf_op jit(solution)/shard_map/sketch/all_to_all | solution.py:13
  53.9 14.9 %all-to-all-start.3 = ((f32[16,8,256]{2,1,0:T(8,128)}), f32[16,8,256]{2,1,0:T(8,128)S(1)}, u32[]{:S(2)}, u32[]{:S(2)}) async-start(f32[16,8,256]{2,1,0:T(8,128)} %broadcast_in_dim.8), calls=%async_computation.3 | async-start | bytes 262144 | tf_op jit(solution)/shard_map/gram/all_to_all | solution.py:13
  68.9 2.1 fusion.7
  71.0 2.0 fusion.6
  76.1 1.0 fusion.2
  78.1 2.7 %all-to-all-done.3 = f32[16,8,256]{2,1,0:T(8,128)S(1)} async-done(((f32[16,8,256]{2,1,0:T(8,128)}), f32[16,8,256]{2,1,0:T(8,128)S(1)}, u32[]{:S(2)}, u32[]{:S(2)}) %all-to-all-start.3) | async-done | bytes 131104 | tf_op jit(solution)/shard_map/gram/all_to_all | solution.py:13
  81.6 7.2 %all-to-all-start.4 = ((f32[32,8,256]{2,1,0:T(8,128)}), f32[32,8,256]{2,1,0:T(8,128)S(1)}, u32[]{:S(2)}, u32[]{:S(2)}) async-start(f32[32,8,256]{2,1,0:T(8,128)} %broadcast_in_dim.9), calls=%async_computation.4 | async-start | bytes 524288 | tf_op jit(solution)/shard_map/gram/all_to_all | solution.py:13
  88.8 2.0 fusion
  90.8 2.3 %dynamic-slice_bitcast_fusion = f32[4,256,256]{2,1,0:T(8,128)} fusion(f32[2,4,256,256]{3,2,1,0:T(8,128)} %bitcast.19, s32[]{:T(128)S(6)} %select_n.13), kind=kLoop, calls=%fused_computation.22 | loop fusion | bytes 2097156 | tf_op jit(solution)/shard_map/moment/jit(dynamic_index_in_dim)/squeeze | solution.py:62
  93.1 2.4 %collective-permute-start = (f32[4,256,256]{2,1,0:T(8,128)}, f32[4,256,256]{2,1,0:T(8,128)S(1)}, u32[]{:S(2)}, u32[]{:S(2)}) collective-permute-start(f32[4,256,256]{2,1,0:T(8,128)} %dynamic-slice_bitcast_fusion), channel_id=1, source_target_pairs={{0,4},{4,0},{1,5},{5,1},{2,6},{6,2},{3,7},{7,3},{8,12},{12,8},{9,1... | collective-permute-start | bytes 3145736 | tf_op jit(solution)/shard_map/moment/ppermute | solution.py:64
  95.5 2.2 all-to-all-done.4
  99.4 11.7 %cholesky.50 = f32[128,128]{1,0:T(8,128)S(1)} custom-call(f32[128,128]{1,0:T(8,128)S(1)} %cholesky.118), custom_call_target="Cholesky" | custom-call | tf_op jit(solution)/shard_map/factor/jit(cholesky)/cholesky | solution.py:41
  111.2 9.8 %custom-call.15 = f32[1,128,128]{1,2,0:T(8,128)S(1)} custom-call(f32[1,128,128]{2,1,0:T(8,128)S(1)} %get-tuple-element.23), custom_call_target="InvertDiagBlocksLowerTriangular" | custom-call | tf_op jit(solution)/shard_map/factor/jit(cholesky)/cholesky | solution.py:41
  121.0 1.0 constant_dynamic-update-slice_fusion
  122.0 1.1 convolution_subtract_fusion.1
  123.1 11.7 %cholesky.105 = f32[128,128]{1,0:T(8,128)S(1)} custom-call(f32[128,128]{1,0:T(8,128)S(1)} %convolution_subtract_fusion.1), custom_call_target="Cholesky" | custom-call | tf_op jit(solution)/shard_map/factor/jit(cholesky)/cholesky | solution.py:41
  136.8 5.2 %while.1 = (s32[]{:T(128)}, f32[256,256]{1,0:T(8,128)S(1)}, s32[2,2]{1,0:T(2,128)S(1)}, f32[2,128,128]{2,1,0:T(8,128)}, s32[]{:T(128)}) while((s32[]{:T(128)}, f32[256,256]{1,0:T(8,128)S(1)}, s32[2,2]{1,0:T(2,128)S(1)}, f32[2,128,128]{2,1,0:T(8,128)}, s32[]{:T(128)}) %tuple.27), condition=%wide.while_cond, body=%wide.while_body.sunk | while | flops 2 | bytes 132705 | solution.py:42
  137.6 1.9 bitcast_dynamic-update-slice_fusion.2
  140.1 1.9 bitcast_dynamic-update-slice_fusion.2
  142.1 21.1 %custom-call.16 = f32[2,128,128]{1,2,0:T(8,128)} custom-call(f32[2,128,128]{2,1,0:T(8,128)} %get-tuple-element.9), custom_call_target="InvertDiagBlocksLowerTriangular" | custom-call | tf_op jit(solution)/shard_map/factor/jit(_solve_triangular)/triangular_solve | solution.py:42
  163.2 2.3 %bitcast_add_fusion = f32[4,256,256]{2,1,0:T(8,128)} fusion(f32[4,256,256]{2,1,0:T(8,128)S(1)} %collective-permute-done, f32[2,4,256,256]{3,2,1,0:T(8,128)} %bitcast.19, s32[]{:T(128)S(6)} %select_n.12), kind=kLoop, calls=%fused_computation.21 | loop fusion | flops 262144 | bytes 3145732 | tf_op jit(solution)/shard_map/moment/add | solution.py:64
  165.5 3.6 %all-to-all-start.5 = ((f32[4,256,256]{2,1,0:T(8,128)}), f32[4,256,256]{2,1,0:T(8,128)S(1)}, u32[]{:S(2)}, u32[]{:S(2)}) async-start(f32[4,256,256]{2,1,0:T(8,128)} %bitcast_add_fusion), calls=%async_computation.5 | async-start | bytes 2097152 | tf_op jit(solution)/shard_map/moment/all_to_all | solution.py:13
  170.9 12.8 %all-to-all-done.5 = f32[4,256,256]{2,1,0:T(8,128)S(1)} async-done(((f32[4,256,256]{2,1,0:T(8,128)}), f32[4,256,256]{2,1,0:T(8,128)S(1)}, u32[]{:S(2)}, u32[]{:S(2)}) %all-to-all-start.5) | async-done | bytes 1048608 | tf_op jit(solution)/shard_map/moment/all_to_all | solution.py:13
  183.8 1.3 fusion.16
  186.1 10.7 %all-to-all-start.6 = ((f32[128,2,256]{2,1,0:T(2,128)}), f32[128,2,256]{2,1,0:T(2,128)S(1)}, u32[]{:S(2)}, u32[]{:S(2)}) async-start(f32[128,2,256]{2,1,0:T(2,128)} %copy.24), calls=%async_computation.6 | async-start | bytes 524288 | tf_op jit(solution)/shard_map/reduced/all_to_all | solution.py:13
  196.7 1.7 convolution_multiply_fusion
  198.4 18.8 %all-to-all-done.6 = f32[128,2,256]{2,1,0:T(2,128)S(1)} async-done(((f32[128,2,256]{2,1,0:T(2,128)}), f32[128,2,256]{2,1,0:T(2,128)S(1)}, u32[]{:S(2)}, u32[]{:S(2)}) %all-to-all-start.6) | async-done | bytes 262176 | tf_op jit(solution)/shard_map/reduced/all_to_all | solution.py:13
  (45 shorter events, 14.2 us)
Async XLA Ops:
  0.6 1.2 copy-start
  38.0 15.3 %all-to-all-start.1 = ((f32[4,192,256]{2,1,0:T(8,128)}), f32[4,192,256]{2,1,0:T(8,128)S(1)}, u32[]{:S(2)}, u32[]{:S(2)}) async-start(f32[4,192,256]{2,1,0:T(8,128)} %broadcast_in_dim.7), calls=%async_computation.1 | async-start | bytes 1572864 | tf_op jit(solution)/shard_map/sketch/all_to_all | solution.py:13
  53.9 26.9 %all-to-all-start.3 = ((f32[16,8,256]{2,1,0:T(8,128)}), f32[16,8,256]{2,1,0:T(8,128)S(1)}, u32[]{:S(2)}, u32[]{:S(2)}) async-start(f32[16,8,256]{2,1,0:T(8,128)} %broadcast_in_dim.8), calls=%async_computation.3 | async-start | bytes 262144 | tf_op jit(solution)/shard_map/gram/all_to_all | solution.py:13
  68.8 4.2 %copy-start.2 = (bf16[768,2048]{1,0:T(8,128)(2,1)S(1)}, bf16[768,2048]{1,0:T(8,128)(2,1)}, u32[]{:S(2)}) copy-start(bf16[768,2048]{1,0:T(8,128)(2,1)} %param.2) | copy-start | bytes 9437188
  81.6 16.1 %all-to-all-start.4 = ((f32[32,8,256]{2,1,0:T(8,128)}), f32[32,8,256]{2,1,0:T(8,128)S(1)}, u32[]{:S(2)}, u32[]{:S(2)}) async-start(f32[32,8,256]{2,1,0:T(8,128)} %broadcast_in_dim.9), calls=%async_computation.4 | async-start | bytes 524288 | tf_op jit(solution)/shard_map/gram/all_to_all | solution.py:13
  93.1 70.1 %collective-permute-start = (f32[4,256,256]{2,1,0:T(8,128)}, f32[4,256,256]{2,1,0:T(8,128)S(1)}, u32[]{:S(2)}, u32[]{:S(2)}) collective-permute-start(f32[4,256,256]{2,1,0:T(8,128)} %dynamic-slice_bitcast_fusion), channel_id=1, source_target_pairs={{0,4},{4,0},{1,5},{5,1},{2,6},{6,2},{3,7},{7,3},{8,12},{12,8},{9,1... | collective-permute-start | bytes 3145736 | tf_op jit(solution)/shard_map/moment/ppermute | solution.py:64
  165.5 3.7 %copy-start.1 = (f32[2,128,128]{1,2,0:T(8,128)S(1)}, f32[2,128,128]{1,2,0:T(8,128)}, u32[]{:S(2)}) copy-start(f32[2,128,128]{1,2,0:T(8,128)} %custom-call.16) | copy-start | bytes 393220
  165.5 18.2 %all-to-all-start.5 = ((f32[4,256,256]{2,1,0:T(8,128)}), f32[4,256,256]{2,1,0:T(8,128)S(1)}, u32[]{:S(2)}, u32[]{:S(2)}) async-start(f32[4,256,256]{2,1,0:T(8,128)} %bitcast_add_fusion), calls=%async_computation.5 | async-start | bytes 2097152 | tf_op jit(solution)/shard_map/moment/all_to_all | solution.py:13
  186.1 31.2 %all-to-all-start.6 = ((f32[128,2,256]{2,1,0:T(2,128)}), f32[128,2,256]{2,1,0:T(2,128)S(1)}, u32[]{:S(2)}, u32[]{:S(2)}) async-start(f32[128,2,256]{2,1,0:T(2,128)} %copy.24), calls=%async_computation.6 | async-start | bytes 524288 | tf_op jit(solution)/shard_map/reduced/all_to_all | solution.py:13

commit v2 on v1

v2 whole, which is shorter than its diff:
```python
import jax
import jax.numpy as jnp
from jax import lax
from jax.experimental import pallas as pl
from jax.experimental.pallas import tpu as pltpu
from jax.sharding import Mesh
from jax.sharding import PartitionSpec as P

HIGHEST = lax.Precision.HIGHEST
ROWS = ("z", "x", "core")
NEAR = ("x", "core", "y")
PANEL = 8
VMEM_LIMIT = 32 * 1024 * 1024


def exchange(blocks, axes):
    return lax.all_to_all(blocks, axes, 0, 0)


def spread(block, axes):
    count = lax.axis_size(axes)
    return exchange(jnp.broadcast_to(block[None], (count, *block.shape)), axes)


def dot(a, b, contract):
    return lax.dot_general(
        a,
        b,
        (contract, ((), ())),
        precision=HIGHEST,
        preferred_element_type=jnp.float32,
    )


def inverse_factor(square):
    n = square.shape[0]
    count = n // PANEL
    sub = lax.broadcasted_iota(jnp.int32, (PANEL, n), 0)
    lane = lax.broadcasted_iota(jnp.int32, (PANEL, n), 1)

    def wide(part):
        return jnp.broadcast_to(part, (PANEL, n))

    left = [square[PANEL * i : PANEL * (i + 1), :] for i in range(count)]
    right = [jnp.where(lane == sub + PANEL * i, 1.0, 0.0) for i in range(count)]
    done = []
    for k in range(count):
        columns = [
            [wide(left[i][:, PANEL * k + j : PANEL * k + j + 1]) for i in range(k, count)]
            for j in range(PANEL)
        ]
        pivots = None
        for j in range(PANEL):
            pivot = wide(columns[j][0][j : j + 1, :])
            pivots = pivot if pivots is None else jnp.where(sub == j, pivot, pivots)
            inverse = 1.0 / pivot
            left_row = wide(left[k][j : j + 1, :])
            right_row = wide(right[k][j : j + 1, :])
            later = [wide(columns[m][0][j : j + 1, :]) for m in range(j + 1, PANEL)]
            for i in range(k, count):
                if i == k and j == PANEL - 1:
                    continue
                scale = columns[j][i - k] * inverse
                if i == k:
                    scale = jnp.where(sub > j, scale, 0.0)
                left[i] = left[i] - scale * left_row
                right[i] = right[i] - scale * right_row
                for m in range(j + 1, PANEL):
                    columns[m][i - k] = columns[m][i - k] - scale * later[m - j - 1]
        done.append(right[k] * lax.rsqrt(pivots))
    return jnp.concatenate(done, 0)


def factor_kernel(gram, out):
    n = gram.shape[0] // 2
    top = inverse_factor(gram[:n, :n])
    low = dot(gram[n:, :n], top, ((1,), (1,)))
    bottom = inverse_factor(gram[n:, n:] - dot(low, low, ((1,), (1,))))
    out[:n, :n] = top
    out[:n, n:] = jnp.zeros((n, n), jnp.float32)
    out[n:, n:] = bottom
    out[n:, :n] = -dot(bottom, dot(low, top, ((1,), (0,))), ((1,), (0,)))


def factor(gram):
    return pl.pallas_call(
        factor_kernel,
        out_shape=jax.ShapeDtypeStruct(gram.shape, jnp.float32),
        in_specs=[pl.BlockSpec(memory_space=pltpu.VMEM)],
        out_specs=pl.BlockSpec(memory_space=pltpu.VMEM),
        compiler_params=pltpu.CompilerParams(vmem_limit_bytes=VMEM_LIMIT),
        cost_estimate=pl.CostEstimate(
            flops=10**10, bytes_accessed=2 * gram.size * 4, transcendentals=0
        ),
        name="factor",
    )(gram)


def moment_kernel(side, half, gradients, *refs):
    value = lax.dot_general(
        half[...],
        gradients[...],
        (((0,), (0,)), ((), ())),
        preferred_element_type=jnp.float32,
    )
    if len(refs) == 2:
        value = value + refs[0][0]
    refs[-1][0] = value


def moment_blocks(half, gradients, side, blocks, added=None):
    rows, rank = half.shape
    width = gradients.shape[1] // (2 * blocks)
    block = pl.BlockSpec((1, rank, width), lambda i, side: (i, 0, 0))
    return pl.pallas_call(
        moment_kernel,
        out_shape=jax.ShapeDtypeStruct((blocks, rank, width), jnp.float32),
        grid_spec=pltpu.PrefetchScalarGridSpec(
            num_scalar_prefetch=1,
            grid=(blocks,),
            in_specs=[
                pl.BlockSpec((rows, rank), lambda i, side: (0, 0)),
                pl.BlockSpec((rows, width), lambda i, side: (0, side[0] * blocks + i)),
            ]
            + ([] if added is None else [block]),
            out_specs=block,
        ),
        compiler_params=pltpu.CompilerParams(vmem_limit_bytes=VMEM_LIMIT),
        cost_estimate=pl.CostEstimate(
            flops=2 * rows * rank * width * blocks,
            bytes_accessed=rows * width * blocks * 2 + rank * width * blocks * 4,
            transcendentals=0,
        ),
        name="moment",
    )(*([side, half, gradients] + ([] if added is None else [added])))


def on_device(gradients, projection):
    rows, feats = gradients.shape
    rank = projection.shape[1]
    scale = float(rows * lax.axis_size(ROWS)) ** 0.5
    cores, xs = lax.axis_size("core"), lax.axis_size("x")
    core = lax.axis_index("core").astype(jnp.int32)

    with jax.named_scope("sketch"):
        partial = jnp.dot(gradients, projection, preferred_element_type=jnp.float32)
        groups = lax.axis_size("y")
        own = exchange(partial.reshape(groups, rows // groups, rank), "y").sum(0)
        sketch = spread(own, "y").reshape(rows, rank)

    with jax.named_scope("gram"):
        local = dot(own, own, ((0,), (0,)))
        near = lax.axis_size(NEAR)
        share = exchange(local.reshape(near, rank // near, rank), NEAR).sum(0)
        share = spread(share, "z").sum(0)
        gram = spread(share, NEAR).reshape(rank, rank)

    with jax.named_scope("factor"):
        inverse = factor(gram)

    with jax.named_scope("moment"):
        half = sketch.astype(jnp.bfloat16)
        away = moment_blocks(half, gradients, (1 - core)[None], xs)
        away = lax.ppermute(away, "core", [(0, 1), (1, 0)])
        moment = moment_blocks(half, gradients, core[None], xs, away)
        moment = exchange(moment, "x").sum(0)

    with jax.named_scope("reduced"):
        width = feats // (cores * xs)
        solved = dot(inverse, moment, ((1,), (0,)))
        members = lax.axis_size(ROWS)
        parts = exchange(solved.reshape(members, rank // members, width), ROWS)
        parts = parts.reshape(lax.axis_size("z"), xs, cores, rank // members, width).sum(0)
        reduced = parts.transpose(2, 1, 0, 3).reshape(rank // members, feats)

    with jax.named_scope("basis"):
        basis = dot(sketch, inverse, ((1,), (1,))) * scale
    return (basis, reduced)


def solution(mesh):
    devices = mesh.devices.reshape(16, 4, 2, 4)
    fine = Mesh(devices, ("z", "x", "core", "y"))
    in_specs = (P(ROWS, "y"), P("y", None))
    out_specs = (P(ROWS, None), P(ROWS, "y"))
    return jax.shard_map(
        on_device, mesh=fine, in_specs=in_specs, out_specs=out_specs, check_vma=False
    )
```

time: 220 us -> 156 us (0.71)
  other arithmetic: 58.5 us -> 2.17 us
  blocking collectives: 31.7 us -> 55 us
  matrix products: 20.5 us -> 6.28 us
  Pallas kernels: 0 us -> 14 us
  waiting for transfers between devices: 48.1 us -> 34.5 us
  starting transfers between devices: 42.3 us -> 30.8 us
  local copies, waits for them, and re-layouts: 14.4 us -> 10.7 us
    another operation x10 -> x0, other arithmetic: 55.1 us -> none  [the longest x6 34 us: on_device(): lower = jnp.linalg.cholesky(gram)]
    all_to_all x2 -> x3, blocking collectives: 31.7 us -> 55 us  [exchange(): return lax.all_to_all(blocks, axes, 0, 0)]
    all_to_all x5 -> x4, starting transfers between devices: 39.9 us -> 22.1 us  [exchange(): return lax.all_to_all(blocks, axes, 0, 0)]
    pallas_call x0 -> x3, Pallas kernels: none -> 14 us  [the longest x1 9.93 us: factor(): pl.pallas_call(factor_kernel, out_shape=jax.ShapeDtypeStruct(gram.shape,...]
    all_to_all x5 -> x4, waiting for transfers between devices: 48.1 us -> 34.5 us  [exchange(): return lax.all_to_all(blocks, axes, 0, 0)]
    dot_general x11 -> x3, matrix products: 14.6 us -> 3.41 us  [dot(): lax.dot_general(a, b, (contract, ((), ())), precision=HIGHEST, preferred_...]
    ppermute x1, starting transfers between devices: 2.4 us -> 8.68 us  [on_device(): away = lax.ppermute(away, 'core', [(0, 1), (1, 0)])]
    another operation x9 -> x0, local copies, waits for them, and re-layouts: 5.96 us -> none
  transfers between devices with their start and end apart: 6 -> 5, of which waited for: 5 -> 4; matrix products, arithmetic and copies ran while one was open for 37% -> 4% of each run, Pallas kernels for 0% -> 8%
where the time goes in v2:
time: 156 us; the launch traced here: 154 us
  blocking collectives  55 us (35%)
  waiting for transfers between devices  34.5 us (22%)
  starting transfers between devices  30.8 us (20%)
  Pallas kernels  14 us (9%)
  local copies, waits for them, and re-layouts  10.7 us (7%)
  matrix products  6.28 us (4%)
  other arithmetic  2.17 us (1%)
    all_to_all x3, blocking collectives, exchange(): return lax.all_to_all(blocks, axes, 0, 0)  55 us
    all_to_all x4, waiting for transfers between devices, exchange(): return lax.all_to_all(blocks, axes, 0, 0)  34.5 us
    all_to_all x4, starting transfers between devices, exchange(): return lax.all_to_all(blocks, axes, 0, 0)  22.1 us
    pallas_call x1, Pallas kernels, factor(): pl.pallas_call(factor_kernel, out_shape=jax.ShapeDtypeStruct(gram.shape,...  9.93 us
    ppermute x1, starting transfers between devices, on_device(): away = lax.ppermute(away, 'core', [(0, 1), (1, 0)])  8.68 us
    unnamed x16, local copies, waits for them, and re-layouts  5.84 us
    pallas_call x2, Pallas kernels, moment_blocks(): pl.pallas_call(moment_kernel, out_shape=jax.ShapeDtypeStruct((blocks, ran...  4.05 us
    dot_general x3, matrix products, dot(): lax.dot_general(a, b, (contract, ((), ())), precision=HIGHEST, preferred_...  3.41 us
  transfers between devices with their start and end apart: 5, of which 4 were waited for; matrix products, arithmetic and copies ran while one was open for 4% of the time, Pallas kernels for 8%

profile of v2, /device:TPU:1, one launch (start us, length us, event | category | flops | bytes accessed | tf_op | source)
XLA Modules:
  0.0 154.3 jit_solution(10941875899501623523)
XLA Ops:
  0.6 1.2 copy-done
  1.9 2.9 %fusion.6 = f32[768,256]{1,0:T(8,128)S(1)} fusion(bf16[768,2048]{1,0:T(8,128)(2,1)} %gradients.3, bf16[2048,256]{1,0:T(8,128)(2,1)S(1)} %copy-done), kind=kOutput, calls=%fused_computation.8 | convolution fusion | flops 805306368 | bytes 4980736 | tf_op jit(solution)/shard_map/sketch/dot_general | solution.py:146
  4.7 13.2 %all_to_all.35 = f32[4,192,256]{2,1,0:T(8,128)S(1)} all-to-all(f32[4,192,256]{2,1,0:T(8,128)S(1)} %bitcast.26), channel_id=1, replica_groups=mesh['z'=16,'x'=4,'core'=2,'y'=4] {'y'}, dimensions={0} | all-to-all | bytes 1572864 | tf_op jit(solution)/shard_map/sketch/all_to_all | solution.py:17
  18.0 1.0 broadcast_in_dim.10
  18.9 3.5 %all-to-all-start.1 = ((f32[4,192,256]{2,1,0:T(8,128)}), f32[4,192,256]{2,1,0:T(8,128)S(1)}, u32[]{:S(2)}, u32[]{:S(2)}) async-start(f32[4,192,256]{2,1,0:T(8,128)} %broadcast_in_dim.10), calls=%async_computation.1 | async-start | bytes 1572864 | tf_op jit(solution)/shard_map/sketch/all_to_all | solution.py:17
  22.4 0.8 copy.15
  23.2 7.5 %all-to-all-done.1 = f32[4,192,256]{2,1,0:T(8,128)S(1)} async-done(((f32[4,192,256]{2,1,0:T(8,128)}), f32[4,192,256]{2,1,0:T(8,128)S(1)}, u32[]{:S(2)}, u32[]{:S(2)}) %all-to-all-start.1) | async-done | bytes 786464 | tf_op jit(solution)/shard_map/sketch/all_to_all | solution.py:17
  30.8 0.8 copy-done.3
  31.6 1.9 %copy-done.1 = bf16[768,2048]{1,0:T(8,128)(2,1)S(1)} copy-done((bf16[768,2048]{1,0:T(8,128)(2,1)S(1)}, bf16[768,2048]{1,0:T(8,128)(2,1)}, u32[]{:S(2)}) %copy-start.1) | copy-done | bytes 3145752
  33.5 1.5 moment.2
  35.0 8.7 %collective-permute-start = (f32[4,256,256]{2,1,0:T(8,128)S(1)}, f32[4,256,256]{2,1,0:T(8,128)S(1)}, u32[]{:S(2)}, u32[]{:S(2)}) collective-permute-start(f32[4,256,256]{2,1,0:T(8,128)S(1)} %moment.2), channel_id=1, source_target_pairs={{0,4},{4,0},{1,5},{5,1},{2,6},{6,2},{3,7},{7,3},{8,12},{12,8},{9,1... | collective-permute-start | bytes 3145736 | tf_op jit(solution)/shard_map/moment/ppermute | solution.py:164
  43.7 0.4 fusion.2
  44.1 15.0 %all_to_all.36 = f32[32,8,256]{2,1,0:T(8,128)} all-to-all(f32[32,8,256]{2,1,0:T(8,128)S(1)} %fusion.2), channel_id=1, replica_groups=mesh['z'=16,'x'=4,'core'=2,'y'=4] {'x','core','y'}, dimensions={0} | all-to-all | bytes 524288 | tf_op jit(solution)/shard_map/gram/all_to_all | solution.py:17
  59.2 1.0 reduce_sum.46
  60.2 26.8 %all_to_all.37 = f32[16,8,256]{2,1,0:T(8,128)} all-to-all(f32[16,8,256]{2,1,0:T(8,128)S(1)} %broadcast_in_dim.11), channel_id=1, replica_groups=mesh['z'=16,'x'=4,'core'=2,'y'=4] {'z'}, dimensions={0} | all-to-all | bytes 262144 | tf_op jit(solution)/shard_map/gram/all_to_all | solution.py:17
  87.0 0.9 reduce_sum.47
  87.9 0.7 broadcast_in_dim.12
  88.6 7.9 %all-to-all-start.4 = ((f32[32,8,256]{2,1,0:T(8,128)}), f32[32,8,256]{2,1,0:T(8,128)}, u32[]{:S(2)}, u32[]{:S(2)}) async-start(f32[32,8,256]{2,1,0:T(8,128)} %broadcast_in_dim.12), calls=%async_computation.4 | async-start | bytes 524288 | tf_op jit(solution)/shard_map/gram/all_to_all | solution.py:17
  96.6 1.9 %copy-done.2 = bf16[768,2048]{1,0:T(8,128)(2,1)S(1)} copy-done((bf16[768,2048]{1,0:T(8,128)(2,1)S(1)}, bf16[768,2048]{1,0:T(8,128)(2,1)}, u32[]{:S(2)}) %copy-start.2) | copy-done | bytes 3145752
  98.4 2.5 %moment.3 = f32[4,256,256]{2,1,0:T(8,128)} custom-call(s32[1]{0:T(128)} %bitcast.6.side, bf16[768,256]{1,0:T(8,128)(2,1)S(1)} %bitcast_convert_fusion.half, bf16[768,2048]{1,0:T(8,128)(2,1)S(1)} %copy-done.2, f32[4,256,256]{2,1,0:T(8,128)S(1)} %collective-permute-done.refs_0_), custom_call_target="tpu_custom_call" | custom-call | flops 402653184 | bytes 2621440 | tf_op jit(solution)/shard_map/moment/moment/pallas_call | solution.py:115
  101.0 4.5 %all-to-all-done.4 = f32[32,8,256]{2,1,0:T(8,128)} async-done(((f32[32,8,256]{2,1,0:T(8,128)}), f32[32,8,256]{2,1,0:T(8,128)}, u32[]{:S(2)}, u32[]{:S(2)}) %all-to-all-start.4) | async-done | bytes 262176 | tf_op jit(solution)/shard_map/gram/all_to_all | solution.py:17
  105.5 3.5 %all-to-all-start.5 = ((f32[4,256,256]{2,1,0:T(8,128)}), f32[4,256,256]{2,1,0:T(8,128)S(1)}, u32[]{:S(2)}, u32[]{:S(2)}) async-start(f32[4,256,256]{2,1,0:T(8,128)} %moment.3), calls=%async_computation.5 | async-start | bytes 2097152 | tf_op jit(solution)/shard_map/moment/all_to_all | solution.py:17
  109.0 9.9 %factor.1 = f32[256,256]{1,0:T(8,128)S(1)} custom-call(f32[256,256]{1,0:T(8,128)} %bitcast.5.gram), custom_call_target="tpu_custom_call" | custom-call | flops 10000000000 | bytes 524288 | tf_op jit(solution)/shard_map/factor/factor/pallas_call | solution.py:86
  119.0 0.9 dot_general.23
  119.8 3.8 %all-to-all-done.5 = f32[4,256,256]{2,1,0:T(8,128)S(1)} async-done(((f32[4,256,256]{2,1,0:T(8,128)}), f32[4,256,256]{2,1,0:T(8,128)S(1)}, u32[]{:S(2)}, u32[]{:S(2)}) %all-to-all-start.5) | async-done | bytes 1048608 | tf_op jit(solution)/shard_map/moment/all_to_all | solution.py:17
  123.7 1.3 fusion
  125.0 0.9 copy.17
  125.9 7.2 %all-to-all-start.6 = ((f32[128,2,256]{2,1,0:T(2,128)}), f32[128,2,256]{2,1,0:T(2,128)S(1)}, u32[]{:S(2)}, u32[]{:S(2)}) async-start(f32[128,2,256]{2,1,0:T(2,128)} %copy.17), calls=%async_computation.6 | async-start | bytes 524288 | tf_op jit(solution)/shard_map/reduced/all_to_all | solution.py:17
  133.2 1.7 %convolution_multiply_fusion = f32[768,256]{1,0:T(8,128)} fusion(f32[768,256]{1,0:T(8,128)S(1)} %bitcast.23, f32[256,256]{1,0:T(8,128)S(1)} %factor.1), kind=kOutput, calls=%fused_computation | convolution fusion | flops 604176384 | bytes 1835008 | tf_op jit(solution)/shard_map/basis/dot_general | solution.py:26
  134.9 18.8 %all-to-all-done.6 = f32[128,2,256]{2,1,0:T(2,128)S(1)} async-done(((f32[128,2,256]{2,1,0:T(2,128)}), f32[128,2,256]{2,1,0:T(2,128)S(1)}, u32[]{:S(2)}, u32[]{:S(2)}) %all-to-all-start.6) | async-done | bytes 262176 | tf_op jit(solution)/shard_map/reduced/all_to_all | solution.py:17
  153.6 0.1 reduce_sum.49
  153.7 0.6 reshape.30
  (18 shorter events, 0.2 us)
Async XLA Ops:
  0.6 1.2 copy-start
  17.9 12.8 %copy-start.5 = (f32[192,256]{1,0:T(8,128)}, f32[192,256]{1,0:T(8,128)S(1)}, u32[]{:S(2)}) copy-start(f32[192,256]{1,0:T(8,128)S(1)} %reduce_sum.45) | copy-start | bytes 589828
  18.9 11.8 %all-to-all-start.1 = ((f32[4,192,256]{2,1,0:T(8,128)}), f32[4,192,256]{2,1,0:T(8,128)S(1)}, u32[]{:S(2)}, u32[]{:S(2)}) async-start(f32[4,192,256]{2,1,0:T(8,128)} %broadcast_in_dim.10), calls=%async_computation.1 | async-start | bytes 1572864 | tf_op jit(solution)/shard_map/sketch/all_to_all | solution.py:17
  30.7 0.9 copy-start.3
  30.7 13.0 %copy-start.7 = (f32[256,192]{1,0:T(8,128)S(1)}, f32[256,192]{1,0:T(8,128)}, u32[]{:S(2)}) copy-start(f32[256,192]{1,0:T(8,128)} %copy.15) | copy-start | bytes 589828
  31.6 1.9 %copy-start.1 = (bf16[768,2048]{1,0:T(8,128)(2,1)S(1)}, bf16[768,2048]{1,0:T(8,128)(2,1)}, u32[]{:S(2)}) copy-start(bf16[768,2048]{1,0:T(8,128)(2,1)} %gradients.3) | copy-start | bytes 9437188
  33.5 10.2 %copy-start.6 = (f32[192,256]{1,0:T(8,128)S(1)}, f32[192,256]{1,0:T(8,128)}, u32[]{:S(2)}) copy-start(f32[192,256]{1,0:T(8,128)} %copy-done.5) | copy-start | bytes 589828
  35.0 61.5 %collective-permute-start = (f32[4,256,256]{2,1,0:T(8,128)S(1)}, f32[4,256,256]{2,1,0:T(8,128)S(1)}, u32[]{:S(2)}, u32[]{:S(2)}) collective-permute-start(f32[4,256,256]{2,1,0:T(8,128)S(1)} %moment.2), channel_id=1, source_target_pairs={{0,4},{4,0},{1,5},{5,1},{2,6},{6,2},{3,7},{7,3},{8,12},{12,8},{9,1... | collective-permute-start | bytes 3145736 | tf_op jit(solution)/shard_map/moment/ppermute | solution.py:164
  88.6 16.9 %all-to-all-start.4 = ((f32[32,8,256]{2,1,0:T(8,128)}), f32[32,8,256]{2,1,0:T(8,128)}, u32[]{:S(2)}, u32[]{:S(2)}) async-start(f32[32,8,256]{2,1,0:T(8,128)} %broadcast_in_dim.12), calls=%async_computation.4 | async-start | bytes 524288 | tf_op jit(solution)/shard_map/gram/all_to_all | solution.py:17
  96.6 1.9 %copy-start.2 = (bf16[768,2048]{1,0:T(8,128)(2,1)S(1)}, bf16[768,2048]{1,0:T(8,128)(2,1)}, u32[]{:S(2)}) copy-start(bf16[768,2048]{1,0:T(8,128)(2,1)} %gradients.3) | copy-start | bytes 9437188
  105.5 18.1 %all-to-all-start.5 = ((f32[4,256,256]{2,1,0:T(8,128)}), f32[4,256,256]{2,1,0:T(8,128)S(1)}, u32[]{:S(2)}, u32[]{:S(2)}) async-start(f32[4,256,256]{2,1,0:T(8,128)} %moment.3), calls=%async_computation.5 | async-start | bytes 2097152 | tf_op jit(solution)/shard_map/moment/all_to_all | solution.py:17
  119.0 14.2 %copy-start.4 = (f32[4,192,256]{2,1,0:T(8,128)S(1)}, f32[4,192,256]{2,1,0:T(8,128)}, u32[]{:S(2)}) copy-start(f32[4,192,256]{2,1,0:T(8,128)} %copy-done.3) | copy-start | bytes 2359300
  125.9 27.7 %all-to-all-start.6 = ((f32[128,2,256]{2,1,0:T(2,128)}), f32[128,2,256]{2,1,0:T(2,128)S(1)}, u32[]{:S(2)}, u32[]{:S(2)}) async-start(f32[128,2,256]{2,1,0:T(2,128)} %copy.17), calls=%async_computation.6 | async-start | bytes 524288 | tf_op jit(solution)/shard_map/reduced/all_to_all | solution.py:17

commit v3 on v2

v3 whole, which is shorter than its diff:
```python
import jax
import jax.numpy as jnp
from jax import lax
from jax.experimental import pallas as pl
from jax.experimental.pallas import tpu as pltpu
from jax.sharding import Mesh
from jax.sharding import PartitionSpec as P

HIGHEST = lax.Precision.HIGHEST
ROWS = ("z", "x", "core")
NEAR = ("x", "core", "y")
PANEL = 8
VMEM_LIMIT = 8 * 1024 * 1024


def exchange(blocks, axes):
    return lax.all_to_all(blocks, axes, 0, 0)


def shifted(value, axis, by):
    count = lax.axis_size(axis)
    return lax.ppermute(value, axis, [(i, (i + by) % count) for i in range(count)])


def dot(a, b, contract):
    return lax.dot_general(
        a,
        b,
        (contract, ((), ())),
        precision=HIGHEST,
        preferred_element_type=jnp.float32,
    )


def inverse_factor(square):
    n = square.shape[0]
    count = n // PANEL
    sub = lax.broadcasted_iota(jnp.int32, (PANEL, n), 0)
    lane = lax.broadcasted_iota(jnp.int32, (PANEL, n), 1)

    def wide(part):
        return jnp.broadcast_to(part, (PANEL, n))

    left = [square[PANEL * i : PANEL * (i + 1), :] for i in range(count)]
    right = [jnp.where(lane == sub + PANEL * i, 1.0, 0.0) for i in range(count)]
    done = []
    for k in range(count):
        columns = [
            [wide(left[i][:, PANEL * k + j : PANEL * k + j + 1]) for i in range(k, count)]
            for j in range(PANEL)
        ]
        pivots = None
        for j in range(PANEL):
            pivot = wide(columns[j][0][j : j + 1, :])
            pivots = pivot if pivots is None else jnp.where(sub == j, pivot, pivots)
            inverse = 1.0 / pivot
            left_row = wide(left[k][j : j + 1, :])
            right_row = wide(right[k][j : j + 1, :])
            later = [wide(columns[m][0][j : j + 1, :]) for m in range(j + 1, PANEL)]
            for i in range(k, count):
                if i == k and j == PANEL - 1:
                    continue
                scale = columns[j][i - k] * inverse
                if i == k:
                    scale = jnp.where(sub > j, scale, 0.0)
                left[i] = left[i] - scale * left_row
                right[i] = right[i] - scale * right_row
                for m in range(j + 1, PANEL):
                    columns[m][i - k] = columns[m][i - k] - scale * later[m - j - 1]
        done.append(right[k] * lax.rsqrt(pivots))
    return jnp.concatenate(done, 0)


def call(kernel, name, flops, outs, *args, after=()):
    whole = pl.BlockSpec()
    smem = pl.BlockSpec(memory_space=pltpu.SMEM)
    moved = sum(a.size * a.dtype.itemsize for a in (*args, *outs))
    return pl.pallas_call(
        lambda *refs: kernel(*refs[len(after) :]),
        out_shape=outs,
        in_specs=[pl.BlockSpec(memory_space=pl.ANY)] * len(after)
        + [smem if a.ndim == 1 else whole for a in args],
        out_specs=[whole] * len(outs),
        compiler_params=pltpu.CompilerParams(vmem_limit_bytes=VMEM_LIMIT),
        cost_estimate=pl.CostEstimate(flops=flops, bytes_accessed=moved, transcendentals=0),
        name=name,
    )(*after, *args)


def f32(*shape):
    return jax.ShapeDtypeStruct(shape, jnp.float32)


def gram_kernel(parts, own, gram):
    total = jnp.sum(parts[...], 0)
    own[...] = total
    gram[...] = dot(total, total, ((0,), (0,))).reshape(gram.shape)


def tile_kernel(parts, tiles):
    total = jnp.sum(parts[...], 0)
    for i in range(tiles.shape[0]):
        tiles[i] = total


def factor_kernel(shares, out):
    gram = shares[...].reshape(out.shape)
    n = gram.shape[0] // 2
    top = inverse_factor(gram[:n, :n])
    low = dot(gram[n:, :n], top, ((1,), (1,)))
    bottom = inverse_factor(gram[n:, n:] - dot(low, low, ((1,), (1,))))
    out[:n, :n] = top
    out[:n, n:] = jnp.zeros((n, n), jnp.float32)
    out[n:, n:] = bottom
    out[n:, :n] = -dot(bottom, dot(low, top, ((1,), (0,))), ((1,), (0,)))


def place_kernel(mine, *refs):
    sketch, half = refs[-2:]
    count = len(refs) - 2
    size = refs[0].shape[0]
    for k in range(count):
        member = lax.rem(mine[0] + count - k, count)
        rows = pl.ds(pl.multiple_of(member * size, size), size)
        block = refs[k][...]
        sketch[rows, :] = block
        half[rows, :] = block.astype(half.dtype)


def solve_kernel(inverse, *refs):
    out = refs[-1]
    total = refs[0][...]
    for part in refs[1:-1]:
        total = total + part[...]
    out[...] = dot(inverse[...], total, ((1,), (0,))).reshape(out.shape)


def sketch_kernel(gradients, projection, partial, held, weights, sems):
    blocks, size, _ = partial.shape
    first = pltpu.make_async_copy(projection, weights, sems.at[blocks])
    first.start()
    copies = []
    for i in range(blocks):
        part = pl.ds(i * size, size)
        copies.append(
            pltpu.make_async_copy(gradients.at[part], held.at[part], sems.at[i])
        )
        copies[-1].start()
    first.wait()
    for i in range(blocks):
        copies[i].wait()
        partial[i] = jnp.dot(
            held[i * size : (i + 1) * size, :],
            weights[...],
            preferred_element_type=jnp.float32,
        )


def sketch_blocks(gradients, projection, blocks):
    rows, feats = gradients.shape
    rank = projection.shape[1]
    return pl.pallas_call(
        sketch_kernel,
        out_shape=[
            f32(blocks, rows // blocks, rank),
            jax.ShapeDtypeStruct(gradients.shape, gradients.dtype),
        ],
        in_specs=[pl.BlockSpec(memory_space=pltpu.HBM)] * 2,
        out_specs=[pl.BlockSpec(), pl.BlockSpec(memory_space=pltpu.VMEM)],
        scratch_shapes=[
            pltpu.VMEM(projection.shape, projection.dtype),
            pltpu.SemaphoreType.DMA((blocks + 1,)),
        ],
        compiler_params=pltpu.CompilerParams(vmem_limit_bytes=VMEM_LIMIT),
        cost_estimate=pl.CostEstimate(
            flops=2 * rows * feats * rank,
            bytes_accessed=2 * feats * (rows + rank),
            transcendentals=0,
        ),
        name="sketch",
    )(gradients, projection)


def moment_kernel(place, half, gradients, *refs):
    count = refs[-1].shape[0] if len(refs) == 1 else len(refs) - 1
    width = gradients.shape[1] // (2 * count)
    turned = half[...].T
    for i in range(count):
        block = place[0] * count + lax.rem(place[1] + i, count)
        columns = pl.ds(pl.multiple_of(block * width, width), width)
        value = jnp.dot(turned, gradients[:, columns], preferred_element_type=jnp.float32)
        if len(refs) == 1:
            refs[0][i] = value
        else:
            refs[1 + i][...] = value + refs[0][i]


def moment_blocks(half, gradients, place, count, added=None):
    rows, rank = half.shape
    width = gradients.shape[1] // (2 * count)
    vmem, whole = pl.BlockSpec(memory_space=pltpu.VMEM), pl.BlockSpec()
    outs = [f32(count, rank, width)] if added is None else [f32(rank, width)] * count
    args = [half, gradients] + ([] if added is None else [added])
    return pl.pallas_call(
        moment_kernel,
        out_shape=outs,
        in_specs=[pl.BlockSpec(memory_space=pltpu.SMEM), vmem, vmem]
        + [whole] * (len(args) - 2),
        out_specs=[whole] * len(outs),
        compiler_params=pltpu.CompilerParams(vmem_limit_bytes=VMEM_LIMIT),
        cost_estimate=pl.CostEstimate(
            flops=2 * rows * rank * width * count,
            bytes_accessed=rows * width * count * 2 + rank * width * count * 4,
            transcendentals=0,
        ),
        name="moment",
    )(place, *args)


def on_device(gradients, projection):
    rows, feats = gradients.shape
    rank = projection.shape[1]
    scale = float(rows * lax.axis_size(ROWS)) ** 0.5
    cores, xs = lax.axis_size("core"), lax.axis_size("x")
    core = lax.axis_index("core").astype(jnp.int32)

    near, members = lax.axis_size(NEAR), lax.axis_size(ROWS)
    zs, groups = lax.axis_size("z"), lax.axis_size("y")
    width = feats // (cores * xs)

    with jax.named_scope("sketch"):
        partial, held = sketch_blocks(gradients, projection, groups)
        parts = exchange(partial, "y")

    with jax.named_scope("gram"):
        own, shares = call(
            gram_kernel,
            "gram",
            12 * rows // groups * rank**2,
            [f32(rows // groups, rank), f32(near, rank // near, rank)],
            parts,
        )
        shares = exchange(shares, NEAR)

    with jax.named_scope("gather"):
        others = [shifted(own, "y", k) for k in range(1, groups)]
        mine = lax.axis_index("y").astype(jnp.int32)[None]
        sketch, half = call(
            place_kernel,
            "place",
            0,
            [f32(rows, rank), jax.ShapeDtypeStruct((rows, rank), jnp.bfloat16)],
            mine,
            own,
            *others,
            after=[shares],
        )

    with jax.named_scope("gram"):
        (shares,) = call(tile_kernel, "tile", 0, [f32(zs, rank // near, rank)], shares)
        shares = exchange(shares, "z")
        (shares,) = call(tile_kernel, "tile", 0, [f32(near, rank // near, rank)], shares)
        shares = exchange(shares, NEAR)

    with jax.named_scope("factor"):
        (inverse,) = call(factor_kernel, "factor", 10**10, [f32(rank, rank)], shares)

    with jax.named_scope("moment"):
        x = lax.axis_index("x").astype(jnp.int32)
        away = moment_blocks(half, held, jnp.stack([1 - core, x]), xs)[0]
        away = lax.ppermute(away, "core", [(0, 1), (1, 0)])
        moment = moment_blocks(half, held, jnp.stack([core, x]), xs, away)
        moment = [moment[0]] + [shifted(moment[k], "x", k) for k in range(1, xs)]

    with jax.named_scope("reduced"):
        (parts,) = call(
            solve_kernel,
            "solve",
            12 * rank**2 * width,
            [f32(members, rank // members, width)],
            inverse,
            *moment,
        )
        parts = exchange(parts, ROWS)
        parts = parts.reshape(zs, xs, cores, rank // members, width).sum(0)
        reduced = parts.transpose(2, 1, 0, 3).reshape(rank // members, feats)

    with jax.named_scope("basis"):
        basis = dot(sketch, inverse, ((1,), (1,))) * scale
    return (basis, reduced)


def solution(mesh):
    devices = mesh.devices.reshape(16, 4, 2, 4)
    fine = Mesh(devices, ("z", "x", "core", "y"))
    in_specs = (P(ROWS, "y"), P("y", None))
    out_specs = (P(ROWS, None), P(ROWS, "y"))
    return jax.shard_map(
        on_device, mesh=fine, in_specs=in_specs, out_specs=out_specs, check_vma=False
    )
```

time: 156 us -> 149 us (0.955)
  starting transfers between devices: 30.8 us -> 48 us
  blocking collectives: 55 us -> 40.3 us
  Pallas kernels: 14 us -> 20.8 us
  waiting for transfers between devices: 34.5 us -> 28.3 us
  matrix products: 6.28 us -> 1.7 us
  local copies, waits for them, and re-layouts: 10.7 us -> 7.05 us
  other arithmetic: 2.17 us -> 0.24 us
    ppermute x0 -> x6, starting transfers between devices: none -> 20.3 us  [shifted(): lax.ppermute(value, axis, [(i, (i + by) % count) for i in range(count)])]
    all_to_all x4 -> x3, waiting for transfers between devices: 34.5 us -> 18.8 us  [exchange(): return lax.all_to_all(blocks, axes, 0, 0)]
    all_to_all x3 -> x2, blocking collectives: 55 us -> 40.3 us  [exchange(): return lax.all_to_all(blocks, axes, 0, 0)]
    ppermute x0 -> x6, waiting for transfers between devices: none -> 9.54 us  [shifted(): lax.ppermute(value, axis, [(i, (i + by) % count) for i in range(count)])]
    pallas_call x3 -> x9, Pallas kernels: 14 us -> 20.8 us  [the longest x6 13.5 us: call(): pl.pallas_call(lambda *refs: kernel(*refs[len(after):]), out_shape=outs,...]
    ppermute x1, starting transfers between devices: 8.68 us -> 2.53 us  [on_device(): away = lax.ppermute(away, 'core', [(0, 1), (1, 0)])]
    all_to_all x4 -> x3, starting transfers between devices: 22.1 us -> 25.2 us  [exchange(): return lax.all_to_all(blocks, axes, 0, 0)]
    dot_general x1 -> x0, matrix products: 2.87 us -> none  [on_device(): partial = jnp.dot(gradients, projection, preferred_element_type=jnp.float32)]
  transfers between devices with their start and end apart: 5 -> 10, of which waited for: 4 -> 4; matrix products, arithmetic and copies ran while one was open for 4% -> 1% of each run, Pallas kernels for 8% -> 9%
where the time goes in v3:
time: 149 us; the launch traced here: 147 us
  starting transfers between devices  48 us (32%)
  blocking collectives  40.3 us (27%)
  waiting for transfers between devices  28.3 us (19%)
  Pallas kernels  20.8 us (14%)
  local copies, waits for them, and re-layouts  7.05 us (5%)
  matrix products  1.7 us (1%)
    all_to_all x2, blocking collectives, exchange(): return lax.all_to_all(blocks, axes, 0, 0)  40.3 us
    all_to_all x3, starting transfers between devices, exchange(): return lax.all_to_all(blocks, axes, 0, 0)  25.2 us
    ppermute x6, starting transfers between devices, shifted(): lax.ppermute(value, axis, [(i, (i + by) % count) for i in range(count)])  20.3 us
    all_to_all x3, waiting for transfers between devices, exchange(): return lax.all_to_all(blocks, axes, 0, 0)  18.8 us
    pallas_call x6, Pallas kernels, call(): pl.pallas_call(lambda *refs: kernel(*refs[len(after):]), out_shape=outs,...  13.5 us
    ppermute x6, waiting for transfers between devices, shifted(): lax.ppermute(value, axis, [(i, (i + by) % count) for i in range(count)])  9.54 us
    unnamed x18, local copies, waits for them, and re-layouts  6.41 us
    pallas_call x2, Pallas kernels, moment_blocks(): pl.pallas_call(moment_kernel, out_shape=outs, in_specs=[pl.BlockSpec(memo...  4.76 us
  transfers between devices with their start and end apart: 10, of which 4 were waited for; matrix products, arithmetic and copies ran while one was open for 1% of the time, Pallas kernels for 9%

profile of v3, /device:TPU:1, one launch (start us, length us, event | category | flops | bytes accessed | tf_op | source)
XLA Modules:
  0.0 147.2 jit_solution(6868827684249371327)
XLA Ops:
  0.6 1.9 %copy-done = bf16[768,2048]{1,0:T(8,128)(2,1)S(1)} copy-done((bf16[768,2048]{1,0:T(8,128)(2,1)S(1)}, bf16[768,2048]{1,0:T(8,128)(2,1)}, u32[]{:S(2)}) %copy-start) | copy-done | bytes 3145752
  2.5 1.2 copy-done.3
  3.7 2.5 %sketch.1 = (f32[4,192,256]{2,1,0:T(8,128)S(1)}, bf16[768,2048]{1,0:T(8,128)(2,1)S(1)}) custom-call(bf16[768,2048]{1,0:T(8,128)(2,1)S(1)} %copy-done, bf16[2048,256]{1,0:T(8,128)(2,1)S(1)} %copy-done.3), custom_call_target="tpu_custom_call" | custom-call | flops 805306368 | bytes 4194304 | tf_op jit(solution)/shard_map/sketch/sketch/pallas_call | solution.py:162
  6.3 13.2 %all_to_all.25.refs_0_ = f32[4,192,256]{2,1,0:T(8,128)S(1)} all-to-all(f32[4,192,256]{2,1,0:T(8,128)S(1)} %get-tuple-element.12), channel_id=1, replica_groups=mesh['z'=16,'x'=4,'core'=2,'y'=4] {'y'}, dimensions={0} | all-to-all | bytes 1572864 | tf_op jit(solution)/shard_map/sketch/all_to_all | solution.py:17
  19.4 0.4 gram.1
  19.9 0.7 copy-done.6
  20.6 0.7 copy-done.7
  21.3 10.0 %all-to-all-start.1 = ((f32[32,8,256]{2,1,0:T(8,128)}), f32[32,8,256]{2,1,0:T(8,128)S(1)}, u32[]{:S(2)}, u32[]{:S(2)}) async-start(f32[32,8,256]{2,1,0:T(8,128)} %copy-done.6), calls=%async_computation.1 | async-start | bytes 524288 | tf_op jit(solution)/shard_map/gram/all_to_all | solution.py:17
  31.2 4.5 %collective-permute-start.2 = (f32[192,256]{1,0:T(8,128)}, f32[192,256]{1,0:T(8,128)}, u32[]{:S(2)}, u32[]{:S(2)}) collective-permute-start(f32[192,256]{1,0:T(8,128)} %copy-done.7), channel_id=1, source_target_pairs={{0,3},{1,0},{2,1},{3,2},{4,7},{5,4},{6,5},{7,6},{8,11},{9,8},{10,9... | collective-permute-start | bytes 589832 | tf_op jit(solution)/shard_map/gather/ppermute | solution.py:22
  35.7 2.5 %collective-permute-start.1 = (f32[192,256]{1,0:T(8,128)}, f32[192,256]{1,0:T(8,128)}, u32[]{:S(2)}, u32[]{:S(2)}) collective-permute-start(f32[192,256]{1,0:T(8,128)} %copy-done.7), channel_id=1, source_target_pairs={{0,2},{1,3},{2,0},{3,1},{4,6},{5,7},{6,4},{7,5},{8,10},{9,11},{10,... | collective-permute-start | bytes 589832 | tf_op jit(solution)/shard_map/gather/ppermute | solution.py:22
  38.2 2.5 %collective-permute-start = (f32[192,256]{1,0:T(8,128)}, f32[192,256]{1,0:T(8,128)}, u32[]{:S(2)}, u32[]{:S(2)}) collective-permute-start(f32[192,256]{1,0:T(8,128)} %copy-done.7), channel_id=1, source_target_pairs={{0,1},{1,2},{2,3},{3,0},{4,5},{5,6},{6,7},{7,4},{8,9},{9,10},{10,1... | collective-permute-start | bytes 589832 | tf_op jit(solution)/shard_map/gather/ppermute | solution.py:22
  40.8 1.2 collective-permute-done.2.refs_5_
  42.0 3.2 %collective-permute-done.1.refs_4_ = f32[192,256]{1,0:T(8,128)} collective-permute-done((f32[192,256]{1,0:T(8,128)}, f32[192,256]{1,0:T(8,128)}, u32[]{:S(2)}, u32[]{:S(2)}) %collective-permute-start.1) | collective-permute-done | bytes 196640 | tf_op jit(solution)/shard_map/gather/ppermute | solution.py:22
  45.3 5.1 %collective-permute-done.refs_3_ = f32[192,256]{1,0:T(8,128)} collective-permute-done((f32[192,256]{1,0:T(8,128)}, f32[192,256]{1,0:T(8,128)}, u32[]{:S(2)}, u32[]{:S(2)}) %collective-permute-start) | collective-permute-done | bytes 196640 | tf_op jit(solution)/shard_map/gather/ppermute | solution.py:22
  50.4 0.9 copy-done.8
  51.3 1.2 place.1
  52.5 2.1 %moment.2 = f32[4,256,256]{2,1,0:T(8,128)} custom-call(s32[2]{0:T(128)S(1)} %pad_add_fusion.1.place, bf16[768,256]{1,0:T(8,128)(2,1)S(1)} %get-tuple-element.16.half, bf16[768,2048]{1,0:T(8,128)(2,1)S(1)} %get-tuple-element.17.gradients), custom_call_target="tpu_custom_call" | custom-call | flops 402653184 | bytes 2621440 | tf_op jit(solution)/shard_map/moment/moment/pallas_call | solution.py:204
  54.6 2.5 %collective-permute-start.3 = (f32[4,256,256]{2,1,0:T(8,128)}, f32[4,256,256]{2,1,0:T(8,128)}, u32[]{:S(2)}, u32[]{:S(2)}) collective-permute-start(f32[4,256,256]{2,1,0:T(8,128)} %moment.2), channel_id=1, source_target_pairs={{0,4},{4,0},{1,5},{5,1},{2,6},{6,2},{3,7},{7,3},{8,12},{12,8},{9,1... | collective-permute-start | bytes 3145736 | tf_op jit(solution)/shard_map/moment/ppermute | solution.py:271
  57.2 27.2 %all_to_all.26.refs_0_ = f32[16,8,256]{2,1,0:T(8,128)S(1)} all-to-all(f32[16,8,256]{2,1,0:T(8,128)S(1)} %tile.2), channel_id=1, replica_groups=mesh['z'=16,'x'=4,'core'=2,'y'=4] {'z'}, dimensions={0} | all-to-all | bytes 262144 | tf_op jit(solution)/shard_map/gram/all_to_all | solution.py:17
  84.4 0.8 tile.3
  85.1 6.6 %all-to-all-start.3 = ((f32[32,8,256]{2,1,0:T(8,128)}), f32[32,8,256]{2,1,0:T(8,128)}, u32[]{:S(2)}, u32[]{:S(2)}) async-start(f32[32,8,256]{2,1,0:T(8,128)} %tile.3), calls=%async_computation.3 | async-start | bytes 524288 | tf_op jit(solution)/shard_map/gram/all_to_all | solution.py:17
  91.9 1.0 copy-done.2
  92.9 2.6 %moment.3 = (f32[256,256]{1,0:T(8,128)S(1)}, f32[256,256]{1,0:T(8,128)}, f32[256,256]{1,0:T(8,128)}, f32[256,256]{1,0:T(8,128)}) custom-call(s32[2]{0:T(128)S(1)} %pad_add_fusion.place, bf16[768,256]{1,0:T(8,128)(2,1)S(1)} %copy-done.2, bf16[768,2048]{1,0:T(8,128)(2,1)S(1)} %get-tuple-element.17.gradients, f32[4,256,256]{2,1,0:T(8,128)} %collective-permute-done.3.refs_0_), custom_call_target="tpu_custom_call" | custom-call | flops 402653184 | bytes 2621440 | tf_op jit(solution)/shard_map/moment/moment/pallas_call | solution.py:204
  95.5 3.3 %collective-permute-start.4 = (f32[256,256]{1,0:T(8,128)}, f32[256,256]{1,0:T(8,128)S(1)}, u32[]{:S(2)}, u32[]{:S(2)}) collective-permute-start(f32[256,256]{1,0:T(8,128)} %get-tuple-element.19), channel_id=1, source_target_pairs={{0,8},{8,16},{16,24},{24,0},{1,9},{9,17},{17,25},{25,1},{2,10},{10... | collective-permute-start | bytes 786440 | tf_op jit(solution)/shard_map/moment/ppermute | solution.py:22
  98.8 4.4 %collective-permute-start.5 = (f32[256,256]{1,0:T(8,128)}, f32[256,256]{1,0:T(8,128)S(1)}, u32[]{:S(2)}, u32[]{:S(2)}) collective-permute-start(f32[256,256]{1,0:T(8,128)} %get-tuple-element.20), channel_id=1, source_target_pairs={{0,16},{8,24},{16,0},{24,8},{1,17},{9,25},{17,1},{25,9},{2,18},{10... | collective-permute-start | bytes 786440 | tf_op jit(solution)/shard_map/moment/ppermute | solution.py:22
  103.2 3.2 %collective-permute-start.6 = (f32[256,256]{1,0:T(8,128)}, f32[256,256]{1,0:T(8,128)S(1)}, u32[]{:S(2)}, u32[]{:S(2)}) collective-permute-start(f32[256,256]{1,0:T(8,128)} %get-tuple-element.21), channel_id=1, source_target_pairs={{0,24},{8,0},{16,8},{24,16},{1,25},{9,1},{17,9},{25,17},{2,26},{10... | collective-permute-start | bytes 786440 | tf_op jit(solution)/shard_map/moment/ppermute | solution.py:22
  106.4 9.9 %factor.1.refs_0_ = f32[256,256]{1,0:T(8,128)S(1)} custom-call(f32[32,8,256]{2,1,0:T(8,128)} %all-to-all-done.3.refs_0_), custom_call_target="tpu_custom_call" | custom-call | flops 10000000000 | bytes 524288 | tf_op jit(solution)/shard_map/factor/factor/pallas_call | solution.py:78
  116.3 1.1 solve.1
  117.5 8.5 %all-to-all-start.4 = ((f32[128,2,256]{2,1,0:T(2,128)}), f32[128,2,256]{2,1,0:T(2,128)S(1)}, u32[]{:S(2)}, u32[]{:S(2)}) async-start(f32[128,2,256]{2,1,0:T(2,128)} %solve.1), calls=%async_computation.4 | async-start | bytes 524288 | tf_op jit(solution)/shard_map/reduced/all_to_all | solution.py:17
  126.0 1.7 %convolution_multiply_fusion = f32[768,256]{1,0:T(8,128)} fusion(f32[768,256]{1,0:T(8,128)S(1)} %copy-done.5, f32[256,256]{1,0:T(8,128)S(1)} %factor.1.refs_0_), kind=kOutput, calls=%fused_computation | convolution fusion | flops 604176384 | bytes 1835008 | tf_op jit(solution)/shard_map/basis/dot_general | solution.py:26
  127.7 18.8 %all-to-all-done.4 = f32[128,2,256]{2,1,0:T(2,128)S(1)} async-done(((f32[128,2,256]{2,1,0:T(2,128)}), f32[128,2,256]{2,1,0:T(2,128)S(1)}, u32[]{:S(2)}, u32[]{:S(2)}) %all-to-all-start.4) | async-done | bytes 262176 | tf_op jit(solution)/shard_map/reduced/all_to_all | solution.py:17
  146.6 0.6 reshape.11
  (23 shorter events, 0.3 us)
Async XLA Ops:
  0.6 1.9 %copy-start = (bf16[768,2048]{1,0:T(8,128)(2,1)S(1)}, bf16[768,2048]{1,0:T(8,128)(2,1)}, u32[]{:S(2)}) copy-start(bf16[768,2048]{1,0:T(8,128)(2,1)} %gradients.1) | copy-start | bytes 9437188
  2.5 1.2 copy-start.3
  19.9 0.7 copy-start.6
  20.6 0.7 copy-start.7
  21.3 29.1 %all-to-all-start.1 = ((f32[32,8,256]{2,1,0:T(8,128)}), f32[32,8,256]{2,1,0:T(8,128)S(1)}, u32[]{:S(2)}, u32[]{:S(2)}) async-start(f32[32,8,256]{2,1,0:T(8,128)} %copy-done.6), calls=%async_computation.1 | async-start | bytes 524288 | tf_op jit(solution)/shard_map/gram/all_to_all | solution.py:17
  31.2 10.8 %collective-permute-start.2 = (f32[192,256]{1,0:T(8,128)}, f32[192,256]{1,0:T(8,128)}, u32[]{:S(2)}, u32[]{:S(2)}) collective-permute-start(f32[192,256]{1,0:T(8,128)} %copy-done.7), channel_id=1, source_target_pairs={{0,3},{1,0},{2,1},{3,2},{4,7},{5,4},{6,5},{7,6},{8,11},{9,8},{10,9... | collective-permute-start | bytes 589832 | tf_op jit(solution)/shard_map/gather/ppermute | solution.py:22
  35.7 9.5 %collective-permute-start.1 = (f32[192,256]{1,0:T(8,128)}, f32[192,256]{1,0:T(8,128)}, u32[]{:S(2)}, u32[]{:S(2)}) collective-permute-start(f32[192,256]{1,0:T(8,128)} %copy-done.7), channel_id=1, source_target_pairs={{0,2},{1,3},{2,0},{3,1},{4,6},{5,7},{6,4},{7,5},{8,10},{9,11},{10,... | collective-permute-start | bytes 589832 | tf_op jit(solution)/shard_map/gather/ppermute | solution.py:22
  38.2 12.1 %collective-permute-start = (f32[192,256]{1,0:T(8,128)}, f32[192,256]{1,0:T(8,128)}, u32[]{:S(2)}, u32[]{:S(2)}) collective-permute-start(f32[192,256]{1,0:T(8,128)} %copy-done.7), channel_id=1, source_target_pairs={{0,1},{1,2},{2,3},{3,0},{4,5},{5,6},{6,7},{7,4},{8,9},{9,10},{10,1... | collective-permute-start | bytes 589832 | tf_op jit(solution)/shard_map/gather/ppermute | solution.py:22
  50.4 0.9 copy-start.8
  52.5 4.7 %copy-start.1 = (bf16[768,256]{1,0:T(8,128)(2,1)}, bf16[768,256]{1,0:T(8,128)(2,1)S(1)}, u32[]{:S(2)}) copy-start(bf16[768,256]{1,0:T(8,128)(2,1)S(1)} %get-tuple-element.16.half) | copy-start | bytes 1179652
  52.5 31.9 %copy-start.4 = (f32[768,256]{1,0:T(8,128)}, f32[768,256]{1,0:T(8,128)S(1)}, u32[]{:S(2)}) copy-start(f32[768,256]{1,0:T(8,128)S(1)} %get-tuple-element.15) | copy-start | bytes 2359300
  54.6 37.2 %collective-permute-start.3 = (f32[4,256,256]{2,1,0:T(8,128)}, f32[4,256,256]{2,1,0:T(8,128)}, u32[]{:S(2)}, u32[]{:S(2)}) collective-permute-start(f32[4,256,256]{2,1,0:T(8,128)} %moment.2), channel_id=1, source_target_pairs={{0,4},{4,0},{1,5},{5,1},{2,6},{6,2},{3,7},{7,3},{8,12},{12,8},{9,1... | collective-permute-start | bytes 3145736 | tf_op jit(solution)/shard_map/moment/ppermute | solution.py:271
  85.1 21.2 %all-to-all-start.3 = ((f32[32,8,256]{2,1,0:T(8,128)}), f32[32,8,256]{2,1,0:T(8,128)}, u32[]{:S(2)}, u32[]{:S(2)}) async-start(f32[32,8,256]{2,1,0:T(8,128)} %tile.3), calls=%async_computation.3 | async-start | bytes 524288 | tf_op jit(solution)/shard_map/gram/all_to_all | solution.py:17
  91.9 1.0 copy-start.2
  95.5 20.8 %collective-permute-start.4 = (f32[256,256]{1,0:T(8,128)}, f32[256,256]{1,0:T(8,128)S(1)}, u32[]{:S(2)}, u32[]{:S(2)}) collective-permute-start(f32[256,256]{1,0:T(8,128)} %get-tuple-element.19), channel_id=1, source_target_pairs={{0,8},{8,16},{16,24},{24,0},{1,9},{9,17},{17,25},{25,1},{2,10},{10... | collective-permute-start | bytes 786440 | tf_op jit(solution)/shard_map/moment/ppermute | solution.py:22
  98.8 17.5 %collective-permute-start.5 = (f32[256,256]{1,0:T(8,128)}, f32[256,256]{1,0:T(8,128)S(1)}, u32[]{:S(2)}, u32[]{:S(2)}) collective-permute-start(f32[256,256]{1,0:T(8,128)} %get-tuple-element.20), channel_id=1, source_target_pairs={{0,16},{8,24},{16,0},{24,8},{1,17},{9,25},{17,1},{25,9},{2,18},{10... | collective-permute-start | bytes 786440 | tf_op jit(solution)/shard_map/moment/ppermute | solution.py:22
  103.2 22.8 %copy-start.5 = (f32[768,256]{1,0:T(8,128)S(1)}, f32[768,256]{1,0:T(8,128)}, u32[]{:S(2)}) copy-start(f32[768,256]{1,0:T(8,128)} %copy-done.4) | copy-start | bytes 2359300
  103.2 13.2 %collective-permute-start.6 = (f32[256,256]{1,0:T(8,128)}, f32[256,256]{1,0:T(8,128)S(1)}, u32[]{:S(2)}, u32[]{:S(2)}) collective-permute-start(f32[256,256]{1,0:T(8,128)} %get-tuple-element.21), channel_id=1, source_target_pairs={{0,24},{8,0},{16,8},{24,16},{1,25},{9,1},{17,9},{25,17},{2,26},{10... | collective-permute-start | bytes 786440 | tf_op jit(solution)/shard_map/moment/ppermute | solution.py:22
  117.5 29.0 %all-to-all-start.4 = ((f32[128,2,256]{2,1,0:T(2,128)}), f32[128,2,256]{2,1,0:T(2,128)S(1)}, u32[]{:S(2)}, u32[]{:S(2)}) async-start(f32[128,2,256]{2,1,0:T(2,128)} %solve.1), calls=%async_computation.4 | async-start | bytes 524288 | tf_op jit(solution)/shard_map/reduced/all_to_all | solution.py:17

commit v4 on v3

--- a/solution.py
+++ b/solution.py
@@ -1,3 +1,5 @@
+import math
+
 import jax
 import jax.numpy as jnp
 from jax import lax
@@ -10,6 +12,7 @@
 ROWS = ("z", "x", "core")
 NEAR = ("x", "core", "y")
 PANEL = 8
+SHORT = 3 * 10**10
 VMEM_LIMIT = 8 * 1024 * 1024
 
 
@@ -71,24 +74,27 @@
     return jnp.concatenate(done, 0)
 
 
-def call(kernel, name, flops, outs, *args, after=()):
+def call(kernel, name, flops, outs, *args):
     whole = pl.BlockSpec()
     smem = pl.BlockSpec(memory_space=pltpu.SMEM)
-    moved = sum(a.size * a.dtype.itemsize for a in (*args, *outs))
+    moved = sum(math.prod(a.shape) * a.dtype.itemsize for a in (*args, *outs))
     return pl.pallas_call(
-        lambda *refs: kernel(*refs[len(after) :]),
+        kernel,
         out_shape=outs,
-        in_specs=[pl.BlockSpec(memory_space=pl.ANY)] * len(after)
-        + [smem if a.ndim == 1 else whole for a in args],
+        in_specs=[smem if a.ndim == 1 else whole for a in args],
         out_specs=[whole] * len(outs),
         compiler_params=pltpu.CompilerParams(vmem_limit_bytes=VMEM_LIMIT),
         cost_estimate=pl.CostEstimate(flops=flops, bytes_accessed=moved, transcendentals=0),
         name=name,
-    )(*after, *args)
+    )(*args)
 
 
 def f32(*shape):
     return jax.ShapeDtypeStruct(shape, jnp.float32)
+
+
+def far(*shape):
+    return pltpu.HBM(shape, jnp.float32)
 
 
 def gram_kernel(parts, own, gram):
@@ -127,11 +133,8 @@
         half[rows, :] = block.astype(half.dtype)
 
 
-def solve_kernel(inverse, *refs):
-    out = refs[-1]
-    total = refs[0][...]
-    for part in refs[1:-1]:
-        total = total + part[...]
+def solve_kernel(inverse, parts, out):
+    total = jnp.sum(parts[...], 0)
     out[...] = dot(inverse[...], total, ((1,), (0,))).reshape(out.shape)
 
 
@@ -178,35 +181,32 @@
             transcendentals=0,
         ),
         name="sketch",
-    )(gradients, projection)
-
-
-def moment_kernel(place, half, gradients, *refs):
-    count = refs[-1].shape[0] if len(refs) == 1 else len(refs) - 1
-    width = gradients.shape[1] // (2 * count)
+    )(
+        pltpu.with_memory_space_constraint(gradients, pltpu.HBM),
+        pltpu.with_memory_space_constraint(projection, pltpu.HBM),
+    )
+
+
+def moment_kernel(side, half, gradients, *refs):
+    out = refs[-1]
+    count, _, width = out.shape
     turned = half[...].T
     for i in range(count):
-        block = place[0] * count + lax.rem(place[1] + i, count)
-        columns = pl.ds(pl.multiple_of(block * width, width), width)
+        columns = pl.ds(pl.multiple_of((side[0] * count + i) * width, width), width)
         value = jnp.dot(turned, gradients[:, columns], preferred_element_type=jnp.float32)
-        if len(refs) == 1:
-            refs[0][i] = value
-        else:
-            refs[1 + i][...] = value + refs[0][i]
-
-
-def moment_blocks(half, gradients, place, count, added=None):
+        out[i] = value if len(refs) == 1 else value + refs[0][i]
+
+
+def moment_blocks(half, gradients, side, count, *added):
     rows, rank = half.shape
     width = gradients.shape[1] // (2 * count)
     vmem, whole = pl.BlockSpec(memory_space=pltpu.VMEM), pl.BlockSpec()
-    outs = [f32(count, rank, width)] if added is None else [f32(rank, width)] * count
-    args = [half, gradients] + ([] if added is None else [added])
     return pl.pallas_call(
         moment_kernel,
-        out_shape=outs,
-        in_specs=[pl.BlockSpec(memory_space=pltpu.SMEM), vmem, vmem]
-        + [whole] * (len(args) - 2),
-        out_specs=[whole] * len(outs),
+        out_shape=far(count, rank, width),
+        in_specs=[pl.BlockSpec(memory_space=pltpu.SMEM), whole, vmem]
+        + [whole] * len(added),
+        out_specs=whole,
         compiler_params=pltpu.CompilerParams(vmem_limit_bytes=VMEM_LIMIT),
         cost_estimate=pl.CostEstimate(
             flops=2 * rows * rank * width * count,
@@ -214,7 +214,7 @@
             transcendentals=0,
         ),
         name="moment",
-    )(place, *args)
+    )(side, half, gradients, *added)
 
 
 def on_device(gradients, projection):
@@ -237,10 +237,13 @@
             gram_kernel,
             "gram",
             12 * rows // groups * rank**2,
-            [f32(rows // groups, rank), f32(near, rank // near, rank)],
+            [far(rows // groups, rank), far(near, rank // near, rank)],
             parts,
         )
         shares = exchange(shares, NEAR)
+
+    with jax.named_scope("gram"):
+        (shares,) = call(tile_kernel, "tile", SHORT, [far(zs, rank // near, rank)], shares)
 
     with jax.named_scope("gather"):
         others = [shifted(own, "y", k) for k in range(1, groups)]
@@ -248,29 +251,27 @@
         sketch, half = call(
             place_kernel,
             "place",
-            0,
-            [f32(rows, rank), jax.ShapeDtypeStruct((rows, rank), jnp.bfloat16)],
+            SHORT,
+            [far(rows, rank), jax.ShapeDtypeStruct((rows, rank), jnp.bfloat16)],
             mine,
             own,
             *others,
-            after=[shares],
         )
 
     with jax.named_scope("gram"):
-        (shares,) = call(tile_kernel, "tile", 0, [f32(zs, rank // near, rank)], shares)
         shares = exchange(shares, "z")
-        (shares,) = call(tile_kernel, "tile", 0, [f32(near, rank // near, rank)], shares)
+        (shares,) = call(
+            tile_kernel, "tile", SHORT, [far(near, rank // near, rank)], shares
+        )
         shares = exchange(shares, NEAR)
 
     with jax.named_scope("factor"):
         (inverse,) = call(factor_kernel, "factor", 10**10, [f32(rank, rank)], shares)
 
     with jax.named_scope("moment"):
-        x = lax.axis_index("x").astype(jnp.int32)
-        away = moment_blocks(half, held, jnp.stack([1 - core, x]), xs)[0]
+        away = moment_blocks(half, held, (1 - core)[None], xs)
         away = lax.ppermute(away, "core", [(0, 1), (1, 0)])
-        moment = moment_blocks(half, held, jnp.stack([core, x]), xs, away)
-        moment = [moment[0]] + [shifted(moment[k], "x", k) for k in range(1, xs)]
+        moment = exchange(moment_blocks(half, held, core[None], xs, away), "x")
 
     with jax.named_scope("reduced"):
         (parts,) = call(
@@ -279,7 +280,7 @@
             12 * rank**2 * width,
             [f32(members, rank // members, width)],
             inverse,
-            *moment,
+            moment,
         )
         parts = exchange(parts, ROWS)
         parts = parts.reshape(zs, xs, cores, rank // members, width).sum(0)

time: 149 us -> 136 us (0.913)
  blocking collectives: 40.3 us -> 13.2 us
  starting transfers between devices: 48 us -> 59.1 us
  local copies, waits for them, and re-layouts: 7.05 us -> 1.56 us
  waiting for transfers between devices: 28.3 us -> 33.4 us
  Pallas kernels: 20.8 us -> 24.8 us
    all_to_all x2 -> x1, blocking collectives: 40.3 us -> 13.2 us  [exchange(): return lax.all_to_all(blocks, axes, 0, 0)]
    all_to_all x3 -> x5, starting transfers between devices: 25.2 us -> 46.2 us  [exchange(): return lax.all_to_all(blocks, axes, 0, 0)]
    all_to_all x3 -> x5, waiting for transfers between devices: 18.8 us -> 33.4 us  [exchange(): return lax.all_to_all(blocks, axes, 0, 0)]
    ppermute x6 -> x3, starting transfers between devices: 20.3 us -> 9.48 us  [shifted(): lax.ppermute(value, axis, [(i, (i + by) % count) for i in range(count)])]
    ppermute x6 -> x3, waiting for transfers between devices: 9.54 us -> 0.01 us  [shifted(): lax.ppermute(value, axis, [(i, (i + by) % count) for i in range(count)])]
    unnamed x18 -> x4, local copies, waits for them, and re-layouts: 6.41 us -> 0.93 us
    pallas_call x8, Pallas kernels: 18.2 us -> 21.1 us  [the longest x6 16.7 us: call(): pl.pallas_call(kernel, out_shape=outs, in_specs=[smem if a.ndim == 1 else...]
  transfers between devices with their start and end apart: 10 -> 9, of which waited for: 4 -> 4; matrix products, arithmetic and copies ran while one was open for 1% -> 1% of each run, Pallas kernels for 9% -> 14%
where the time goes in v4:
time: 136 us; the launch traced here: 135 us
  starting transfers between devices  59.1 us (43%)
  waiting for transfers between devices  33.4 us (25%)
  Pallas kernels  24.8 us (18%)
  blocking collectives  13.2 us (10%)
  matrix products  1.7 us (1%)
  local copies, waits for them, and re-layouts  1.56 us (1%)
    all_to_all x5, starting transfers between devices, exchange(): return lax.all_to_all(blocks, axes, 0, 0)  46.2 us
    all_to_all x5, waiting for transfers between devices, exchange(): return lax.all_to_all(blocks, axes, 0, 0)  33.4 us
    pallas_call x6, Pallas kernels, call(): pl.pallas_call(kernel, out_shape=outs, in_specs=[smem if a.ndim == 1 else...  16.7 us
    all_to_all x1, blocking collectives, exchange(): return lax.all_to_all(blocks, axes, 0, 0)  13.2 us
    ppermute x3, starting transfers between devices, shifted(): lax.ppermute(value, axis, [(i, (i + by) % count) for i in range(count)])  9.48 us
    pallas_call x2, Pallas kernels, moment_blocks(): pl.pallas_call(moment_kernel, out_shape=far(count, rank, width), in_specs...  4.43 us
    pallas_call x1, Pallas kernels, sketch_blocks(): pl.pallas_call(sketch_kernel, out_shape=[f32(blocks, rows // blocks, rank...  3.71 us
    ppermute x1, starting transfers between devices, on_device(): away = lax.ppermute(away, 'core', [(0, 1), (1, 0)])  3.37 us
  transfers between devices with their start and end apart: 9, of which 4 were waited for; matrix products, arithmetic and copies ran while one was open for 1% of the time, Pallas kernels for 14%

profile of v4, /device:TPU:1, one launch (start us, length us, event | category | flops | bytes accessed | tf_op | source)
XLA Modules:
  0.0 134.6 jit_solution(954889500355066332)
XLA Ops:
  0.6 3.7 %sketch.1 = (f32[4,192,256]{2,1,0:T(8,128)S(1)}, bf16[768,2048]{1,0:T(8,128)(2,1)S(1)}) custom-call(bf16[768,2048]{1,0:T(8,128)(2,1)} %gradients.1, bf16[2048,256]{1,0:T(8,128)(2,1)} %projection.1), custom_call_target="tpu_custom_call" | custom-call | flops 805306368 | bytes 4194304 | tf_op jit(solution)/shard_map/sketch/sketch/pallas_call | solution.py:165
  4.3 13.2 %all_to_all.30.parts = f32[4,192,256]{2,1,0:T(8,128)S(1)} all-to-all(f32[4,192,256]{2,1,0:T(8,128)S(1)} %get-tuple-element.8), channel_id=1, replica_groups=mesh['z'=16,'x'=4,'core'=2,'y'=4] {'y'}, dimensions={0} | all-to-all | bytes 1572864 | tf_op jit(solution)/shard_map/sketch/all_to_all | solution.py:20
  17.5 1.1 gram.1
  18.6 10.0 %all-to-all-start.1 = ((f32[32,8,256]{2,1,0:T(8,128)}), f32[32,8,256]{2,1,0:T(8,128)S(1)}, u32[]{:S(2)}, u32[]{:S(2)}) async-start(f32[32,8,256]{2,1,0:T(8,128)} %get-tuple-element.11), calls=%async_computation.1 | async-start | bytes 524288 | tf_op jit(solution)/shard_map/gram/all_to_all | solution.py:20
  28.6 4.5 %collective-permute-start.2 = (f32[192,256]{1,0:T(8,128)}, f32[192,256]{1,0:T(8,128)}, u32[]{:S(2)}, u32[]{:S(2)}) collective-permute-start(f32[192,256]{1,0:T(8,128)} %get-tuple-element.9.refs_0_), channel_id=1, source_target_pairs={{0,3},{1,0},{2,1},{3,2},{4,7},{5,4},{6,5},{7,6},{8,11},{9,8},{10,9... | collective-permute-start | bytes 589832 | tf_op jit(solution)/shard_map/gather/ppermute | solution.py:25
  33.1 2.5 %collective-permute-start.1 = (f32[192,256]{1,0:T(8,128)}, f32[192,256]{1,0:T(8,128)}, u32[]{:S(2)}, u32[]{:S(2)}) collective-permute-start(f32[192,256]{1,0:T(8,128)} %get-tuple-element.9.refs_0_), channel_id=1, source_target_pairs={{0,2},{1,3},{2,0},{3,1},{4,6},{5,7},{6,4},{7,5},{8,10},{9,11},{10,... | collective-permute-start | bytes 589832 | tf_op jit(solution)/shard_map/gather/ppermute | solution.py:25
  35.6 2.5 %collective-permute-start = (f32[192,256]{1,0:T(8,128)}, f32[192,256]{1,0:T(8,128)}, u32[]{:S(2)}, u32[]{:S(2)}) collective-permute-start(f32[192,256]{1,0:T(8,128)} %get-tuple-element.9.refs_0_), channel_id=1, source_target_pairs={{0,1},{1,2},{2,3},{3,0},{4,5},{5,6},{6,7},{7,4},{8,9},{9,10},{10,1... | collective-permute-start | bytes 589832 | tf_op jit(solution)/shard_map/gather/ppermute | solution.py:25
  38.1 0.0 all-to-all-done.1.parts
  38.1 0.7 tile.2
  38.8 15.0 %all-to-all-start.2 = ((f32[16,8,256]{2,1,0:T(8,128)}), f32[16,8,256]{2,1,0:T(8,128)}, u32[]{:S(2)}, u32[]{:S(2)}) async-start(f32[16,8,256]{2,1,0:T(8,128)} %tile.2), calls=%async_computation.2 | async-start | bytes 262144 | tf_op jit(solution)/shard_map/gram/all_to_all | solution.py:20
  53.8 0.0 collective-permute-done.2.refs_3_
  53.8 0.0 collective-permute-done.refs_1_
  53.8 0.9 copy-done
  54.8 2.1 %place.1 = (f32[768,256]{1,0:T(8,128)}, bf16[768,256]{1,0:T(8,128)(2,1)S(1)}) custom-call(s32[1]{0:T(128)} %bitcast.mine, f32[192,256]{1,0:T(8,128)S(1)} %copy-done, f32[192,256]{1,0:T(8,128)} %collective-permute-done.refs_1_, f32[192,256]{1,0:T(8,128)} %collective-permute-done.1.refs_2_, f32[192,256]{1,0:T(8,128)} %collective-permute-done.2.refs_3_), custom_call_target="tpu_custom_call" | custom-call | flops 30000001024 | bytes 1966084 | tf_op jit(solution)/shard_map/gather/place/pallas_call | solution.py:81
  56.8 1.6 %moment.2 = f32[4,256,256]{2,1,0:T(8,128)} custom-call(s32[1]{0:T(128)} %bitcast.2.side, bf16[768,256]{1,0:T(8,128)(2,1)S(1)} %get-tuple-element.12.half, bf16[768,2048]{1,0:T(8,128)(2,1)S(1)} %get-tuple-element.13.gradients), custom_call_target="tpu_custom_call" | custom-call | flops 402653184 | bytes 2621440 | tf_op jit(solution)/shard_map/moment/moment/pallas_call | solution.py:204
  58.4 3.4 %collective-permute-start.3 = (f32[4,256,256]{2,1,0:T(8,128)}, f32[4,256,256]{2,1,0:T(8,128)}, u32[]{:S(2)}, u32[]{:S(2)}) collective-permute-start(f32[4,256,256]{2,1,0:T(8,128)} %moment.2), channel_id=1, source_target_pairs={{0,4},{4,0},{1,5},{5,1},{2,6},{6,2},{3,7},{7,3},{8,12},{12,8},{9,1... | collective-permute-start | bytes 3145736 | tf_op jit(solution)/shard_map/moment/ppermute | solution.py:273
  61.8 4.0 %all-to-all-done.2.parts = f32[16,8,256]{2,1,0:T(8,128)} async-done(((f32[16,8,256]{2,1,0:T(8,128)}), f32[16,8,256]{2,1,0:T(8,128)}, u32[]{:S(2)}, u32[]{:S(2)}) %all-to-all-start.2) | async-done | bytes 131104 | tf_op jit(solution)/shard_map/gram/all_to_all | solution.py:20
  65.8 1.7 %tile.3 = f32[32,8,256]{2,1,0:T(8,128)} custom-call(f32[16,8,256]{2,1,0:T(8,128)} %all-to-all-done.2.parts), custom_call_target="tpu_custom_call" | custom-call | flops 30000001024 | bytes 393216 | tf_op jit(solution)/shard_map/gram/tile/pallas_call | solution.py:81
  67.5 9.9 %all-to-all-start.3 = ((f32[32,8,256]{2,1,0:T(8,128)}), f32[32,8,256]{2,1,0:T(8,128)}, u32[]{:S(2)}, u32[]{:S(2)}) async-start(f32[32,8,256]{2,1,0:T(8,128)} %tile.3), calls=%async_computation.3 | async-start | bytes 524288 | tf_op jit(solution)/shard_map/gram/all_to_all | solution.py:20
  77.4 0.0 collective-permute-done.3.refs_0_
  77.4 2.8 %moment.3 = f32[4,256,256]{2,1,0:T(8,128)} custom-call(s32[1]{0:T(128)} %bitcast.1.side, bf16[768,256]{1,0:T(8,128)(2,1)S(1)} %get-tuple-element.12.half, bf16[768,2048]{1,0:T(8,128)(2,1)S(1)} %get-tuple-element.13.gradients, f32[4,256,256]{2,1,0:T(8,128)} %collective-permute-done.3.refs_0_), custom_call_target="tpu_custom_call" | custom-call | flops 402653184 | bytes 2621440 | tf_op jit(solution)/shard_map/moment/moment/pallas_call | solution.py:204
  80.2 6.0 %all-to-all-done.3.shares = f32[32,8,256]{2,1,0:T(8,128)} async-done(((f32[32,8,256]{2,1,0:T(8,128)}), f32[32,8,256]{2,1,0:T(8,128)}, u32[]{:S(2)}, u32[]{:S(2)}) %all-to-all-start.3) | async-done | bytes 262176 | tf_op jit(solution)/shard_map/gram/all_to_all | solution.py:20
  86.2 3.5 %all-to-all-start.4 = ((f32[4,256,256]{2,1,0:T(8,128)}), f32[4,256,256]{2,1,0:T(8,128)S(1)}, u32[]{:S(2)}, u32[]{:S(2)}) async-start(f32[4,256,256]{2,1,0:T(8,128)} %moment.3), calls=%async_computation.4 | async-start | bytes 2097152 | tf_op jit(solution)/shard_map/moment/all_to_all | solution.py:20
  89.8 0.0 copy-start.1
  89.8 10.0 %factor.1.inverse = f32[256,256]{1,0:T(8,128)S(1)} custom-call(f32[32,8,256]{2,1,0:T(8,128)} %all-to-all-done.3.shares), custom_call_target="tpu_custom_call" | custom-call | flops 10000000000 | bytes 524288 | tf_op jit(solution)/shard_map/factor/factor/pallas_call | solution.py:81
  99.8 4.6 %all-to-all-done.4.parts = f32[4,256,256]{2,1,0:T(8,128)S(1)} async-done(((f32[4,256,256]{2,1,0:T(8,128)}), f32[4,256,256]{2,1,0:T(8,128)S(1)}, u32[]{:S(2)}, u32[]{:S(2)}) %all-to-all-start.4) | async-done | bytes 1048608 | tf_op jit(solution)/shard_map/moment/all_to_all | solution.py:20
  104.3 1.1 solve.1
  105.4 7.9 %all-to-all-start.5 = ((f32[128,2,256]{2,1,0:T(2,128)}), f32[128,2,256]{2,1,0:T(2,128)S(1)}, u32[]{:S(2)}, u32[]{:S(2)}) async-start(f32[128,2,256]{2,1,0:T(2,128)} %solve.1), calls=%async_computation.5 | async-start | bytes 524288 | tf_op jit(solution)/shard_map/reduced/all_to_all | solution.py:20
  113.4 1.7 %convolution_multiply_fusion = f32[768,256]{1,0:T(8,128)} fusion(f32[768,256]{1,0:T(8,128)S(1)} %copy-done.1, f32[256,256]{1,0:T(8,128)S(1)} %factor.1.inverse), kind=kOutput, calls=%fused_computation | convolution fusion | flops 604176384 | bytes 1835008 | tf_op jit(solution)/shard_map/basis/dot_general | solution.py:29
  115.1 18.8 %all-to-all-done.5 = f32[128,2,256]{2,1,0:T(2,128)S(1)} async-done(((f32[128,2,256]{2,1,0:T(2,128)}), f32[128,2,256]{2,1,0:T(2,128)S(1)}, u32[]{:S(2)}, u32[]{:S(2)}) %all-to-all-start.5) | async-done | bytes 262176 | tf_op jit(solution)/shard_map/reduced/all_to_all | solution.py:20
  133.8 0.1 reduce_sum.9
  133.9 0.6 reshape.11
  (4 shorter events, 0.0 us)
Async XLA Ops:
  18.6 19.5 %all-to-all-start.1 = ((f32[32,8,256]{2,1,0:T(8,128)}), f32[32,8,256]{2,1,0:T(8,128)S(1)}, u32[]{:S(2)}, u32[]{:S(2)}) async-start(f32[32,8,256]{2,1,0:T(8,128)} %get-tuple-element.11), calls=%async_computation.1 | async-start | bytes 524288 | tf_op jit(solution)/shard_map/gram/all_to_all | solution.py:20
  28.6 25.2 %collective-permute-start.2 = (f32[192,256]{1,0:T(8,128)}, f32[192,256]{1,0:T(8,128)}, u32[]{:S(2)}, u32[]{:S(2)}) collective-permute-start(f32[192,256]{1,0:T(8,128)} %get-tuple-element.9.refs_0_), channel_id=1, source_target_pairs={{0,3},{1,0},{2,1},{3,2},{4,7},{5,4},{6,5},{7,6},{8,11},{9,8},{10,9... | collective-permute-start | bytes 589832 | tf_op jit(solution)/shard_map/gather/ppermute | solution.py:25
  33.1 20.7 %collective-permute-start.1 = (f32[192,256]{1,0:T(8,128)}, f32[192,256]{1,0:T(8,128)}, u32[]{:S(2)}, u32[]{:S(2)}) collective-permute-start(f32[192,256]{1,0:T(8,128)} %get-tuple-element.9.refs_0_), channel_id=1, source_target_pairs={{0,2},{1,3},{2,0},{3,1},{4,6},{5,7},{6,4},{7,5},{8,10},{9,11},{10,... | collective-permute-start | bytes 589832 | tf_op jit(solution)/shard_map/gather/ppermute | solution.py:25
  35.6 18.2 %collective-permute-start = (f32[192,256]{1,0:T(8,128)}, f32[192,256]{1,0:T(8,128)}, u32[]{:S(2)}, u32[]{:S(2)}) collective-permute-start(f32[192,256]{1,0:T(8,128)} %get-tuple-element.9.refs_0_), channel_id=1, source_target_pairs={{0,1},{1,2},{2,3},{3,0},{4,5},{5,6},{6,7},{7,4},{8,9},{9,10},{10,1... | collective-permute-start | bytes 589832 | tf_op jit(solution)/shard_map/gather/ppermute | solution.py:25
  38.8 27.0 %all-to-all-start.2 = ((f32[16,8,256]{2,1,0:T(8,128)}), f32[16,8,256]{2,1,0:T(8,128)}, u32[]{:S(2)}, u32[]{:S(2)}) async-start(f32[16,8,256]{2,1,0:T(8,128)} %tile.2), calls=%async_computation.2 | async-start | bytes 262144 | tf_op jit(solution)/shard_map/gram/all_to_all | solution.py:20
  53.8 0.9 copy-start
  58.4 19.0 %collective-permute-start.3 = (f32[4,256,256]{2,1,0:T(8,128)}, f32[4,256,256]{2,1,0:T(8,128)}, u32[]{:S(2)}, u32[]{:S(2)}) collective-permute-start(f32[4,256,256]{2,1,0:T(8,128)} %moment.2), channel_id=1, source_target_pairs={{0,4},{4,0},{1,5},{5,1},{2,6},{6,2},{3,7},{7,3},{8,12},{12,8},{9,1... | collective-permute-start | bytes 3145736 | tf_op jit(solution)/shard_map/moment/ppermute | solution.py:273
  67.5 18.8 %all-to-all-start.3 = ((f32[32,8,256]{2,1,0:T(8,128)}), f32[32,8,256]{2,1,0:T(8,128)}, u32[]{:S(2)}, u32[]{:S(2)}) async-start(f32[32,8,256]{2,1,0:T(8,128)} %tile.3), calls=%async_computation.3 | async-start | bytes 524288 | tf_op jit(solution)/shard_map/gram/all_to_all | solution.py:20
  86.2 18.1 %all-to-all-start.4 = ((f32[4,256,256]{2,1,0:T(8,128)}), f32[4,256,256]{2,1,0:T(8,128)S(1)}, u32[]{:S(2)}, u32[]{:S(2)}) async-start(f32[4,256,256]{2,1,0:T(8,128)} %moment.3), calls=%async_computation.4 | async-start | bytes 2097152 | tf_op jit(solution)/shard_map/moment/all_to_all | solution.py:20
  89.8 23.6 %copy-start.1 = (f32[768,256]{1,0:T(8,128)S(1)}, f32[768,256]{1,0:T(8,128)}, u32[]{:S(2)}) copy-start(f32[768,256]{1,0:T(8,128)} %get-tuple-element.10) | copy-start | bytes 2359300
  105.4 28.4 %all-to-all-start.5 = ((f32[128,2,256]{2,1,0:T(2,128)}), f32[128,2,256]{2,1,0:T(2,128)S(1)}, u32[]{:S(2)}, u32[]{:S(2)}) async-start(f32[128,2,256]{2,1,0:T(2,128)} %solve.1), calls=%async_computation.5 | async-start | bytes 524288 | tf_op jit(solution)/shard_map/reduced/all_to_all | solution.py:20

commit v5 on v4

--- a/solution.py
+++ b/solution.py
@@ -1,3 +1,4 @@
+import functools
 import math
 
 import jax
@@ -9,8 +10,11 @@
 from jax.sharding import PartitionSpec as P
 
 HIGHEST = lax.Precision.HIGHEST
-ROWS = ("z", "x", "core")
+ROWS = ("far", "pair", "x", "core")
+DEEP = ("far", "pair")
+CROSS = ("pair", "x")
 NEAR = ("x", "core", "y")
+GROUPS = 4
 PANEL = 8
 SHORT = 3 * 10**10
 VMEM_LIMIT = 8 * 1024 * 1024
@@ -121,16 +125,18 @@
     out[n:, :n] = -dot(bottom, dot(low, top, ((1,), (0,))), ((1,), (0,)))
 
 
-def place_kernel(mine, *refs):
-    sketch, half = refs[-2:]
-    count = len(refs) - 2
+def members(place, refs):
+    count = len(refs)
     size = refs[0].shape[0]
-    for k in range(count):
-        member = lax.rem(mine[0] + count - k, count)
-        rows = pl.ds(pl.multiple_of(member * size, size), size)
-        block = refs[k][...]
-        sketch[rows, :] = block
-        half[rows, :] = block.astype(half.dtype)
+    for k, ref in enumerate(refs):
+        member = lax.rem(place + count - k, count)
+        yield pl.ds(pl.multiple_of(member * size, size), size), ref
+
+
+def basis_kernel(scale, place, inverse, *refs):
+    blocks, out = refs[:-1], refs[-1]
+    for rows, block in members(place[0], blocks):
+        out[rows, :] = dot(block[...], inverse[...], ((1,), (1,))) * scale
 
 
 def solve_kernel(inverse, parts, out):
@@ -187,113 +193,124 @@
     )
 
 
-def moment_kernel(side, half, gradients, *refs):
-    out = refs[-1]
+def moment_kernel(place, gradients, *refs):
+    half, out = refs[-1], refs[-2]
+    blocks, added = refs[:GROUPS], refs[GROUPS:-2]
+    for rows, block in members(place[1], blocks):
+        half[rows, :] = block[...].astype(half.dtype)
+    turned = half[...].T
     count, _, width = out.shape
-    turned = half[...].T
-    for i in range(count):
-        columns = pl.ds(pl.multiple_of((side[0] * count + i) * width, width), width)
-        value = jnp.dot(turned, gradients[:, columns], preferred_element_type=jnp.float32)
-        out[i] = value if len(refs) == 1 else value + refs[0][i]
-
-
-def moment_blocks(half, gradients, side, count, *added):
-    rows, rank = half.shape
-    width = gradients.shape[1] // (2 * count)
-    vmem, whole = pl.BlockSpec(memory_space=pltpu.VMEM), pl.BlockSpec()
+    for i in range(0, count, 2):
+        start = pl.multiple_of((place[0] * count + i) * width, 2 * width)
+        value = jnp.dot(
+            turned,
+            gradients[:, pl.ds(start, 2 * width)],
+            preferred_element_type=jnp.float32,
+        )
+        for j in range(2):
+            part = value[:, j * width : (j + 1) * width]
+            out[i + j] = part + added[0][i + j] if added else part
+
+
+def moment_blocks(place, gradients, blocks, count, flops, *added):
+    rows, feats = gradients.shape
+    rank = blocks[0].shape[1]
+    width = feats // (2 * count)
+    whole = pl.BlockSpec()
     return pl.pallas_call(
         moment_kernel,
         out_shape=far(count, rank, width),
-        in_specs=[pl.BlockSpec(memory_space=pltpu.SMEM), whole, vmem]
-        + [whole] * len(added),
+        in_specs=[
+            pl.BlockSpec(memory_space=pltpu.SMEM),
+            pl.BlockSpec(memory_space=pltpu.VMEM),
+        ]
+        + [whole] * (len(blocks) + len(added)),
         out_specs=whole,
+        scratch_shapes=[pltpu.VMEM((rows, rank), jnp.bfloat16)],
         compiler_params=pltpu.CompilerParams(vmem_limit_bytes=VMEM_LIMIT),
         cost_estimate=pl.CostEstimate(
-            flops=2 * rows * rank * width * count,
+            flops=flops,
             bytes_accessed=rows * width * count * 2 + rank * width * count * 4,
             transcendentals=0,
         ),
         name="moment",
-    )(side, half, gradients, *added)
+    )(place, gradients, *blocks, *added)
 
 
 def on_device(gradients, projection):
     rows, feats = gradients.shape
     rank = projection.shape[1]
-    scale = float(rows * lax.axis_size(ROWS)) ** 0.5
-    cores, xs = lax.axis_size("core"), lax.axis_size("x")
+    members_of_rows, near = lax.axis_size(ROWS), lax.axis_size(NEAR)
+    deep, pairs, xs, cores = (lax.axis_size(a) for a in (DEEP, "pair", "x", "core"))
+    scale = float(rows * members_of_rows) ** 0.5
     core = lax.axis_index("core").astype(jnp.int32)
-
-    near, members = lax.axis_size(NEAR), lax.axis_size(ROWS)
-    zs, groups = lax.axis_size("z"), lax.axis_size("y")
-    width = feats // (cores * xs)
+    mine = lax.axis_index("y").astype(jnp.int32)
+    size = rank // near
+    width = feats // (cores * pairs * xs)
 
     with jax.named_scope("sketch"):
-        partial, held = sketch_blocks(gradients, projection, groups)
+        partial, held = sketch_blocks(gradients, projection, GROUPS)
         parts = exchange(partial, "y")
 
     with jax.named_scope("gram"):
         own, shares = call(
             gram_kernel,
             "gram",
-            12 * rows // groups * rank**2,
-            [far(rows // groups, rank), far(near, rank // near, rank)],
+            12 * rows // GROUPS * rank**2,
+            [far(rows // GROUPS, rank), far(near, size, rank)],
             parts,
         )
         shares = exchange(shares, NEAR)
-
-    with jax.named_scope("gram"):
-        (shares,) = call(tile_kernel, "tile", SHORT, [far(zs, rank // near, rank)], shares)
-
-    with jax.named_scope("gather"):
-        others = [shifted(own, "y", k) for k in range(1, groups)]
-        mine = lax.axis_index("y").astype(jnp.int32)[None]
-        sketch, half = call(
-            place_kernel,
-            "place",
-            SHORT,
-            [far(rows, rank), jax.ShapeDtypeStruct((rows, rank), jnp.bfloat16)],
-            mine,
-            own,
-            *others,
-        )
-
-    with jax.named_scope("gram"):
-        shares = exchange(shares, "z")
-        (shares,) = call(
-            tile_kernel, "tile", SHORT, [far(near, rank // near, rank)], shares
-        )
+        (shares,) = call(tile_kernel, "tile", SHORT, [far(deep, size, rank)], shares)
+        shares = exchange(shares, DEEP)
+        (shares,) = call(tile_kernel, "tile", SHORT, [far(near, size, rank)], shares)
         shares = exchange(shares, NEAR)
 
     with jax.named_scope("factor"):
         (inverse,) = call(factor_kernel, "factor", 10**10, [f32(rank, rank)], shares)
 
+    with jax.named_scope("gather"):
+        blocks = [own] + [shifted(own, "y", k) for k in range(1, GROUPS)]
+        blocks = [pltpu.with_memory_space_constraint(b, pltpu.HBM) for b in blocks]
+
     with jax.named_scope("moment"):
-        away = moment_blocks(half, held, (1 - core)[None], xs)
+        count = pairs * xs
+        away = moment_blocks(jnp.stack([1 - core, mine]), held, blocks, count, SHORT)
         away = lax.ppermute(away, "core", [(0, 1), (1, 0)])
-        moment = exchange(moment_blocks(half, held, core[None], xs, away), "x")
+        moment = moment_blocks(
+            jnp.stack([core, mine]), held, blocks, count, 10**9, away
+        )
+        moment = exchange(moment, CROSS)
 
     with jax.named_scope("reduced"):
         (parts,) = call(
             solve_kernel,
             "solve",
             12 * rank**2 * width,
-            [f32(members, rank // members, width)],
+            [f32(members_of_rows, rank // members_of_rows, width)],
             inverse,
             moment,
         )
         parts = exchange(parts, ROWS)
-        parts = parts.reshape(zs, xs, cores, rank // members, width).sum(0)
-        reduced = parts.transpose(2, 1, 0, 3).reshape(rank // members, feats)
+        parts = parts.reshape(-1, pairs, xs, cores, rank // members_of_rows, width).sum(0)
+        reduced = parts.transpose(3, 2, 0, 1, 4).reshape(rank // members_of_rows, feats)
 
     with jax.named_scope("basis"):
-        basis = dot(sketch, inverse, ((1,), (1,))) * scale
+        (basis,) = call(
+            functools.partial(basis_kernel, scale),
+            "basis",
+            12 * rows * rank**2,
+            [f32(rows, rank)],
+            mine[None],
+            inverse,
+            *blocks,
+        )
     return (basis, reduced)
 
 
 def solution(mesh):
-    devices = mesh.devices.reshape(16, 4, 2, 4)
-    fine = Mesh(devices, ("z", "x", "core", "y"))
+    devices = mesh.devices.reshape(8, 2, 4, 2, 4)
+    fine = Mesh(devices, ("far", "pair", "x", "core", "y"))
     in_specs = (P(ROWS, "y"), P("y", None))
     out_specs = (P(ROWS, None), P(ROWS, "y"))
     return jax.shard_map(

time: 136 us -> 129 us (0.949)
  waiting for transfers between devices: 33.4 us -> 29.7 us
  matrix products: 1.7 us -> 0 us
    all_to_all x5, waiting for transfers between devices: 33.4 us -> 29.7 us  [exchange(): return lax.all_to_all(blocks, axes, 0, 0)]
    all_to_all x5, starting transfers between devices: 46.2 us -> 44.3 us  [exchange(): return lax.all_to_all(blocks, axes, 0, 0)]
    pallas_call x2, Pallas kernels: 4.43 us -> 6.16 us  [moment_blocks(): pl.pallas_call(moment_kernel, out_shape=far(count, rank, width), in_specs...]
    dot_general x1 -> x0, matrix products: 1.7 us -> none  [dot(): lax.dot_general(a, b, (contract, ((), ())), precision=HIGHEST, preferred_...]
  transfers between devices with their start and end apart: 9 -> 9, of which waited for: 4 -> 4; matrix products, arithmetic and copies ran while one was open for 1% -> 0% of each run, Pallas kernels for 14% -> 15%
where the time goes in v5:
time: 129 us
  starting transfers between devices  58.3 us (45%)
  waiting for transfers between devices  29.7 us (23%)
  Pallas kernels  25.8 us (20%)
  blocking collectives  13.2 us (10%)
    all_to_all x5, starting transfers between devices, exchange(): return lax.all_to_all(blocks, axes, 0, 0)  44.3 us
    all_to_all x5, waiting for transfers between devices, exchange(): return lax.all_to_all(blocks, axes, 0, 0)  29.7 us
    pallas_call x6, Pallas kernels, call(): pl.pallas_call(kernel, out_shape=outs, in_specs=[smem if a.ndim == 1 else...  15.9 us
    all_to_all x1, blocking collectives, exchange(): return lax.all_to_all(blocks, axes, 0, 0)  13.2 us
    ppermute x3, starting transfers between devices, shifted(): lax.ppermute(value, axis, [(i, (i + by) % count) for i in range(count)])  10.7 us
    pallas_call x2, Pallas kernels, moment_blocks(): pl.pallas_call(moment_kernel, out_shape=far(count, rank, width), in_specs...  6.16 us
    pallas_call x1, Pallas kernels, sketch_blocks(): pl.pallas_call(sketch_kernel, out_shape=[f32(blocks, rows // blocks, rank...  3.71 us
    ppermute x1, starting transfers between devices, on_device(): away = lax.ppermute(away, 'core', [(0, 1), (1, 0)])  3.38 us
  transfers between devices with their start and end apart: 9, of which 4 were waited for; matrix products, arithmetic and copies ran while one was open for 0% of the time, Pallas kernels for 15%

profile of v5, /device:TPU:1, one launch (start us, length us, event | category | flops | bytes accessed | tf_op | source)
XLA Modules:
  0.0 128.6 jit_solution(1021357503831264964)
XLA Ops:
  0.6 3.7 %sketch.1 = (f32[4,192,256]{2,1,0:T(8,128)S(1)}, bf16[768,2048]{1,0:T(8,128)(2,1)S(1)}) custom-call(bf16[768,2048]{1,0:T(8,128)(2,1)} %gradients.1, bf16[2048,256]{1,0:T(8,128)(2,1)} %projection.1), custom_call_target="tpu_custom_call" | custom-call | flops 805306368 | bytes 4194304 | tf_op jit(solution)/shard_map/sketch/sketch/pallas_call | solution.py:171
  4.3 13.2 %all_to_all.30.parts = f32[4,192,256]{2,1,0:T(8,128)S(1)} all-to-all(f32[4,192,256]{2,1,0:T(8,128)S(1)} %get-tuple-element.6), channel_id=1, replica_groups=mesh['far'=8,'pair'=2,'x'=4,'core'=2,'y'=4] {'y'}, dimensions={0} | all-to-all | bytes 1572864 | tf_op jit(solution)/shard_map/sketch/all_to_all | solution.py:24
  17.5 1.1 gram.1
  18.6 10.0 %all-to-all-start.1 = ((f32[32,8,256]{2,1,0:T(8,128)}), f32[32,8,256]{2,1,0:T(8,128)S(1)}, u32[]{:S(2)}, u32[]{:S(2)}) async-start(f32[32,8,256]{2,1,0:T(8,128)} %get-tuple-element.7), calls=%async_computation.1 | async-start | bytes 524288 | tf_op jit(solution)/shard_map/gram/all_to_all | solution.py:24
  28.6 0.1 pad_add_fusion.1.place
  28.7 3.3 %collective-permute-start = (f32[192,256]{1,0:T(8,128)}, f32[192,256]{1,0:T(8,128)}, u32[]{:S(2)}, u32[]{:S(2)}) collective-permute-start(f32[192,256]{1,0:T(8,128)} %get-tuple-element.8.refs_0_), channel_id=1, source_target_pairs={{0,1},{1,2},{2,3},{3,0},{4,5},{5,6},{6,7},{7,4},{8,9},{9,10},{10,1... | collective-permute-start | bytes 589832 | tf_op jit(solution)/shard_map/gather/ppermute | solution.py:29
  32.0 4.3 %collective-permute-start.1 = (f32[192,256]{1,0:T(8,128)}, f32[192,256]{1,0:T(8,128)}, u32[]{:S(2)}, u32[]{:S(2)}) collective-permute-start(f32[192,256]{1,0:T(8,128)} %get-tuple-element.8.refs_0_), channel_id=1, source_target_pairs={{0,2},{1,3},{2,0},{3,1},{4,6},{5,7},{6,4},{7,5},{8,10},{9,11},{10,... | collective-permute-start | bytes 589832 | tf_op jit(solution)/shard_map/gather/ppermute | solution.py:29
  36.3 3.1 %collective-permute-start.2 = (f32[192,256]{1,0:T(8,128)}, f32[192,256]{1,0:T(8,128)}, u32[]{:S(2)}, u32[]{:S(2)}) collective-permute-start(f32[192,256]{1,0:T(8,128)} %get-tuple-element.8.refs_0_), channel_id=1, source_target_pairs={{0,3},{1,0},{2,1},{3,2},{4,7},{5,4},{6,5},{7,6},{8,11},{9,8},{10,9... | collective-permute-start | bytes 589832 | tf_op jit(solution)/shard_map/gather/ppermute | solution.py:29
  39.4 0.0 all-to-all-done.1.parts
  39.4 0.7 tile.2
  40.1 14.9 %all-to-all-start.2 = ((f32[16,8,256]{2,1,0:T(8,128)}), f32[16,8,256]{2,1,0:T(8,128)S(1)}, u32[]{:S(2)}, u32[]{:S(2)}) async-start(f32[16,8,256]{2,1,0:T(8,128)} %tile.2), calls=%async_computation.2 | async-start | bytes 262144 | tf_op jit(solution)/shard_map/gram/all_to_all | solution.py:24
  55.0 0.0 collective-permute-done.refs_1_
  55.0 0.0 collective-permute-done.1.refs_2_
  55.0 0.0 collective-permute-done.2.refs_3_
  55.1 2.9 %moment.2 = f32[8,256,128]{2,1,0:T(8,128)} custom-call(s32[2]{0:T(128)S(1)} %pad_add_fusion.1.place, bf16[768,2048]{1,0:T(8,128)(2,1)S(1)} %get-tuple-element.9.gradients, f32[192,256]{1,0:T(8,128)} %get-tuple-element.8.refs_0_, f32[192,256]{1,0:T(8,128)} %collective-permute-done.refs_1_, f32[192,256]{1,0:T(8,128)} %collective-permute-done.1.refs_2_, ...), custom_call_target="tpu_custom_call" | custom-call | flops 30000001024 | bytes 2621440 | tf_op jit(solution)/shard_map/moment/moment/pallas_call | solution.py:220
  58.0 3.4 %collective-permute-start.3 = (f32[8,256,128]{2,1,0:T(8,128)}, f32[8,256,128]{2,1,0:T(8,128)}, u32[]{:S(2)}, u32[]{:S(2)}) collective-permute-start(f32[8,256,128]{2,1,0:T(8,128)} %moment.2), channel_id=1, source_target_pairs={{0,4},{4,0},{1,5},{5,1},{2,6},{6,2},{3,7},{7,3},{8,12},{12,8},{9,1... | collective-permute-start | bytes 3145736 | tf_op jit(solution)/shard_map/moment/ppermute | solution.py:279
  61.3 5.7 %all-to-all-done.2.parts = f32[16,8,256]{2,1,0:T(8,128)S(1)} async-done(((f32[16,8,256]{2,1,0:T(8,128)}), f32[16,8,256]{2,1,0:T(8,128)S(1)}, u32[]{:S(2)}, u32[]{:S(2)}) %all-to-all-start.2) | async-done | bytes 131104 | tf_op jit(solution)/shard_map/gram/all_to_all | solution.py:24
  67.0 0.7 tile.3
  67.7 8.2 %all-to-all-start.3 = ((f32[32,8,256]{2,1,0:T(8,128)}), f32[32,8,256]{2,1,0:T(8,128)S(1)}, u32[]{:S(2)}, u32[]{:S(2)}) async-start(f32[32,8,256]{2,1,0:T(8,128)} %tile.3), calls=%async_computation.3 | async-start | bytes 524288 | tf_op jit(solution)/shard_map/gram/all_to_all | solution.py:24
  75.9 0.1 pad_add_fusion.place
  76.0 0.0 collective-permute-done.3.refs_4_
  76.0 3.3 %moment.3 = f32[8,256,128]{2,1,0:T(8,128)} custom-call(s32[2]{0:T(128)S(1)} %pad_add_fusion.place, bf16[768,2048]{1,0:T(8,128)(2,1)S(1)} %get-tuple-element.9.gradients, f32[192,256]{1,0:T(8,128)} %get-tuple-element.8.refs_0_, f32[192,256]{1,0:T(8,128)} %collective-permute-done.refs_1_, f32[192,256]{1,0:T(8,128)} %collective-permute-done.1.refs_2_, ...), custom_call_target="tpu_custom_call" | custom-call | flops 1000000000 | bytes 2621440 | tf_op jit(solution)/shard_map/moment/moment/pallas_call | solution.py:220
  79.3 5.5 %all-to-all-done.3.shares = f32[32,8,256]{2,1,0:T(8,128)S(1)} async-done(((f32[32,8,256]{2,1,0:T(8,128)}), f32[32,8,256]{2,1,0:T(8,128)S(1)}, u32[]{:S(2)}, u32[]{:S(2)}) %all-to-all-start.3) | async-done | bytes 262176 | tf_op jit(solution)/shard_map/gram/all_to_all | solution.py:24
  84.7 3.6 %all-to-all-start.4 = ((f32[8,256,128]{2,1,0:T(8,128)}), f32[8,256,128]{2,1,0:T(8,128)S(1)}, u32[]{:S(2)}, u32[]{:S(2)}) async-start(f32[8,256,128]{2,1,0:T(8,128)} %moment.3), calls=%async_computation.4 | async-start | bytes 2097152 | tf_op jit(solution)/shard_map/moment/all_to_all | solution.py:24
  88.3 9.0 %factor.1.inverse = f32[256,256]{1,0:T(8,128)S(1)} custom-call(f32[32,8,256]{2,1,0:T(8,128)S(1)} %all-to-all-done.3.shares), custom_call_target="tpu_custom_call" | custom-call | flops 10000000000 | bytes 524288 | tf_op jit(solution)/shard_map/factor/factor/pallas_call | solution.py:85
  97.3 5.9 %all-to-all-done.4.parts = f32[8,256,128]{2,1,0:T(8,128)S(1)} async-done(((f32[8,256,128]{2,1,0:T(8,128)}), f32[8,256,128]{2,1,0:T(8,128)S(1)}, u32[]{:S(2)}, u32[]{:S(2)}) %all-to-all-start.4) | async-done | bytes 1048608 | tf_op jit(solution)/shard_map/moment/all_to_all | solution.py:24
  103.2 1.1 solve.1
  104.2 7.7 %all-to-all-start.5 = ((f32[128,2,128]{2,1,0:T(2,128)}), f32[128,2,128]{2,1,0:T(2,128)S(1)}, u32[]{:S(2)}, u32[]{:S(2)}) async-start(f32[128,2,128]{2,1,0:T(2,128)} %solve.1), calls=%async_computation.5 | async-start | bytes 262144 | tf_op jit(solution)/shard_map/reduced/all_to_all | solution.py:24
  111.9 3.3 %basis.1 = f32[768,256]{1,0:T(8,128)} custom-call(s32[1]{0:T(128)} %bitcast.place, f32[256,256]{1,0:T(8,128)S(1)} %factor.1.inverse, f32[192,256]{1,0:T(8,128)} %get-tuple-element.8.refs_0_, f32[192,256]{1,0:T(8,128)} %collective-permute-done.refs_1_, f32[192,256]{1,0:T(8,128)} %collective-permute-done.1.refs_2_, f32[192,256]{1,0:T(8,128)} %collective-permute-done.2.refs_3_), custom_call_target="tpu_custom_call" | custom-call | flops 603979776 | bytes 1835012 | tf_op jit(solution)/shard_map/basis/basis/pallas_call | solution.py:85
  115.2 12.7 %all-to-all-done.5 = f32[128,2,128]{2,1,0:T(2,128)S(1)} async-done(((f32[128,2,128]{2,1,0:T(2,128)}), f32[128,2,128]{2,1,0:T(2,128)S(1)}, u32[]{:S(2)}, u32[]{:S(2)}) %all-to-all-start.5) | async-done | bytes 131104 | tf_op jit(solution)/shard_map/reduced/all_to_all | solution.py:24
  128.0 0.6 reshape.11
  (2 shorter events, 0.1 us)
Async XLA Ops:
  18.6 20.8 %all-to-all-start.1 = ((f32[32,8,256]{2,1,0:T(8,128)}), f32[32,8,256]{2,1,0:T(8,128)S(1)}, u32[]{:S(2)}, u32[]{:S(2)}) async-start(f32[32,8,256]{2,1,0:T(8,128)} %get-tuple-element.7), calls=%async_computation.1 | async-start | bytes 524288 | tf_op jit(solution)/shard_map/gram/all_to_all | solution.py:24
  28.7 26.3 %collective-permute-start = (f32[192,256]{1,0:T(8,128)}, f32[192,256]{1,0:T(8,128)}, u32[]{:S(2)}, u32[]{:S(2)}) collective-permute-start(f32[192,256]{1,0:T(8,128)} %get-tuple-element.8.refs_0_), channel_id=1, source_target_pairs={{0,1},{1,2},{2,3},{3,0},{4,5},{5,6},{6,7},{7,4},{8,9},{9,10},{10,1... | collective-permute-start | bytes 589832 | tf_op jit(solution)/shard_map/gather/ppermute | solution.py:29
  32.0 23.1 %collective-permute-start.1 = (f32[192,256]{1,0:T(8,128)}, f32[192,256]{1,0:T(8,128)}, u32[]{:S(2)}, u32[]{:S(2)}) collective-permute-start(f32[192,256]{1,0:T(8,128)} %get-tuple-element.8.refs_0_), channel_id=1, source_target_pairs={{0,2},{1,3},{2,0},{3,1},{4,6},{5,7},{6,4},{7,5},{8,10},{9,11},{10,... | collective-permute-start | bytes 589832 | tf_op jit(solution)/shard_map/gather/ppermute | solution.py:29
  36.3 18.8 %collective-permute-start.2 = (f32[192,256]{1,0:T(8,128)}, f32[192,256]{1,0:T(8,128)}, u32[]{:S(2)}, u32[]{:S(2)}) collective-permute-start(f32[192,256]{1,0:T(8,128)} %get-tuple-element.8.refs_0_), channel_id=1, source_target_pairs={{0,3},{1,0},{2,1},{3,2},{4,7},{5,4},{6,5},{7,6},{8,11},{9,8},{10,9... | collective-permute-start | bytes 589832 | tf_op jit(solution)/shard_map/gather/ppermute | solution.py:29
  40.1 26.9 %all-to-all-start.2 = ((f32[16,8,256]{2,1,0:T(8,128)}), f32[16,8,256]{2,1,0:T(8,128)S(1)}, u32[]{:S(2)}, u32[]{:S(2)}) async-start(f32[16,8,256]{2,1,0:T(8,128)} %tile.2), calls=%async_computation.2 | async-start | bytes 262144 | tf_op jit(solution)/shard_map/gram/all_to_all | solution.py:24
  58.0 18.0 %collective-permute-start.3 = (f32[8,256,128]{2,1,0:T(8,128)}, f32[8,256,128]{2,1,0:T(8,128)}, u32[]{:S(2)}, u32[]{:S(2)}) collective-permute-start(f32[8,256,128]{2,1,0:T(8,128)} %moment.2), channel_id=1, source_target_pairs={{0,4},{4,0},{1,5},{5,1},{2,6},{6,2},{3,7},{7,3},{8,12},{12,8},{9,1... | collective-permute-start | bytes 3145736 | tf_op jit(solution)/shard_map/moment/ppermute | solution.py:279
  67.7 17.0 %all-to-all-start.3 = ((f32[32,8,256]{2,1,0:T(8,128)}), f32[32,8,256]{2,1,0:T(8,128)S(1)}, u32[]{:S(2)}, u32[]{:S(2)}) async-start(f32[32,8,256]{2,1,0:T(8,128)} %tile.3), calls=%async_computation.3 | async-start | bytes 524288 | tf_op jit(solution)/shard_map/gram/all_to_all | solution.py:24
  84.7 18.4 %all-to-all-start.4 = ((f32[8,256,128]{2,1,0:T(8,128)}), f32[8,256,128]{2,1,0:T(8,128)S(1)}, u32[]{:S(2)}, u32[]{:S(2)}) async-start(f32[8,256,128]{2,1,0:T(8,128)} %moment.3), calls=%async_computation.4 | async-start | bytes 2097152 | tf_op jit(solution)/shard_map/moment/all_to_all | solution.py:24
  104.2 23.7 %all-to-all-start.5 = ((f32[128,2,128]{2,1,0:T(2,128)}), f32[128,2,128]{2,1,0:T(2,128)S(1)}, u32[]{:S(2)}, u32[]{:S(2)}) async-start(f32[128,2,128]{2,1,0:T(2,128)} %solve.1), calls=%async_computation.5 | async-start | bytes 262144 | tf_op jit(solution)/shard_map/reduced/all_to_all | solution.py:24

commit v6 on v5

--- a/solution.py
+++ b/solution.py
@@ -12,7 +12,6 @@
 HIGHEST = lax.Precision.HIGHEST
 ROWS = ("far", "pair", "x", "core")
 DEEP = ("far", "pair")
-CROSS = ("pair", "x")
 NEAR = ("x", "core", "y")
 GROUPS = 4
 PANEL = 8
@@ -194,22 +193,27 @@
 
 
 def moment_kernel(place, gradients, *refs):
-    half, out = refs[-1], refs[-2]
-    blocks, added = refs[:GROUPS], refs[GROUPS:-2]
+    blocks, added = refs[:GROUPS], refs[GROUPS]
+    outs, half = refs[GROUPS:-1], refs[-1]
     for rows, block in members(place[1], blocks):
         half[rows, :] = block[...].astype(half.dtype)
     turned = half[...].T
-    count, _, width = out.shape
-    for i in range(0, count, 2):
-        start = pl.multiple_of((place[0] * count + i) * width, 2 * width)
-        value = jnp.dot(
-            turned,
-            gradients[:, pl.ds(start, 2 * width)],
-            preferred_element_type=jnp.float32,
-        )
-        for j in range(2):
-            part = value[:, j * width : (j + 1) * width]
-            out[i + j] = part + added[0][i + j] if added else part
+    single = len(outs) == 1
+    outs = outs if single else outs[1:]
+    count, _, width = outs[0].shape
+    total = count * len(outs)
+    for n, out in enumerate(outs):
+        for i in range(0, count, 2):
+            block = i if single else lax.rem(place[2] + n, 2) * count + i
+            start = pl.multiple_of((place[0] * total + block) * width, 2 * width)
+            value = jnp.dot(
+                turned,
+                gradients[:, pl.ds(start, 2 * width)],
+                preferred_element_type=jnp.float32,
+            )
+            for j in range(2):
+                part = value[:, j * width : (j + 1) * width]
+                out[i + j] = part if single else part + added[block + j]
 
 
 def moment_blocks(place, gradients, blocks, count, flops, *added):
@@ -217,15 +221,16 @@
     rank = blocks[0].shape[1]
     width = feats // (2 * count)
     whole = pl.BlockSpec()
+    outs = [far(count // 2, rank, width)] * 2 if added else far(count, rank, width)
     return pl.pallas_call(
         moment_kernel,
-        out_shape=far(count, rank, width),
+        out_shape=outs,
         in_specs=[
             pl.BlockSpec(memory_space=pltpu.SMEM),
             pl.BlockSpec(memory_space=pltpu.VMEM),
         ]
         + [whole] * (len(blocks) + len(added)),
-        out_specs=whole,
+        out_specs=[whole] * 2 if added else whole,
         scratch_shapes=[pltpu.VMEM((rows, rank), jnp.bfloat16)],
         compiler_params=pltpu.CompilerParams(vmem_limit_bytes=VMEM_LIMIT),
         cost_estimate=pl.CostEstimate(
@@ -235,6 +240,10 @@
         ),
         name="moment",
     )(place, gradients, *blocks, *added)
+
+
+def add_kernel(a, b, out):
+    out[...] = a[...] + b[...]
 
 
 def on_device(gradients, projection):
@@ -274,13 +283,17 @@
         blocks = [pltpu.with_memory_space_constraint(b, pltpu.HBM) for b in blocks]
 
     with jax.named_scope("moment"):
+        swap = [(0, 1), (1, 0)]
+        pair = lax.axis_index("pair").astype(jnp.int32)
         count = pairs * xs
         away = moment_blocks(jnp.stack([1 - core, mine]), held, blocks, count, SHORT)
-        away = lax.ppermute(away, "core", [(0, 1), (1, 0)])
-        moment = moment_blocks(
-            jnp.stack([core, mine]), held, blocks, count, 10**9, away
-        )
-        moment = exchange(moment, CROSS)
+        away = lax.ppermute(away, "core", swap)
+        kept, given = moment_blocks(
+            jnp.stack([core, mine, pair]), held, blocks, count, 10**8, away
+        )
+        given = lax.ppermute(given, "pair", swap)
+        (moment,) = call(add_kernel, "add", 0, [far(xs, rank, width)], kept, given)
+        moment = exchange(moment, "x")
 
     with jax.named_scope("reduced"):
         (parts,) = call(

time: 129 us -> 132 us (1.023)
  starting transfers between devices: 58.3 us -> 60.6 us
    all_to_all x5, starting transfers between devices: 44.3 us -> 46.7 us  [exchange(): return lax.all_to_all(blocks, axes, 0, 0)]
    ppermute x3, starting transfers between devices: 10.7 us -> 8.4 us  [shifted(): lax.ppermute(value, axis, [(i, (i + by) % count) for i in range(count)])]
    ppermute x1 -> x2, starting transfers between devices: 3.38 us -> 5.52 us  [the longest x1 3.38 us: on_device(): given = lax.ppermute(given, 'pair', swap)]
    pallas_call x6 -> x7, Pallas kernels: 15.9 us -> 16.7 us  [call(): pl.pallas_call(kernel, out_shape=outs, in_specs=[smem if a.ndim == 1 else...]
  transfers between devices with their start and end apart: 9 -> 10, of which waited for: 4 -> 5; matrix products, arithmetic and copies ran while one was open for 0% -> 0% of each run, Pallas kernels for 15% -> 16%
where the time goes in v6:
time: 132 us
  starting transfers between devices  60.6 us (46%)
  waiting for transfers between devices  30 us (23%)
  Pallas kernels  26.4 us (20%)
  blocking collectives  13.2 us (10%)
    all_to_all x5, starting transfers between devices, exchange(): return lax.all_to_all(blocks, axes, 0, 0)  46.7 us
    all_to_all x5, waiting for transfers between devices, exchange(): return lax.all_to_all(blocks, axes, 0, 0)  29.9 us
    pallas_call x7, Pallas kernels, call(): pl.pallas_call(kernel, out_shape=outs, in_specs=[smem if a.ndim == 1 else...  16.7 us
    all_to_all x1, blocking collectives, exchange(): return lax.all_to_all(blocks, axes, 0, 0)  13.2 us
    ppermute x3, starting transfers between devices, shifted(): lax.ppermute(value, axis, [(i, (i + by) % count) for i in range(count)])  8.4 us
    pallas_call x2, Pallas kernels, moment_blocks(): pl.pallas_call(moment_kernel, out_shape=outs, in_specs=[pl.BlockSpec(memo...  5.97 us
    pallas_call x1, Pallas kernels, sketch_blocks(): pl.pallas_call(sketch_kernel, out_shape=[f32(blocks, rows // blocks, rank...  3.71 us
    ppermute x1, starting transfers between devices, on_device(): given = lax.ppermute(given, 'pair', swap)  3.38 us
  transfers between devices with their start and end apart: 10, of which 5 were waited for; matrix products, arithmetic and copies ran while one was open for 0% of the time, Pallas kernels for 16%

profile of v6, /device:TPU:1, one launch (start us, length us, event | category | flops | bytes accessed | tf_op | source)
XLA Modules:
  0.0 131.8 jit_solution(2643346180763262415)
XLA Ops:
  0.6 3.7 %sketch.1 = (f32[4,192,256]{2,1,0:T(8,128)S(1)}, bf16[768,2048]{1,0:T(8,128)(2,1)S(1)}) custom-call(bf16[768,2048]{1,0:T(8,128)(2,1)} %gradients.1, bf16[2048,256]{1,0:T(8,128)(2,1)} %projection.1), custom_call_target="tpu_custom_call" | custom-call | flops 805306368 | bytes 4194304 | tf_op jit(solution)/shard_map/sketch/sketch/pallas_call | solution.py:170
  4.3 13.2 %all_to_all.30.parts = f32[4,192,256]{2,1,0:T(8,128)S(1)} all-to-all(f32[4,192,256]{2,1,0:T(8,128)S(1)} %get-tuple-element.8), channel_id=1, replica_groups=mesh['far'=8,'pair'=2,'x'=4,'core'=2,'y'=4] {'y'}, dimensions={0} | all-to-all | bytes 1572864 | tf_op jit(solution)/shard_map/sketch/all_to_all | solution.py:23
  17.5 1.1 gram.1
  18.6 2.2 %collective-permute-start = (f32[192,256]{1,0:T(8,128)}, f32[192,256]{1,0:T(8,128)}, u32[]{:S(2)}, u32[]{:S(2)}) collective-permute-start(f32[192,256]{1,0:T(8,128)} %get-tuple-element.10.refs_0_), channel_id=1, source_target_pairs={{0,1},{1,2},{2,3},{3,0},{4,5},{5,6},{6,7},{7,4},{8,9},{9,10},{10,1... | collective-permute-start | bytes 589832 | tf_op jit(solution)/shard_map/gather/ppermute | solution.py:28
  20.8 3.7 %collective-permute-start.1 = (f32[192,256]{1,0:T(8,128)}, f32[192,256]{1,0:T(8,128)}, u32[]{:S(2)}, u32[]{:S(2)}) collective-permute-start(f32[192,256]{1,0:T(8,128)} %get-tuple-element.10.refs_0_), channel_id=1, source_target_pairs={{0,2},{1,3},{2,0},{3,1},{4,6},{5,7},{6,4},{7,5},{8,10},{9,11},{10,... | collective-permute-start | bytes 589832 | tf_op jit(solution)/shard_map/gather/ppermute | solution.py:28
  24.6 2.5 %collective-permute-start.2 = (f32[192,256]{1,0:T(8,128)}, f32[192,256]{1,0:T(8,128)}, u32[]{:S(2)}, u32[]{:S(2)}) collective-permute-start(f32[192,256]{1,0:T(8,128)} %get-tuple-element.10.refs_0_), channel_id=1, source_target_pairs={{0,3},{1,0},{2,1},{3,2},{4,7},{5,4},{6,5},{7,6},{8,11},{9,8},{10,9... | collective-permute-start | bytes 589832 | tf_op jit(solution)/shard_map/gather/ppermute | solution.py:28
  27.1 0.1 pad_add_fusion.1.place
  27.2 12.3 %all-to-all-start.1 = ((f32[32,8,256]{2,1,0:T(8,128)}), f32[32,8,256]{2,1,0:T(8,128)S(1)}, u32[]{:S(2)}, u32[]{:S(2)}) async-start(f32[32,8,256]{2,1,0:T(8,128)} %get-tuple-element.9), calls=%async_computation.1 | async-start | bytes 524288 | tf_op jit(solution)/shard_map/gram/all_to_all | solution.py:23
  39.4 0.0 collective-permute-done.1.refs_2_
  39.4 0.0 collective-permute-done.2.refs_3_
  39.5 2.9 %moment.2 = f32[8,256,128]{2,1,0:T(8,128)} custom-call(s32[2]{0:T(128)S(1)} %pad_add_fusion.1.place, bf16[768,2048]{1,0:T(8,128)(2,1)S(1)} %get-tuple-element.11.gradients, f32[192,256]{1,0:T(8,128)} %get-tuple-element.10.refs_0_, f32[192,256]{1,0:T(8,128)} %collective-permute-done.refs_1_, f32[192,256]{1,0:T(8,128)} %collective-permute-done.1.refs_2_, ...), custom_call_target="tpu_custom_call" | custom-call | flops 30000001024 | bytes 2621440 | tf_op jit(solution)/shard_map/moment/moment/pallas_call | solution.py:225
  42.3 2.1 %collective-permute-start.3 = (f32[8,256,128]{2,1,0:T(8,128)}, f32[8,256,128]{2,1,0:T(8,128)}, u32[]{:S(2)}, u32[]{:S(2)}) collective-permute-start(f32[8,256,128]{2,1,0:T(8,128)} %moment.2), channel_id=1, source_target_pairs={{0,4},{4,0},{1,5},{5,1},{2,6},{6,2},{3,7},{7,3},{8,12},{12,8},{9,1... | collective-permute-start | bytes 3145736 | tf_op jit(solution)/shard_map/moment/ppermute | solution.py:290
  44.5 3.7 %all-to-all-done.1.parts = f32[32,8,256]{2,1,0:T(8,128)S(1)} async-done(((f32[32,8,256]{2,1,0:T(8,128)}), f32[32,8,256]{2,1,0:T(8,128)S(1)}, u32[]{:S(2)}, u32[]{:S(2)}) %all-to-all-start.1) | async-done | bytes 262176 | tf_op jit(solution)/shard_map/gram/all_to_all | solution.py:23
  48.2 0.7 tile.2
  48.9 14.9 %all-to-all-start.2 = ((f32[16,8,256]{2,1,0:T(8,128)}), f32[16,8,256]{2,1,0:T(8,128)S(1)}, u32[]{:S(2)}, u32[]{:S(2)}) async-start(f32[16,8,256]{2,1,0:T(8,128)} %tile.2), calls=%async_computation.2 | async-start | bytes 262144 | tf_op jit(solution)/shard_map/gram/all_to_all | solution.py:23
  63.9 0.1 pad_add_fusion.place
  63.9 3.1 %moment.3 = (f32[4,256,128]{2,1,0:T(8,128)}, f32[4,256,128]{2,1,0:T(8,128)}) custom-call(s32[3]{0:T(128)S(1)} %pad_add_fusion.place, bf16[768,2048]{1,0:T(8,128)(2,1)S(1)} %get-tuple-element.11.gradients, f32[192,256]{1,0:T(8,128)} %get-tuple-element.10.refs_0_, f32[192,256]{1,0:T(8,128)} %collective-permute-done.refs_1_, ...), custom_call_target="tpu_custom_call" | custom-call | flops 100000000 | bytes 2621440 | tf_op jit(solution)/shard_map/moment/moment/pallas_call | solution.py:225
  67.0 3.4 %collective-permute-start.4 = (f32[4,256,128]{2,1,0:T(8,128)}, f32[4,256,128]{2,1,0:T(8,128)S(1)}, u32[]{:S(2)}, u32[]{:S(2)}) collective-permute-start(f32[4,256,128]{2,1,0:T(8,128)} %get-tuple-element.13), channel_id=1, source_target_pairs={{0,32},{32,0},{1,33},{33,1},{2,34},{34,2},{3,35},{35,3},{4,36},{36... | collective-permute-start | bytes 1572872 | tf_op jit(solution)/shard_map/moment/ppermute | solution.py:294
  70.4 5.4 %all-to-all-done.2.parts = f32[16,8,256]{2,1,0:T(8,128)S(1)} async-done(((f32[16,8,256]{2,1,0:T(8,128)}), f32[16,8,256]{2,1,0:T(8,128)S(1)}, u32[]{:S(2)}, u32[]{:S(2)}) %all-to-all-start.2) | async-done | bytes 131104 | tf_op jit(solution)/shard_map/gram/all_to_all | solution.py:23
  75.9 0.7 tile.3
  76.6 7.3 %all-to-all-start.3 = ((f32[32,8,256]{2,1,0:T(8,128)}), f32[32,8,256]{2,1,0:T(8,128)S(1)}, u32[]{:S(2)}, u32[]{:S(2)}) async-start(f32[32,8,256]{2,1,0:T(8,128)} %tile.3), calls=%async_computation.3 | async-start | bytes 524288 | tf_op jit(solution)/shard_map/gram/all_to_all | solution.py:23
  83.8 0.1 collective-permute-done.4.b
  84.0 0.8 add.7
  84.8 7.9 %all-to-all-done.3.shares = f32[32,8,256]{2,1,0:T(8,128)S(1)} async-done(((f32[32,8,256]{2,1,0:T(8,128)}), f32[32,8,256]{2,1,0:T(8,128)S(1)}, u32[]{:S(2)}, u32[]{:S(2)}) %all-to-all-start.3) | async-done | bytes 262176 | tf_op jit(solution)/shard_map/gram/all_to_all | solution.py:23
  92.7 3.5 %all-to-all-start.4 = ((f32[4,256,128]{2,1,0:T(8,128)}), f32[4,256,128]{2,1,0:T(8,128)S(1)}, u32[]{:S(2)}, u32[]{:S(2)}) async-start(f32[4,256,128]{2,1,0:T(8,128)} %add.7), calls=%async_computation.4 | async-start | bytes 1048576 | tf_op jit(solution)/shard_map/moment/all_to_all | solution.py:23
  96.2 9.0 %factor.1.inverse = f32[256,256]{1,0:T(8,128)S(1)} custom-call(f32[32,8,256]{2,1,0:T(8,128)S(1)} %all-to-all-done.3.shares), custom_call_target="tpu_custom_call" | custom-call | flops 10000000000 | bytes 524288 | tf_op jit(solution)/shard_map/factor/factor/pallas_call | solution.py:84
  105.2 0.0 all-to-all-done.4.parts
  105.2 1.0 solve.1
  106.3 8.8 %all-to-all-start.5 = ((f32[128,2,128]{2,1,0:T(2,128)}), f32[128,2,128]{2,1,0:T(2,128)S(1)}, u32[]{:S(2)}, u32[]{:S(2)}) async-start(f32[128,2,128]{2,1,0:T(2,128)} %solve.1), calls=%async_computation.5 | async-start | bytes 262144 | tf_op jit(solution)/shard_map/reduced/all_to_all | solution.py:23
  115.0 3.3 %basis.1 = f32[768,256]{1,0:T(8,128)} custom-call(s32[1]{0:T(128)} %bitcast.place, f32[256,256]{1,0:T(8,128)S(1)} %factor.1.inverse, f32[192,256]{1,0:T(8,128)} %get-tuple-element.10.refs_0_, f32[192,256]{1,0:T(8,128)} %collective-permute-done.refs_1_, f32[192,256]{1,0:T(8,128)} %collective-permute-done.1.refs_2_, f32[192,256]{1,0:T(8,128)} %collective-permute-done.2.refs_3_), custom_call_target="tpu_custom_call" | custom-call | flops 603979776 | bytes 1835012 | tf_op jit(solution)/shard_map/basis/basis/pallas_call | solution.py:84
  118.3 12.8 %all-to-all-done.5 = f32[128,2,128]{2,1,0:T(2,128)S(1)} async-done(((f32[128,2,128]{2,1,0:T(2,128)}), f32[128,2,128]{2,1,0:T(2,128)S(1)}, u32[]{:S(2)}, u32[]{:S(2)}) %all-to-all-start.5) | async-done | bytes 131104 | tf_op jit(solution)/shard_map/reduced/all_to_all | solution.py:23
  131.1 0.6 reshape.11
  (6 shorter events, 0.1 us)
Async XLA Ops:
  18.6 20.8 %collective-permute-start = (f32[192,256]{1,0:T(8,128)}, f32[192,256]{1,0:T(8,128)}, u32[]{:S(2)}, u32[]{:S(2)}) collective-permute-start(f32[192,256]{1,0:T(8,128)} %get-tuple-element.10.refs_0_), channel_id=1, source_target_pairs={{0,1},{1,2},{2,3},{3,0},{4,5},{5,6},{6,7},{7,4},{8,9},{9,10},{10,1... | collective-permute-start | bytes 589832 | tf_op jit(solution)/shard_map/gather/ppermute | solution.py:28
  20.8 18.6 %collective-permute-start.1 = (f32[192,256]{1,0:T(8,128)}, f32[192,256]{1,0:T(8,128)}, u32[]{:S(2)}, u32[]{:S(2)}) collective-permute-start(f32[192,256]{1,0:T(8,128)} %get-tuple-element.10.refs_0_), channel_id=1, source_target_pairs={{0,2},{1,3},{2,0},{3,1},{4,6},{5,7},{6,4},{7,5},{8,10},{9,11},{10,... | collective-permute-start | bytes 589832 | tf_op jit(solution)/shard_map/gather/ppermute | solution.py:28
  24.6 14.9 %collective-permute-start.2 = (f32[192,256]{1,0:T(8,128)}, f32[192,256]{1,0:T(8,128)}, u32[]{:S(2)}, u32[]{:S(2)}) collective-permute-start(f32[192,256]{1,0:T(8,128)} %get-tuple-element.10.refs_0_), channel_id=1, source_target_pairs={{0,3},{1,0},{2,1},{3,2},{4,7},{5,4},{6,5},{7,6},{8,11},{9,8},{10,9... | collective-permute-start | bytes 589832 | tf_op jit(solution)/shard_map/gather/ppermute | solution.py:28
  27.2 21.1 %all-to-all-start.1 = ((f32[32,8,256]{2,1,0:T(8,128)}), f32[32,8,256]{2,1,0:T(8,128)S(1)}, u32[]{:S(2)}, u32[]{:S(2)}) async-start(f32[32,8,256]{2,1,0:T(8,128)} %get-tuple-element.9), calls=%async_computation.1 | async-start | bytes 524288 | tf_op jit(solution)/shard_map/gram/all_to_all | solution.py:23
  42.3 21.6 %collective-permute-start.3 = (f32[8,256,128]{2,1,0:T(8,128)}, f32[8,256,128]{2,1,0:T(8,128)}, u32[]{:S(2)}, u32[]{:S(2)}) collective-permute-start(f32[8,256,128]{2,1,0:T(8,128)} %moment.2), channel_id=1, source_target_pairs={{0,4},{4,0},{1,5},{5,1},{2,6},{6,2},{3,7},{7,3},{8,12},{12,8},{9,1... | collective-permute-start | bytes 3145736 | tf_op jit(solution)/shard_map/moment/ppermute | solution.py:290
  48.9 26.9 %all-to-all-start.2 = ((f32[16,8,256]{2,1,0:T(8,128)}), f32[16,8,256]{2,1,0:T(8,128)S(1)}, u32[]{:S(2)}, u32[]{:S(2)}) async-start(f32[16,8,256]{2,1,0:T(8,128)} %tile.2), calls=%async_computation.2 | async-start | bytes 262144 | tf_op jit(solution)/shard_map/gram/all_to_all | solution.py:23
  67.0 16.9 %copy-start = (f32[4,256,128]{2,1,0:T(8,128)S(1)}, f32[4,256,128]{2,1,0:T(8,128)}, u32[]{:S(2)}) copy-start(f32[4,256,128]{2,1,0:T(8,128)} %get-tuple-element.12.a) | copy-start | bytes 1572868
  67.0 16.9 %collective-permute-start.4 = (f32[4,256,128]{2,1,0:T(8,128)}, f32[4,256,128]{2,1,0:T(8,128)S(1)}, u32[]{:S(2)}, u32[]{:S(2)}) collective-permute-start(f32[4,256,128]{2,1,0:T(8,128)} %get-tuple-element.13), channel_id=1, source_target_pairs={{0,32},{32,0},{1,33},{33,1},{2,34},{34,2},{3,35},{35,3},{4,36},{36... | collective-permute-start | bytes 1572872 | tf_op jit(solution)/shard_map/moment/ppermute | solution.py:294
  76.6 16.2 %all-to-all-start.3 = ((f32[32,8,256]{2,1,0:T(8,128)}), f32[32,8,256]{2,1,0:T(8,128)S(1)}, u32[]{:S(2)}, u32[]{:S(2)}) async-start(f32[32,8,256]{2,1,0:T(8,128)} %tile.3), calls=%async_computation.3 | async-start | bytes 524288 | tf_op jit(solution)/shard_map/gram/all_to_all | solution.py:23
  92.7 12.5 %all-to-all-start.4 = ((f32[4,256,128]{2,1,0:T(8,128)}), f32[4,256,128]{2,1,0:T(8,128)S(1)}, u32[]{:S(2)}, u32[]{:S(2)}) async-start(f32[4,256,128]{2,1,0:T(8,128)} %add.7), calls=%async_computation.4 | async-start | bytes 1048576 | tf_op jit(solution)/shard_map/moment/all_to_all | solution.py:23
  106.3 24.8 %all-to-all-start.5 = ((f32[128,2,128]{2,1,0:T(2,128)}), f32[128,2,128]{2,1,0:T(2,128)S(1)}, u32[]{:S(2)}, u32[]{:S(2)}) async-start(f32[128,2,128]{2,1,0:T(2,128)} %solve.1), calls=%async_computation.5 | async-start | bytes 262144 | tf_op jit(solution)/shard_map/reduced/all_to_all | solution.py:23

commit v7 on v5

--- a/solution.py
+++ b/solution.py
@@ -15,6 +15,7 @@
 CROSS = ("pair", "x")
 NEAR = ("x", "core", "y")
 GROUPS = 4
+PIECES = 4
 PANEL = 8
 SHORT = 3 * 10**10
 VMEM_LIMIT = 8 * 1024 * 1024
@@ -78,7 +79,7 @@
     return jnp.concatenate(done, 0)
 
 
-def call(kernel, name, flops, outs, *args):
+def call(kernel, name, flops, outs, *args, scratch=()):
     whole = pl.BlockSpec()
     smem = pl.BlockSpec(memory_space=pltpu.SMEM)
     moved = sum(math.prod(a.shape) * a.dtype.itemsize for a in (*args, *outs))
@@ -87,6 +88,7 @@
         out_shape=outs,
         in_specs=[smem if a.ndim == 1 else whole for a in args],
         out_specs=[whole] * len(outs),
+        scratch_shapes=scratch,
         compiler_params=pltpu.CompilerParams(vmem_limit_bytes=VMEM_LIMIT),
         cost_estimate=pl.CostEstimate(flops=flops, bytes_accessed=moved, transcendentals=0),
         name=name,
@@ -104,7 +106,11 @@
 def gram_kernel(parts, own, gram):
     total = jnp.sum(parts[...], 0)
     own[...] = total
-    gram[...] = dot(total, total, ((0,), (0,))).reshape(gram.shape)
+    n = total.shape[1] // 2
+    left = dot(total, total[:, :n], ((0,), (0,)))
+    right = dot(total[:, n:], total[:, n:], ((0,), (0,)))
+    packed = jnp.concatenate([left[:n], left[n:], right], 1)
+    gram[...] = packed.reshape(gram.shape)
 
 
 def tile_kernel(parts, tiles):
@@ -113,12 +119,12 @@
         tiles[i] = total
 
 
-def factor_kernel(shares, out):
-    gram = shares[...].reshape(out.shape)
-    n = gram.shape[0] // 2
-    top = inverse_factor(gram[:n, :n])
-    low = dot(gram[n:, :n], top, ((1,), (1,)))
-    bottom = inverse_factor(gram[n:, n:] - dot(low, low, ((1,), (1,))))
+def factor_kernel(shares, out, packed):
+    n = out.shape[0] // 2
+    packed[...] = shares[...].reshape(packed.shape)
+    top = inverse_factor(packed[:, :n])
+    low = dot(packed[:, n : 2 * n], top, ((1,), (1,)))
+    bottom = inverse_factor(packed[:, 2 * n :] - dot(low, low, ((1,), (1,))))
     out[:n, :n] = top
     out[:n, n:] = jnp.zeros((n, n), jnp.float32)
     out[n:, n:] = bottom
@@ -145,24 +151,19 @@
 
 
 def sketch_kernel(gradients, projection, partial, held, weights, sems):
-    blocks, size, _ = partial.shape
-    first = pltpu.make_async_copy(projection, weights, sems.at[blocks])
-    first.start()
-    copies = []
-    for i in range(blocks):
+    copies = [pltpu.make_async_copy(projection, weights, sems.at[0])]
+    size = held.shape[0] // PIECES
+    for i in range(PIECES):
         part = pl.ds(i * size, size)
         copies.append(
-            pltpu.make_async_copy(gradients.at[part], held.at[part], sems.at[i])
-        )
-        copies[-1].start()
-    first.wait()
-    for i in range(blocks):
-        copies[i].wait()
-        partial[i] = jnp.dot(
-            held[i * size : (i + 1) * size, :],
-            weights[...],
-            preferred_element_type=jnp.float32,
-        )
+            pltpu.make_async_copy(gradients.at[part], held.at[part], sems.at[i + 1])
+        )
+    for copy in copies:
+        copy.start()
+    for copy in copies:
+        copy.wait()
+    value = jnp.dot(held[...], weights[...], preferred_element_type=jnp.float32)
+    partial[...] = value.reshape(partial.shape)
 
 
 def sketch_blocks(gradients, projection, blocks):
@@ -178,7 +179,7 @@
         out_specs=[pl.BlockSpec(), pl.BlockSpec(memory_space=pltpu.VMEM)],
         scratch_shapes=[
             pltpu.VMEM(projection.shape, projection.dtype),
-            pltpu.SemaphoreType.DMA((blocks + 1,)),
+            pltpu.SemaphoreType.DMA((PIECES + 1,)),
         ],
         compiler_params=pltpu.CompilerParams(vmem_limit_bytes=VMEM_LIMIT),
         cost_estimate=pl.CostEstimate(
@@ -245,7 +246,7 @@
     scale = float(rows * members_of_rows) ** 0.5
     core = lax.axis_index("core").astype(jnp.int32)
     mine = lax.axis_index("y").astype(jnp.int32)
-    size = rank // near
+    share = (rank // 2 // near, 3 * rank // 2)
     width = feats // (cores * pairs * xs)
 
     with jax.named_scope("sketch"):
@@ -257,17 +258,24 @@
             gram_kernel,
             "gram",
             12 * rows // GROUPS * rank**2,
-            [far(rows // GROUPS, rank), far(near, size, rank)],
+            [far(rows // GROUPS, rank), far(near, *share)],
             parts,
         )
         shares = exchange(shares, NEAR)
-        (shares,) = call(tile_kernel, "tile", SHORT, [far(deep, size, rank)], shares)
+        (shares,) = call(tile_kernel, "tile", SHORT, [far(deep, *share)], shares)
         shares = exchange(shares, DEEP)
-        (shares,) = call(tile_kernel, "tile", SHORT, [far(near, size, rank)], shares)
+        (shares,) = call(tile_kernel, "tile", SHORT, [far(near, *share)], shares)
         shares = exchange(shares, NEAR)
 
     with jax.named_scope("factor"):
-        (inverse,) = call(factor_kernel, "factor", 10**10, [f32(rank, rank)], shares)
+        (inverse,) = call(
+            factor_kernel,
+            "factor",
+            10**10,
+            [f32(rank, rank)],
+            shares,
+            scratch=[pltpu.VMEM((rank // 2, 3 * rank // 2), jnp.float32)],
+        )
 
     with jax.named_scope("gather"):
         blocks = [own] + [shifted(own, "y", k) for k in range(1, GROUPS)]

time: 129 us -> 127 us (0.984)
  waiting for transfers between devices: 29.7 us -> 28.4 us
    all_to_all x5, waiting for transfers between devices: 29.7 us -> 28.4 us  [exchange(): return lax.all_to_all(blocks, axes, 0, 0)]
  transfers between devices with their start and end apart: 9 -> 9, of which waited for: 4 -> 4; matrix products, arithmetic and copies ran while one was open for 0% -> 0% of each run, Pallas kernels for 15% -> 16%
where the time goes in v7:
time: 127 us
  starting transfers between devices  57.5 us (45%)
  waiting for transfers between devices  28.4 us (22%)
  Pallas kernels  25.3 us (20%)
  blocking collectives  13.2 us (10%)
  local copies, waits for them, and re-layouts  1.29 us (1%)
    all_to_all x5, starting transfers between devices, exchange(): return lax.all_to_all(blocks, axes, 0, 0)  43.4 us
    all_to_all x5, waiting for transfers between devices, exchange(): return lax.all_to_all(blocks, axes, 0, 0)  28.4 us
    pallas_call x6, Pallas kernels, call(): pl.pallas_call(kernel, out_shape=outs, in_specs=[smem if a.ndim == 1 else...  15.9 us
    all_to_all x1, blocking collectives, exchange(): return lax.all_to_all(blocks, axes, 0, 0)  13.2 us
    ppermute x3, starting transfers between devices, shifted(): lax.ppermute(value, axis, [(i, (i + by) % count) for i in range(count)])  10.7 us
    pallas_call x2, Pallas kernels, moment_blocks(): pl.pallas_call(moment_kernel, out_shape=far(count, rank, width), in_specs...  6.17 us
    ppermute x1, starting transfers between devices, on_device(): away = lax.ppermute(away, 'core', [(0, 1), (1, 0)])  3.37 us
    pallas_call x1, Pallas kernels, sketch_blocks(): pl.pallas_call(sketch_kernel, out_shape=[f32(blocks, rows // blocks, rank...  3.18 us
  transfers between devices with their start and end apart: 9, of which 4 were waited for; matrix products, arithmetic and copies ran while one was open for 0% of the time, Pallas kernels for 16%

profile of v7, /device:TPU:1, one launch (start us, length us, event | category | flops | bytes accessed | tf_op | source)
XLA Modules:
  0.0 126.6 jit_solution(428696037187227050)
XLA Ops:
  0.6 3.2 %sketch.1 = (f32[4,192,256]{2,1,0:T(8,128)S(1)}, bf16[768,2048]{1,0:T(8,128)(2,1)S(1)}) custom-call(bf16[768,2048]{1,0:T(8,128)(2,1)} %gradients.1, bf16[2048,256]{1,0:T(8,128)(2,1)} %projection.1), custom_call_target="tpu_custom_call" | custom-call | flops 805306368 | bytes 4194304 | tf_op jit(solution)/shard_map/sketch/sketch/pallas_call | solution.py:172
  3.8 13.2 %all_to_all.30.parts = f32[4,192,256]{2,1,0:T(8,128)S(1)} all-to-all(f32[4,192,256]{2,1,0:T(8,128)S(1)} %get-tuple-element.6), channel_id=1, replica_groups=mesh['far'=8,'pair'=2,'x'=4,'core'=2,'y'=4] {'y'}, dimensions={0} | all-to-all | bytes 1572864 | tf_op jit(solution)/shard_map/sketch/all_to_all | solution.py:25
  17.0 1.2 gram.1
  18.2 10.0 %all-to-all-start.1 = ((f32[32,4,384]{2,1,0:T(4,128)}), f32[32,4,384]{2,1,0:T(4,128)S(1)}, u32[]{:S(2)}, u32[]{:S(2)}) async-start(f32[32,4,384]{2,1,0:T(4,128)} %get-tuple-element.7), calls=%async_computation.1 | async-start | bytes 393216 | tf_op jit(solution)/shard_map/gram/all_to_all | solution.py:25
  28.2 0.1 pad_add_fusion.1.place
  28.2 3.3 %collective-permute-start = (f32[192,256]{1,0:T(8,128)}, f32[192,256]{1,0:T(8,128)S(1)}, u32[]{:S(2)}, u32[]{:S(2)}) collective-permute-start(f32[192,256]{1,0:T(8,128)} %get-tuple-element.8.refs_0_), channel_id=1, source_target_pairs={{0,1},{1,2},{2,3},{3,0},{4,5},{5,6},{6,7},{7,4},{8,9},{9,10},{10,1... | collective-permute-start | bytes 589832 | tf_op jit(solution)/shard_map/gather/ppermute | solution.py:30
  31.5 4.3 %collective-permute-start.1 = (f32[192,256]{1,0:T(8,128)}, f32[192,256]{1,0:T(8,128)}, u32[]{:S(2)}, u32[]{:S(2)}) collective-permute-start(f32[192,256]{1,0:T(8,128)} %get-tuple-element.8.refs_0_), channel_id=1, source_target_pairs={{0,2},{1,3},{2,0},{3,1},{4,6},{5,7},{6,4},{7,5},{8,10},{9,11},{10,... | collective-permute-start | bytes 589832 | tf_op jit(solution)/shard_map/gather/ppermute | solution.py:30
  35.8 3.1 %collective-permute-start.2 = (f32[192,256]{1,0:T(8,128)}, f32[192,256]{1,0:T(8,128)}, u32[]{:S(2)}, u32[]{:S(2)}) collective-permute-start(f32[192,256]{1,0:T(8,128)} %get-tuple-element.8.refs_0_), channel_id=1, source_target_pairs={{0,3},{1,0},{2,1},{3,2},{4,7},{5,4},{6,5},{7,6},{8,11},{9,8},{10,9... | collective-permute-start | bytes 589832 | tf_op jit(solution)/shard_map/gather/ppermute | solution.py:30
  38.9 0.0 all-to-all-done.1.parts
  38.9 0.7 tile.2
  39.6 14.9 %all-to-all-start.2 = ((f32[16,4,384]{2,1,0:T(4,128)}), f32[16,4,384]{2,1,0:T(4,128)S(1)}, u32[]{:S(2)}, u32[]{:S(2)}) async-start(f32[16,4,384]{2,1,0:T(4,128)} %tile.2), calls=%async_computation.2 | async-start | bytes 196608 | tf_op jit(solution)/shard_map/gram/all_to_all | solution.py:25
  54.6 0.0 collective-permute-done.refs_1_
  54.6 0.0 collective-permute-done.1.refs_2_
  54.6 0.0 collective-permute-done.2.refs_3_
  54.6 0.7 copy-done
  55.3 2.9 %moment.2 = f32[8,256,128]{2,1,0:T(8,128)} custom-call(s32[2]{0:T(128)S(1)} %pad_add_fusion.1.place, bf16[768,2048]{1,0:T(8,128)(2,1)S(1)} %get-tuple-element.9.gradients, f32[192,256]{1,0:T(8,128)} %get-tuple-element.8.refs_0_, f32[192,256]{1,0:T(8,128)} %copy-done, f32[192,256]{1,0:T(8,128)} %collective-permute-done.1.refs_2_, ...), custom_call_target="tpu_custom_call" | custom-call | flops 30000001024 | bytes 2621440 | tf_op jit(solution)/shard_map/moment/moment/pallas_call | solution.py:221
  58.2 3.4 %collective-permute-start.3 = (f32[8,256,128]{2,1,0:T(8,128)}, f32[8,256,128]{2,1,0:T(8,128)}, u32[]{:S(2)}, u32[]{:S(2)}) collective-permute-start(f32[8,256,128]{2,1,0:T(8,128)} %moment.2), channel_id=1, source_target_pairs={{0,4},{4,0},{1,5},{5,1},{2,6},{6,2},{3,7},{7,3},{8,12},{12,8},{9,1... | collective-permute-start | bytes 3145736 | tf_op jit(solution)/shard_map/moment/ppermute | solution.py:287
  61.5 4.9 %all-to-all-done.2.parts = f32[16,4,384]{2,1,0:T(4,128)S(1)} async-done(((f32[16,4,384]{2,1,0:T(4,128)}), f32[16,4,384]{2,1,0:T(4,128)S(1)}, u32[]{:S(2)}, u32[]{:S(2)}) %all-to-all-start.2) | async-done | bytes 98336 | tf_op jit(solution)/shard_map/gram/all_to_all | solution.py:25
  66.4 0.7 tile.3
  67.1 7.2 %all-to-all-start.3 = ((f32[32,4,384]{2,1,0:T(4,128)}), f32[32,4,384]{2,1,0:T(4,128)S(1)}, u32[]{:S(2)}, u32[]{:S(2)}) async-start(f32[32,4,384]{2,1,0:T(4,128)} %tile.3), calls=%async_computation.3 | async-start | bytes 393216 | tf_op jit(solution)/shard_map/gram/all_to_all | solution.py:25
  74.4 0.1 pad_add_fusion.place
  74.4 0.0 collective-permute-done.3.refs_4_
  74.4 3.3 %moment.3 = f32[8,256,128]{2,1,0:T(8,128)} custom-call(s32[2]{0:T(128)S(1)} %pad_add_fusion.place, bf16[768,2048]{1,0:T(8,128)(2,1)S(1)} %get-tuple-element.9.gradients, f32[192,256]{1,0:T(8,128)} %get-tuple-element.8.refs_0_, f32[192,256]{1,0:T(8,128)} %copy-done, f32[192,256]{1,0:T(8,128)} %collective-permute-done.1.refs_2_, ...), custom_call_target="tpu_custom_call" | custom-call | flops 1000000000 | bytes 2621440 | tf_op jit(solution)/shard_map/moment/moment/pallas_call | solution.py:221
  77.7 4.8 %all-to-all-done.3.shares = f32[32,4,384]{2,1,0:T(4,128)S(1)} async-done(((f32[32,4,384]{2,1,0:T(4,128)}), f32[32,4,384]{2,1,0:T(4,128)S(1)}, u32[]{:S(2)}, u32[]{:S(2)}) %all-to-all-start.3) | async-done | bytes 196640 | tf_op jit(solution)/shard_map/gram/all_to_all | solution.py:25
  82.5 3.6 %all-to-all-start.4 = ((f32[8,256,128]{2,1,0:T(8,128)}), f32[8,256,128]{2,1,0:T(8,128)S(1)}, u32[]{:S(2)}, u32[]{:S(2)}) async-start(f32[8,256,128]{2,1,0:T(8,128)} %moment.3), calls=%async_computation.4 | async-start | bytes 2097152 | tf_op jit(solution)/shard_map/moment/all_to_all | solution.py:25
  86.1 9.0 %factor.1.inverse = f32[256,256]{1,0:T(8,128)S(1)} custom-call(f32[32,4,384]{2,1,0:T(4,128)S(1)} %all-to-all-done.3.shares), custom_call_target="tpu_custom_call" | custom-call | flops 10000000000 | bytes 458752 | tf_op jit(solution)/shard_map/factor/factor/pallas_call | solution.py:86
  95.1 5.9 %all-to-all-done.4.parts = f32[8,256,128]{2,1,0:T(8,128)S(1)} async-done(((f32[8,256,128]{2,1,0:T(8,128)}), f32[8,256,128]{2,1,0:T(8,128)S(1)}, u32[]{:S(2)}, u32[]{:S(2)}) %all-to-all-start.4) | async-done | bytes 1048608 | tf_op jit(solution)/shard_map/moment/all_to_all | solution.py:25
  101.0 1.0 solve.1
  102.0 7.8 %all-to-all-start.5 = ((f32[128,2,128]{2,1,0:T(2,128)}), f32[128,2,128]{2,1,0:T(2,128)S(1)}, u32[]{:S(2)}, u32[]{:S(2)}) async-start(f32[128,2,128]{2,1,0:T(2,128)} %solve.1), calls=%async_computation.5 | async-start | bytes 262144 | tf_op jit(solution)/shard_map/reduced/all_to_all | solution.py:25
  109.8 3.3 %basis.1 = f32[768,256]{1,0:T(8,128)} custom-call(s32[1]{0:T(128)} %bitcast.place, f32[256,256]{1,0:T(8,128)S(1)} %factor.1.inverse, f32[192,256]{1,0:T(8,128)} %get-tuple-element.8.refs_0_, f32[192,256]{1,0:T(8,128)} %copy-done, f32[192,256]{1,0:T(8,128)} %collective-permute-done.1.refs_2_, f32[192,256]{1,0:T(8,128)} %collective-permute-done.2.refs_3_), custom_call_target="tpu_custom_call" | custom-call | flops 603979776 | bytes 1835012 | tf_op jit(solution)/shard_map/basis/basis/pallas_call | solution.py:86
  113.1 12.8 %all-to-all-done.5 = f32[128,2,128]{2,1,0:T(2,128)S(1)} async-done(((f32[128,2,128]{2,1,0:T(2,128)}), f32[128,2,128]{2,1,0:T(2,128)S(1)}, u32[]{:S(2)}, u32[]{:S(2)}) %all-to-all-start.5) | async-done | bytes 131104 | tf_op jit(solution)/shard_map/reduced/all_to_all | solution.py:25
  126.0 0.6 reshape.11
  (3 shorter events, 0.1 us)
Async XLA Ops:
  18.2 20.8 %all-to-all-start.1 = ((f32[32,4,384]{2,1,0:T(4,128)}), f32[32,4,384]{2,1,0:T(4,128)S(1)}, u32[]{:S(2)}, u32[]{:S(2)}) async-start(f32[32,4,384]{2,1,0:T(4,128)} %get-tuple-element.7), calls=%async_computation.1 | async-start | bytes 393216 | tf_op jit(solution)/shard_map/gram/all_to_all | solution.py:25
  28.2 26.3 %collective-permute-start = (f32[192,256]{1,0:T(8,128)}, f32[192,256]{1,0:T(8,128)S(1)}, u32[]{:S(2)}, u32[]{:S(2)}) collective-permute-start(f32[192,256]{1,0:T(8,128)} %get-tuple-element.8.refs_0_), channel_id=1, source_target_pairs={{0,1},{1,2},{2,3},{3,0},{4,5},{5,6},{6,7},{7,4},{8,9},{9,10},{10,1... | collective-permute-start | bytes 589832 | tf_op jit(solution)/shard_map/gather/ppermute | solution.py:30
  31.5 23.1 %collective-permute-start.1 = (f32[192,256]{1,0:T(8,128)}, f32[192,256]{1,0:T(8,128)}, u32[]{:S(2)}, u32[]{:S(2)}) collective-permute-start(f32[192,256]{1,0:T(8,128)} %get-tuple-element.8.refs_0_), channel_id=1, source_target_pairs={{0,2},{1,3},{2,0},{3,1},{4,6},{5,7},{6,4},{7,5},{8,10},{9,11},{10,... | collective-permute-start | bytes 589832 | tf_op jit(solution)/shard_map/gather/ppermute | solution.py:30
  35.8 18.8 %collective-permute-start.2 = (f32[192,256]{1,0:T(8,128)}, f32[192,256]{1,0:T(8,128)}, u32[]{:S(2)}, u32[]{:S(2)}) collective-permute-start(f32[192,256]{1,0:T(8,128)} %get-tuple-element.8.refs_0_), channel_id=1, source_target_pairs={{0,3},{1,0},{2,1},{3,2},{4,7},{5,4},{6,5},{7,6},{8,11},{9,8},{10,9... | collective-permute-start | bytes 589832 | tf_op jit(solution)/shard_map/gather/ppermute | solution.py:30
  39.6 26.8 %all-to-all-start.2 = ((f32[16,4,384]{2,1,0:T(4,128)}), f32[16,4,384]{2,1,0:T(4,128)S(1)}, u32[]{:S(2)}, u32[]{:S(2)}) async-start(f32[16,4,384]{2,1,0:T(4,128)} %tile.2), calls=%async_computation.2 | async-start | bytes 196608 | tf_op jit(solution)/shard_map/gram/all_to_all | solution.py:25
  54.6 0.7 copy-start
  58.2 16.3 %collective-permute-start.3 = (f32[8,256,128]{2,1,0:T(8,128)}, f32[8,256,128]{2,1,0:T(8,128)}, u32[]{:S(2)}, u32[]{:S(2)}) collective-permute-start(f32[8,256,128]{2,1,0:T(8,128)} %moment.2), channel_id=1, source_target_pairs={{0,4},{4,0},{1,5},{5,1},{2,6},{6,2},{3,7},{7,3},{8,12},{12,8},{9,1... | collective-permute-start | bytes 3145736 | tf_op jit(solution)/shard_map/moment/ppermute | solution.py:287
  67.1 15.4 %all-to-all-start.3 = ((f32[32,4,384]{2,1,0:T(4,128)}), f32[32,4,384]{2,1,0:T(4,128)S(1)}, u32[]{:S(2)}, u32[]{:S(2)}) async-start(f32[32,4,384]{2,1,0:T(4,128)} %tile.3), calls=%async_computation.3 | async-start | bytes 393216 | tf_op jit(solution)/shard_map/gram/all_to_all | solution.py:25
  82.5 18.5 %all-to-all-start.4 = ((f32[8,256,128]{2,1,0:T(8,128)}), f32[8,256,128]{2,1,0:T(8,128)S(1)}, u32[]{:S(2)}, u32[]{:S(2)}) async-start(f32[8,256,128]{2,1,0:T(8,128)} %moment.3), calls=%async_computation.4 | async-start | bytes 2097152 | tf_op jit(solution)/shard_map/moment/all_to_all | solution.py:25
  102.0 23.8 %all-to-all-start.5 = ((f32[128,2,128]{2,1,0:T(2,128)}), f32[128,2,128]{2,1,0:T(2,128)S(1)}, u32[]{:S(2)}, u32[]{:S(2)}) async-start(f32[128,2,128]{2,1,0:T(2,128)} %solve.1), calls=%async_computation.5 | async-start | bytes 262144 | tf_op jit(solution)/shard_map/reduced/all_to_all | solution.py:25

commit v8 on v7

--- a/solution.py
+++ b/solution.py
@@ -12,7 +12,6 @@
 HIGHEST = lax.Precision.HIGHEST
 ROWS = ("far", "pair", "x", "core")
 DEEP = ("far", "pair")
-CROSS = ("pair", "x")
 NEAR = ("x", "core", "y")
 GROUPS = 4
 PIECES = 4
@@ -172,7 +171,7 @@
     return pl.pallas_call(
         sketch_kernel,
         out_shape=[
-            f32(blocks, rows // blocks, rank),
+            far(blocks, rows // blocks, rank),
             jax.ShapeDtypeStruct(gradients.shape, gradients.dtype),
         ],
         in_specs=[pl.BlockSpec(memory_space=pltpu.HBM)] * 2,
@@ -238,6 +237,17 @@
     )(place, gradients, *blocks, *added)
 
 
+def part_kernel(pair, local, away, kept, given):
+    count = kept.shape[0]
+    for n, out in enumerate((kept, given)):
+        rows = pl.ds(lax.rem(pair[0] + n, 2) * count, count)
+        out[...] = local[rows] + away[rows]
+
+
+def add_kernel(a, b, out):
+    out[...] = a[...] + b[...]
+
+
 def on_device(gradients, projection):
     rows, feats = gradients.shape
     rank = projection.shape[1]
@@ -262,10 +272,33 @@
             parts,
         )
         shares = exchange(shares, NEAR)
+
+    with jax.named_scope("gather"):
+        blocks = [own] + [shifted(own, "y", k) for k in range(1, GROUPS)]
+        blocks = [pltpu.with_memory_space_constraint(b, pltpu.HBM) for b in blocks]
+
+    with jax.named_scope("moment"):
+        swap = [(0, 1), (1, 0)]
+        pair = lax.axis_index("pair").astype(jnp.int32)
+        count = pairs * xs
+        away = moment_blocks(jnp.stack([1 - core, mine]), held, blocks, count, 10**8)
+        away = lax.ppermute(away, "core", swap)
+        local = moment_blocks(jnp.stack([core, mine]), held, blocks, count, SHORT)
+        local = pltpu.with_memory_space_constraint(local, pltpu.HBM)
+        kept, given = call(
+            part_kernel, "part", 0, [far(xs, rank, width)] * 2, pair[None], local, away
+        )
+        given = lax.ppermute(given, "pair", swap)
+        (moment,) = call(add_kernel, "add", 0, [far(xs, rank, width)], kept, given)
+
+    with jax.named_scope("gram"):
         (shares,) = call(tile_kernel, "tile", SHORT, [far(deep, *share)], shares)
         shares = exchange(shares, DEEP)
         (shares,) = call(tile_kernel, "tile", SHORT, [far(near, *share)], shares)
         shares = exchange(shares, NEAR)
+
+    with jax.named_scope("moment"):
+        moment = exchange(moment, "x")
 
     with jax.named_scope("factor"):
         (inverse,) = call(
@@ -276,19 +309,6 @@
             shares,
             scratch=[pltpu.VMEM((rank // 2, 3 * rank // 2), jnp.float32)],
         )
-
-    with jax.named_scope("gather"):
-        blocks = [own] + [shifted(own, "y", k) for k in range(1, GROUPS)]
-        blocks = [pltpu.with_memory_space_constraint(b, pltpu.HBM) for b in blocks]
-
-    with jax.named_scope("moment"):
-        count = pairs * xs
-        away = moment_blocks(jnp.stack([1 - core, mine]), held, blocks, count, SHORT)
-        away = lax.ppermute(away, "core", [(0, 1), (1, 0)])
-        moment = moment_blocks(
-            jnp.stack([core, mine]), held, blocks, count, 10**9, away
-        )
-        moment = exchange(moment, CROSS)
 
     with jax.named_scope("reduced"):
         (parts,) = call(

time: 127 us -> 135 us (1.063)
  starting transfers between devices: 57.5 us -> 73.1 us
  blocking collectives: 13.2 us -> 0 us
  Pallas kernels: 25.3 us -> 30 us
    all_to_all x1 -> x0, blocking collectives: 13.2 us -> none  [exchange(): return lax.all_to_all(blocks, axes, 0, 0)]
    all_to_all x5 -> x6, starting transfers between devices: 43.4 us -> 55.4 us  [exchange(): return lax.all_to_all(blocks, axes, 0, 0)]
    ppermute x1 -> x2, waiting for transfers between devices: 0.01 us -> 6.93 us  [the longest x1 6.93 us: on_device(): given = lax.ppermute(given, 'pair', swap)]
    all_to_all x5 -> x6, waiting for transfers between devices: 28.4 us -> 21.6 us  [exchange(): return lax.all_to_all(blocks, axes, 0, 0)]
    pallas_call x6 -> x8, Pallas kernels: 15.9 us -> 20.2 us  [call(): pl.pallas_call(kernel, out_shape=outs, in_specs=[smem if a.ndim == 1 else...]
    ppermute x1 -> x2, starting transfers between devices: 3.37 us -> 7.04 us  [the longest x1 3.66 us: on_device(): given = lax.ppermute(given, 'pair', swap)]
  transfers between devices with their start and end apart: 9 -> 11, of which waited for: 4 -> 4; matrix products, arithmetic and copies ran while one was open for 0% -> 0% of each run, Pallas kernels for 16% -> 17%
where the time goes in v8:
time: 135 us; the launch traced here: 134 us
  starting transfers between devices  73.1 us (54%)
  Pallas kernels  30 us (22%)
  waiting for transfers between devices  28.5 us (21%)
    all_to_all x6, starting transfers between devices, exchange(): return lax.all_to_all(blocks, axes, 0, 0)  55.4 us
    all_to_all x6, waiting for transfers between devices, exchange(): return lax.all_to_all(blocks, axes, 0, 0)  21.6 us
    pallas_call x8, Pallas kernels, call(): pl.pallas_call(kernel, out_shape=outs, in_specs=[smem if a.ndim == 1 else...  20.2 us
    ppermute x3, starting transfers between devices, shifted(): lax.ppermute(value, axis, [(i, (i + by) % count) for i in range(count)])  10.7 us
    ppermute x1, waiting for transfers between devices, on_device(): given = lax.ppermute(given, 'pair', swap)  6.93 us
    pallas_call x2, Pallas kernels, moment_blocks(): pl.pallas_call(moment_kernel, out_shape=far(count, rank, width), in_specs...  5.75 us
    pallas_call x1, Pallas kernels, sketch_blocks(): pl.pallas_call(sketch_kernel, out_shape=[far(blocks, rows // blocks, rank...  4.06 us
    ppermute x1, starting transfers between devices, on_device(): given = lax.ppermute(given, 'pair', swap)  3.66 us
  transfers between devices with their start and end apart: 11, of which 4 were waited for; matrix products, arithmetic and copies ran while one was open for 0% of the time, Pallas kernels for 17%

profile of v8, /device:TPU:1, one launch (start us, length us, event | category | flops | bytes accessed | tf_op | source)
XLA Modules:
  0.0 133.9 jit_solution(4391693914764933508)
XLA Ops:
  0.6 4.1 %sketch.1 = (f32[4,192,256]{2,1,0:T(8,128)}, bf16[768,2048]{1,0:T(8,128)(2,1)S(1)}) custom-call(bf16[768,2048]{1,0:T(8,128)(2,1)} %gradients.1, bf16[2048,256]{1,0:T(8,128)(2,1)} %projection.1), custom_call_target="tpu_custom_call" | custom-call | flops 805306368 | bytes 4194304 | tf_op jit(solution)/shard_map/sketch/sketch/pallas_call | solution.py:171
  4.7 5.0 %all-to-all-start = ((f32[4,192,256]{2,1,0:T(8,128)}), f32[4,192,256]{2,1,0:T(8,128)}, u32[]{:S(2)}, u32[]{:S(2)}) async-start(f32[4,192,256]{2,1,0:T(8,128)} %get-tuple-element.8), calls=%async_computation | async-start | bytes 1572864 | tf_op jit(solution)/shard_map/sketch/all_to_all | solution.py:24
  9.7 8.4 %all-to-all-done.parts = f32[4,192,256]{2,1,0:T(8,128)} async-done(((f32[4,192,256]{2,1,0:T(8,128)}), f32[4,192,256]{2,1,0:T(8,128)}, u32[]{:S(2)}, u32[]{:S(2)}) %all-to-all-start) | async-done | bytes 786464 | tf_op jit(solution)/shard_map/sketch/all_to_all | solution.py:24
  18.2 2.3 %gram.1 = (f32[192,256]{1,0:T(8,128)}, f32[32,4,384]{2,1,0:T(4,128)}) custom-call(f32[4,192,256]{2,1,0:T(8,128)} %all-to-all-done.parts), custom_call_target="tpu_custom_call" | custom-call | flops 150994944 | bytes 1179648 | tf_op jit(solution)/shard_map/gram/gram/pallas_call | solution.py:85
  20.5 10.7 %all-to-all-start.1 = ((f32[32,4,384]{2,1,0:T(4,128)}), f32[32,4,384]{2,1,0:T(4,128)S(1)}, u32[]{:S(2)}, u32[]{:S(2)}) async-start(f32[32,4,384]{2,1,0:T(4,128)} %get-tuple-element.9), calls=%async_computation.1 | async-start | bytes 393216 | tf_op jit(solution)/shard_map/gram/all_to_all | solution.py:24
  31.2 0.1 pad_add_fusion.1.place
  31.3 0.1 pad_add_fusion.place
  31.4 3.3 %collective-permute-start = (f32[192,256]{1,0:T(8,128)}, f32[192,256]{1,0:T(8,128)S(1)}, u32[]{:S(2)}, u32[]{:S(2)}) collective-permute-start(f32[192,256]{1,0:T(8,128)} %get-tuple-element.10.refs_0_), channel_id=1, source_target_pairs={{0,1},{1,2},{2,3},{3,0},{4,5},{5,6},{6,7},{7,4},{8,9},{9,10},{10,1... | collective-permute-start | bytes 589832 | tf_op jit(solution)/shard_map/gather/ppermute | solution.py:29
  34.7 4.3 %collective-permute-start.1 = (f32[192,256]{1,0:T(8,128)}, f32[192,256]{1,0:T(8,128)}, u32[]{:S(2)}, u32[]{:S(2)}) collective-permute-start(f32[192,256]{1,0:T(8,128)} %get-tuple-element.10.refs_0_), channel_id=1, source_target_pairs={{0,2},{1,3},{2,0},{3,1},{4,6},{5,7},{6,4},{7,5},{8,10},{9,11},{10,... | collective-permute-start | bytes 589832 | tf_op jit(solution)/shard_map/gather/ppermute | solution.py:29
  39.0 3.1 %collective-permute-start.2 = (f32[192,256]{1,0:T(8,128)}, f32[192,256]{1,0:T(8,128)}, u32[]{:S(2)}, u32[]{:S(2)}) collective-permute-start(f32[192,256]{1,0:T(8,128)} %get-tuple-element.10.refs_0_), channel_id=1, source_target_pairs={{0,3},{1,0},{2,1},{3,2},{4,7},{5,4},{6,5},{7,6},{8,11},{9,8},{10,9... | collective-permute-start | bytes 589832 | tf_op jit(solution)/shard_map/gather/ppermute | solution.py:29
  42.1 0.0 all-to-all-done.1.parts
  42.1 0.7 tile.2
  42.8 14.2 %all-to-all-start.2 = ((f32[16,4,384]{2,1,0:T(4,128)}), f32[16,4,384]{2,1,0:T(4,128)S(1)}, u32[]{:S(2)}, u32[]{:S(2)}) async-start(f32[16,4,384]{2,1,0:T(4,128)} %tile.2), calls=%async_computation.2 | async-start | bytes 196608 | tf_op jit(solution)/shard_map/gram/all_to_all | solution.py:24
  57.0 0.0 collective-permute-done.refs_1_
  57.0 0.7 copy-done.1
  57.7 2.9 %moment.3 = f32[8,256,128]{2,1,0:T(8,128)} custom-call(s32[2]{0:T(128)S(1)} %pad_add_fusion.1.place, bf16[768,2048]{1,0:T(8,128)(2,1)S(1)} %get-tuple-element.11.gradients, f32[192,256]{1,0:T(8,128)} %get-tuple-element.10.refs_0_, f32[192,256]{1,0:T(8,128)} %copy-done.1, f32[192,256]{1,0:T(8,128)} %collective-permute-done.1.refs_2_, ...), custom_call_target="tpu_custom_call" | custom-call | flops 100000000 | bytes 2621440 | tf_op jit(solution)/shard_map/moment/moment/pallas_call | solution.py:220
  60.5 3.4 %collective-permute-start.3 = (f32[8,256,128]{2,1,0:T(8,128)}, f32[8,256,128]{2,1,0:T(8,128)S(1)}, u32[]{:S(2)}, u32[]{:S(2)}) collective-permute-start(f32[8,256,128]{2,1,0:T(8,128)} %moment.3), channel_id=1, source_target_pairs={{0,4},{4,0},{1,5},{5,1},{2,6},{6,2},{3,7},{7,3},{8,12},{12,8},{9,1... | collective-permute-start | bytes 3145736 | tf_op jit(solution)/shard_map/moment/ppermute | solution.py:285
  63.9 2.9 %moment.2.local = f32[8,256,128]{2,1,0:T(8,128)} custom-call(s32[2]{0:T(128)S(1)} %pad_add_fusion.place, bf16[768,2048]{1,0:T(8,128)(2,1)S(1)} %get-tuple-element.11.gradients, f32[192,256]{1,0:T(8,128)} %get-tuple-element.10.refs_0_, f32[192,256]{1,0:T(8,128)} %copy-done.1, f32[192,256]{1,0:T(8,128)} %collective-permute-done.1.refs_2_, ...), custom_call_target="tpu_custom_call" | custom-call | flops 30000001024 | bytes 2621440 | tf_op jit(solution)/shard_map/moment/moment/pallas_call | solution.py:220
  66.8 2.3 %part.1 = (f32[4,256,128]{2,1,0:T(8,128)}, f32[4,256,128]{2,1,0:T(8,128)}) custom-call(s32[1]{0:T(128)} %bitcast.1.pair, f32[8,256,128]{2,1,0:T(8,128)} %moment.2.local, f32[8,256,128]{2,1,0:T(8,128)S(1)} %collective-permute-done.3.away), custom_call_target="tpu_custom_call" | custom-call | bytes 3145732 | tf_op jit(solution)/shard_map/moment/part/pallas_call | solution.py:85
  69.1 3.7 %collective-permute-start.4 = (f32[4,256,128]{2,1,0:T(8,128)}, f32[4,256,128]{2,1,0:T(8,128)S(1)}, u32[]{:S(2)}, u32[]{:S(2)}) collective-permute-start(f32[4,256,128]{2,1,0:T(8,128)} %get-tuple-element.13), channel_id=1, source_target_pairs={{0,32},{32,0},{1,33},{33,1},{2,34},{34,2},{3,35},{35,3},{4,36},{36... | collective-permute-start | bytes 1572872 | tf_op jit(solution)/shard_map/moment/ppermute | solution.py:291
  72.8 0.7 tile.3
  73.5 4.7 %all-to-all-start.3 = ((f32[32,4,384]{2,1,0:T(4,128)}), f32[32,4,384]{2,1,0:T(4,128)S(1)}, u32[]{:S(2)}, u32[]{:S(2)}) async-start(f32[32,4,384]{2,1,0:T(4,128)} %tile.3), calls=%async_computation.3 | async-start | bytes 393216 | tf_op jit(solution)/shard_map/gram/all_to_all | solution.py:24
  78.2 6.9 %collective-permute-done.4.b = f32[4,256,128]{2,1,0:T(8,128)S(1)} collective-permute-done((f32[4,256,128]{2,1,0:T(8,128)}, f32[4,256,128]{2,1,0:T(8,128)S(1)}, u32[]{:S(2)}, u32[]{:S(2)}) %collective-permute-start.4) | collective-permute-done | bytes 524320 | tf_op jit(solution)/shard_map/moment/ppermute | solution.py:291
  85.2 0.8 add.5
  86.0 0.4 all-to-all-done.3.shares
  86.4 3.6 %all-to-all-start.4 = ((f32[4,256,128]{2,1,0:T(8,128)}), f32[4,256,128]{2,1,0:T(8,128)S(1)}, u32[]{:S(2)}, u32[]{:S(2)}) async-start(f32[4,256,128]{2,1,0:T(8,128)} %add.5), calls=%async_computation.4 | async-start | bytes 1048576 | tf_op jit(solution)/shard_map/moment/all_to_all | solution.py:24
  90.0 9.0 %factor.1.inverse = f32[256,256]{1,0:T(8,128)S(1)} custom-call(f32[32,4,384]{2,1,0:T(4,128)S(1)} %all-to-all-done.3.shares), custom_call_target="tpu_custom_call" | custom-call | flops 10000000000 | bytes 458752 | tf_op jit(solution)/shard_map/factor/factor/pallas_call | solution.py:85
  99.0 1.0 solve.1
  100.0 17.2 %all-to-all-start.5 = ((f32[128,2,128]{2,1,0:T(2,128)}), f32[128,2,128]{2,1,0:T(2,128)S(1)}, u32[]{:S(2)}, u32[]{:S(2)}) async-start(f32[128,2,128]{2,1,0:T(2,128)} %solve.1), calls=%async_computation.5 | async-start | bytes 262144 | tf_op jit(solution)/shard_map/reduced/all_to_all | solution.py:24
  117.2 3.3 %basis.1 = f32[768,256]{1,0:T(8,128)} custom-call(s32[1]{0:T(128)} %bitcast.place, f32[256,256]{1,0:T(8,128)S(1)} %factor.1.inverse, f32[192,256]{1,0:T(8,128)} %get-tuple-element.10.refs_0_, f32[192,256]{1,0:T(8,128)} %copy-done.1, f32[192,256]{1,0:T(8,128)} %collective-permute-done.1.refs_2_, f32[192,256]{1,0:T(8,128)} %collective-permute-done.2.refs_3_), custom_call_target="tpu_custom_call" | custom-call | flops 603979776 | bytes 1835012 | tf_op jit(solution)/shard_map/basis/basis/pallas_call | solution.py:85
  120.5 12.7 %all-to-all-done.5 = f32[128,2,128]{2,1,0:T(2,128)S(1)} async-done(((f32[128,2,128]{2,1,0:T(2,128)}), f32[128,2,128]{2,1,0:T(2,128)S(1)}, u32[]{:S(2)}, u32[]{:S(2)}) %all-to-all-start.5) | async-done | bytes 131104 | tf_op jit(solution)/shard_map/reduced/all_to_all | solution.py:24
  133.3 0.6 reshape.11
  (10 shorter events, 0.1 us)
Async XLA Ops:
  4.7 13.5 %all-to-all-start = ((f32[4,192,256]{2,1,0:T(8,128)}), f32[4,192,256]{2,1,0:T(8,128)}, u32[]{:S(2)}, u32[]{:S(2)}) async-start(f32[4,192,256]{2,1,0:T(8,128)} %get-tuple-element.8), calls=%async_computation | async-start | bytes 1572864 | tf_op jit(solution)/shard_map/sketch/all_to_all | solution.py:24
  20.5 21.6 %all-to-all-start.1 = ((f32[32,4,384]{2,1,0:T(4,128)}), f32[32,4,384]{2,1,0:T(4,128)S(1)}, u32[]{:S(2)}, u32[]{:S(2)}) async-start(f32[32,4,384]{2,1,0:T(4,128)} %get-tuple-element.9), calls=%async_computation.1 | async-start | bytes 393216 | tf_op jit(solution)/shard_map/gram/all_to_all | solution.py:24
  31.4 25.6 %collective-permute-start = (f32[192,256]{1,0:T(8,128)}, f32[192,256]{1,0:T(8,128)S(1)}, u32[]{:S(2)}, u32[]{:S(2)}) collective-permute-start(f32[192,256]{1,0:T(8,128)} %get-tuple-element.10.refs_0_), channel_id=1, source_target_pairs={{0,1},{1,2},{2,3},{3,0},{4,5},{5,6},{6,7},{7,4},{8,9},{9,10},{10,1... | collective-permute-start | bytes 589832 | tf_op jit(solution)/shard_map/gather/ppermute | solution.py:29
  34.7 22.3 %collective-permute-start.1 = (f32[192,256]{1,0:T(8,128)}, f32[192,256]{1,0:T(8,128)}, u32[]{:S(2)}, u32[]{:S(2)}) collective-permute-start(f32[192,256]{1,0:T(8,128)} %get-tuple-element.10.refs_0_), channel_id=1, source_target_pairs={{0,2},{1,3},{2,0},{3,1},{4,6},{5,7},{6,4},{7,5},{8,10},{9,11},{10,... | collective-permute-start | bytes 589832 | tf_op jit(solution)/shard_map/gather/ppermute | solution.py:29
  39.0 18.0 %collective-permute-start.2 = (f32[192,256]{1,0:T(8,128)}, f32[192,256]{1,0:T(8,128)}, u32[]{:S(2)}, u32[]{:S(2)}) collective-permute-start(f32[192,256]{1,0:T(8,128)} %get-tuple-element.10.refs_0_), channel_id=1, source_target_pairs={{0,3},{1,0},{2,1},{3,2},{4,7},{5,4},{6,5},{7,6},{8,11},{9,8},{10,9... | collective-permute-start | bytes 589832 | tf_op jit(solution)/shard_map/gather/ppermute | solution.py:29
  42.8 30.0 %all-to-all-start.2 = ((f32[16,4,384]{2,1,0:T(4,128)}), f32[16,4,384]{2,1,0:T(4,128)S(1)}, u32[]{:S(2)}, u32[]{:S(2)}) async-start(f32[16,4,384]{2,1,0:T(4,128)} %tile.2), calls=%async_computation.2 | async-start | bytes 196608 | tf_op jit(solution)/shard_map/gram/all_to_all | solution.py:24
  57.0 0.7 copy-start.1
  60.5 6.3 %collective-permute-start.3 = (f32[8,256,128]{2,1,0:T(8,128)}, f32[8,256,128]{2,1,0:T(8,128)S(1)}, u32[]{:S(2)}, u32[]{:S(2)}) collective-permute-start(f32[8,256,128]{2,1,0:T(8,128)} %moment.3), channel_id=1, source_target_pairs={{0,4},{4,0},{1,5},{5,1},{2,6},{6,2},{3,7},{7,3},{8,12},{12,8},{9,1... | collective-permute-start | bytes 3145736 | tf_op jit(solution)/shard_map/moment/ppermute | solution.py:285
  69.1 16.1 %copy-start = (f32[4,256,128]{2,1,0:T(8,128)S(1)}, f32[4,256,128]{2,1,0:T(8,128)}, u32[]{:S(2)}) copy-start(f32[4,256,128]{2,1,0:T(8,128)} %get-tuple-element.12.a) | copy-start | bytes 1572868
  69.1 16.0 %collective-permute-start.4 = (f32[4,256,128]{2,1,0:T(8,128)}, f32[4,256,128]{2,1,0:T(8,128)S(1)}, u32[]{:S(2)}, u32[]{:S(2)}) collective-permute-start(f32[4,256,128]{2,1,0:T(8,128)} %get-tuple-element.13), channel_id=1, source_target_pairs={{0,32},{32,0},{1,33},{33,1},{2,34},{34,2},{3,35},{35,3},{4,36},{36... | collective-permute-start | bytes 1572872 | tf_op jit(solution)/shard_map/moment/ppermute | solution.py:291
  73.5 12.9 %all-to-all-start.3 = ((f32[32,4,384]{2,1,0:T(4,128)}), f32[32,4,384]{2,1,0:T(4,128)S(1)}, u32[]{:S(2)}, u32[]{:S(2)}) async-start(f32[32,4,384]{2,1,0:T(4,128)} %tile.3), calls=%async_computation.3 | async-start | bytes 393216 | tf_op jit(solution)/shard_map/gram/all_to_all | solution.py:24
  86.4 12.6 %all-to-all-start.4 = ((f32[4,256,128]{2,1,0:T(8,128)}), f32[4,256,128]{2,1,0:T(8,128)S(1)}, u32[]{:S(2)}, u32[]{:S(2)}) async-start(f32[4,256,128]{2,1,0:T(8,128)} %add.5), calls=%async_computation.4 | async-start | bytes 1048576 | tf_op jit(solution)/shard_map/moment/all_to_all | solution.py:24
  100.0 33.2 %all-to-all-start.5 = ((f32[128,2,128]{2,1,0:T(2,128)}), f32[128,2,128]{2,1,0:T(2,128)S(1)}, u32[]{:S(2)}, u32[]{:S(2)}) async-start(f32[128,2,128]{2,1,0:T(2,128)} %solve.1), calls=%async_computation.5 | async-start | bytes 262144 | tf_op jit(solution)/shard_map/reduced/all_to_all | solution.py:24

commit v9 on v7

--- a/solution.py
+++ b/solution.py
@@ -79,14 +79,15 @@
     return jnp.concatenate(done, 0)
 
 
-def call(kernel, name, flops, outs, *args, scratch=()):
+def call(kernel, name, flops, outs, *args, scratch=(), held=True):
     whole = pl.BlockSpec()
+    given = pl.BlockSpec(memory_space=pltpu.VMEM) if held else whole
     smem = pl.BlockSpec(memory_space=pltpu.SMEM)
     moved = sum(math.prod(a.shape) * a.dtype.itemsize for a in (*args, *outs))
     return pl.pallas_call(
         kernel,
         out_shape=outs,
-        in_specs=[smem if a.ndim == 1 else whole for a in args],
+        in_specs=[smem if a.ndim == 1 else given for a in args],
         out_specs=[whole] * len(outs),
         scratch_shapes=scratch,
         compiler_params=pltpu.CompilerParams(vmem_limit_bytes=VMEM_LIMIT),
@@ -148,6 +149,15 @@
 def solve_kernel(inverse, parts, out):
     total = jnp.sum(parts[...], 0)
     out[...] = dot(inverse[...], total, ((1,), (0,))).reshape(out.shape)
+
+
+def last_kernel(cores, parts, out):
+    width = parts.shape[2]
+    count = out.shape[1] // width
+    total = jnp.sum(parts[...].reshape(-1, count, *parts.shape[1:]), 0)
+    for i in range(count):
+        block = i % cores * (count // cores) + i // cores
+        out[:, block * width : (block + 1) * width] = total[i]
 
 
 def sketch_kernel(gradients, projection, partial, held, weights, sems):
@@ -300,8 +310,13 @@
             moment,
         )
         parts = exchange(parts, ROWS)
-        parts = parts.reshape(-1, pairs, xs, cores, rank // members_of_rows, width).sum(0)
-        reduced = parts.transpose(3, 2, 0, 1, 4).reshape(rank // members_of_rows, feats)
+        (reduced,) = call(
+            functools.partial(last_kernel, cores),
+            "last",
+            0,
+            [f32(rank // members_of_rows, feats)],
+            parts,
+        )
 
     with jax.named_scope("basis"):
         (basis,) = call(
@@ -312,6 +327,7 @@
             mine[None],
             inverse,
             *blocks,
+            held=False,
         )
     return (basis, reduced)
 

time: 127 us -> 127 us (level)
    pallas_call x6 -> x7, Pallas kernels: 15.9 us -> 16.6 us  [call(): pl.pallas_call(kernel, out_shape=outs, in_specs=[smem if a.ndim == 1 else...]
where the time goes in v9:
time: 127 us
  starting transfers between devices  57.4 us (45%)
  waiting for transfers between devices  28.4 us (22%)
  Pallas kernels  25.9 us (20%)
  blocking collectives  13.2 us (10%)
    all_to_all x5, starting transfers between devices, exchange(): return lax.all_to_all(blocks, axes, 0, 0)  43.4 us
    all_to_all x5, waiting for transfers between devices, exchange(): return lax.all_to_all(blocks, axes, 0, 0)  28.4 us
    pallas_call x7, Pallas kernels, call(): pl.pallas_call(kernel, out_shape=outs, in_specs=[smem if a.ndim == 1 else...  16.6 us
    all_to_all x1, blocking collectives, exchange(): return lax.all_to_all(blocks, axes, 0, 0)  13.2 us
    ppermute x3, starting transfers between devices, shifted(): lax.ppermute(value, axis, [(i, (i + by) % count) for i in range(count)])  10.7 us
    pallas_call x2, Pallas kernels, moment_blocks(): pl.pallas_call(moment_kernel, out_shape=far(count, rank, width), in_specs...  6.14 us
    ppermute x1, starting transfers between devices, on_device(): away = lax.ppermute(away, 'core', [(0, 1), (1, 0)])  3.37 us
    pallas_call x1, Pallas kernels, sketch_blocks(): pl.pallas_call(sketch_kernel, out_shape=[f32(blocks, rows // blocks, rank...  3.18 us
  transfers between devices with their start and end apart: 9, of which 4 were waited for; matrix products, arithmetic and copies ran while one was open for 0% of the time, Pallas kernels for 16%

profile of v9, /device:TPU:1, one launch (start us, length us, event | category | flops | bytes accessed | tf_op | source)
XLA Modules:
  0.0 126.5 jit_solution(11929678606259752773)
XLA Ops:
  0.6 3.2 %sketch.1 = (f32[4,192,256]{2,1,0:T(8,128)S(1)}, bf16[768,2048]{1,0:T(8,128)(2,1)S(1)}) custom-call(bf16[768,2048]{1,0:T(8,128)(2,1)} %gradients.1, bf16[2048,256]{1,0:T(8,128)(2,1)} %projection.1), custom_call_target="tpu_custom_call" | custom-call | flops 805306368 | bytes 4194304 | tf_op jit(solution)/shard_map/sketch/sketch/pallas_call | solution.py:182
  3.8 13.2 %all_to_all.30.parts = f32[4,192,256]{2,1,0:T(8,128)S(1)} all-to-all(f32[4,192,256]{2,1,0:T(8,128)S(1)} %get-tuple-element.6), channel_id=1, replica_groups=mesh['far'=8,'pair'=2,'x'=4,'core'=2,'y'=4] {'y'}, dimensions={0} | all-to-all | bytes 1572864 | tf_op jit(solution)/shard_map/sketch/all_to_all | solution.py:25
  17.0 1.2 gram.1
  18.2 10.0 %all-to-all-start.1 = ((f32[32,4,384]{2,1,0:T(4,128)}), f32[32,4,384]{2,1,0:T(4,128)S(1)}, u32[]{:S(2)}, u32[]{:S(2)}) async-start(f32[32,4,384]{2,1,0:T(4,128)} %get-tuple-element.7), calls=%async_computation.1 | async-start | bytes 393216 | tf_op jit(solution)/shard_map/gram/all_to_all | solution.py:25
  28.2 0.1 pad_add_fusion.1.place
  28.2 3.3 %collective-permute-start = (f32[192,256]{1,0:T(8,128)}, f32[192,256]{1,0:T(8,128)S(1)}, u32[]{:S(2)}, u32[]{:S(2)}) collective-permute-start(f32[192,256]{1,0:T(8,128)} %get-tuple-element.8.refs_0_), channel_id=1, source_target_pairs={{0,1},{1,2},{2,3},{3,0},{4,5},{5,6},{6,7},{7,4},{8,9},{9,10},{10,1... | collective-permute-start | bytes 589832 | tf_op jit(solution)/shard_map/gather/ppermute | solution.py:30
  31.5 4.3 %collective-permute-start.1 = (f32[192,256]{1,0:T(8,128)}, f32[192,256]{1,0:T(8,128)}, u32[]{:S(2)}, u32[]{:S(2)}) collective-permute-start(f32[192,256]{1,0:T(8,128)} %get-tuple-element.8.refs_0_), channel_id=1, source_target_pairs={{0,2},{1,3},{2,0},{3,1},{4,6},{5,7},{6,4},{7,5},{8,10},{9,11},{10,... | collective-permute-start | bytes 589832 | tf_op jit(solution)/shard_map/gather/ppermute | solution.py:30
  35.8 3.1 %collective-permute-start.2 = (f32[192,256]{1,0:T(8,128)}, f32[192,256]{1,0:T(8,128)}, u32[]{:S(2)}, u32[]{:S(2)}) collective-permute-start(f32[192,256]{1,0:T(8,128)} %get-tuple-element.8.refs_0_), channel_id=1, source_target_pairs={{0,3},{1,0},{2,1},{3,2},{4,7},{5,4},{6,5},{7,6},{8,11},{9,8},{10,9... | collective-permute-start | bytes 589832 | tf_op jit(solution)/shard_map/gather/ppermute | solution.py:30
  38.9 0.0 all-to-all-done.1.parts
  38.9 0.7 tile.2
  39.6 14.9 %all-to-all-start.2 = ((f32[16,4,384]{2,1,0:T(4,128)}), f32[16,4,384]{2,1,0:T(4,128)S(1)}, u32[]{:S(2)}, u32[]{:S(2)}) async-start(f32[16,4,384]{2,1,0:T(4,128)} %tile.2), calls=%async_computation.2 | async-start | bytes 196608 | tf_op jit(solution)/shard_map/gram/all_to_all | solution.py:25
  54.6 0.0 collective-permute-done.refs_1_
  54.6 0.0 collective-permute-done.1.refs_2_
  54.6 0.0 collective-permute-done.2.refs_3_
  54.6 0.6 copy-done
  55.2 2.9 %moment.2 = f32[8,256,128]{2,1,0:T(8,128)} custom-call(s32[2]{0:T(128)S(1)} %pad_add_fusion.1.place, bf16[768,2048]{1,0:T(8,128)(2,1)S(1)} %get-tuple-element.9.gradients, f32[192,256]{1,0:T(8,128)} %get-tuple-element.8.refs_0_, f32[192,256]{1,0:T(8,128)} %copy-done, f32[192,256]{1,0:T(8,128)} %collective-permute-done.1.refs_2_, ...), custom_call_target="tpu_custom_call" | custom-call | flops 30000001024 | bytes 2621440 | tf_op jit(solution)/shard_map/moment/moment/pallas_call | solution.py:231
  58.1 3.4 %collective-permute-start.3 = (f32[8,256,128]{2,1,0:T(8,128)}, f32[8,256,128]{2,1,0:T(8,128)}, u32[]{:S(2)}, u32[]{:S(2)}) collective-permute-start(f32[8,256,128]{2,1,0:T(8,128)} %moment.2), channel_id=1, source_target_pairs={{0,4},{4,0},{1,5},{5,1},{2,6},{6,2},{3,7},{7,3},{8,12},{12,8},{9,1... | collective-permute-start | bytes 3145736 | tf_op jit(solution)/shard_map/moment/ppermute | solution.py:297
  61.5 4.9 %all-to-all-done.2.parts = f32[16,4,384]{2,1,0:T(4,128)S(1)} async-done(((f32[16,4,384]{2,1,0:T(4,128)}), f32[16,4,384]{2,1,0:T(4,128)S(1)}, u32[]{:S(2)}, u32[]{:S(2)}) %all-to-all-start.2) | async-done | bytes 98336 | tf_op jit(solution)/shard_map/gram/all_to_all | solution.py:25
  66.4 0.7 tile.3
  67.1 7.2 %all-to-all-start.3 = ((f32[32,4,384]{2,1,0:T(4,128)}), f32[32,4,384]{2,1,0:T(4,128)S(1)}, u32[]{:S(2)}, u32[]{:S(2)}) async-start(f32[32,4,384]{2,1,0:T(4,128)} %tile.3), calls=%async_computation.3 | async-start | bytes 393216 | tf_op jit(solution)/shard_map/gram/all_to_all | solution.py:25
  74.4 0.1 pad_add_fusion.place
  74.4 0.0 collective-permute-done.3.refs_4_
  74.4 3.3 %moment.3 = f32[8,256,128]{2,1,0:T(8,128)} custom-call(s32[2]{0:T(128)S(1)} %pad_add_fusion.place, bf16[768,2048]{1,0:T(8,128)(2,1)S(1)} %get-tuple-element.9.gradients, f32[192,256]{1,0:T(8,128)} %get-tuple-element.8.refs_0_, f32[192,256]{1,0:T(8,128)} %copy-done, f32[192,256]{1,0:T(8,128)} %collective-permute-done.1.refs_2_, ...), custom_call_target="tpu_custom_call" | custom-call | flops 1000000000 | bytes 2621440 | tf_op jit(solution)/shard_map/moment/moment/pallas_call | solution.py:231
  77.7 4.8 %all-to-all-done.3.shares = f32[32,4,384]{2,1,0:T(4,128)S(1)} async-done(((f32[32,4,384]{2,1,0:T(4,128)}), f32[32,4,384]{2,1,0:T(4,128)S(1)}, u32[]{:S(2)}, u32[]{:S(2)}) %all-to-all-start.3) | async-done | bytes 196640 | tf_op jit(solution)/shard_map/gram/all_to_all | solution.py:25
  82.5 3.6 %all-to-all-start.4 = ((f32[8,256,128]{2,1,0:T(8,128)}), f32[8,256,128]{2,1,0:T(8,128)S(1)}, u32[]{:S(2)}, u32[]{:S(2)}) async-start(f32[8,256,128]{2,1,0:T(8,128)} %moment.3), calls=%async_computation.4 | async-start | bytes 2097152 | tf_op jit(solution)/shard_map/moment/all_to_all | solution.py:25
  86.1 9.0 %factor.1.inverse = f32[256,256]{1,0:T(8,128)S(1)} custom-call(f32[32,4,384]{2,1,0:T(4,128)S(1)} %all-to-all-done.3.shares), custom_call_target="tpu_custom_call" | custom-call | flops 10000000000 | bytes 458752 | tf_op jit(solution)/shard_map/factor/factor/pallas_call | solution.py:87
  95.1 5.9 %all-to-all-done.4.parts = f32[8,256,128]{2,1,0:T(8,128)S(1)} async-done(((f32[8,256,128]{2,1,0:T(8,128)}), f32[8,256,128]{2,1,0:T(8,128)S(1)}, u32[]{:S(2)}, u32[]{:S(2)}) %all-to-all-start.4) | async-done | bytes 1048608 | tf_op jit(solution)/shard_map/moment/all_to_all | solution.py:25
  101.0 1.1 solve.1
  102.1 7.7 %all-to-all-start.5 = ((f32[128,2,128]{2,1,0:T(2,128)}), f32[128,2,128]{2,1,0:T(2,128)S(1)}, u32[]{:S(2)}, u32[]{:S(2)}) async-start(f32[128,2,128]{2,1,0:T(2,128)} %solve.1), calls=%async_computation.5 | async-start | bytes 262144 | tf_op jit(solution)/shard_map/reduced/all_to_all | solution.py:25
  109.8 3.3 %basis.1 = f32[768,256]{1,0:T(8,128)} custom-call(s32[1]{0:T(128)} %bitcast.place, f32[256,256]{1,0:T(8,128)S(1)} %factor.1.inverse, f32[192,256]{1,0:T(8,128)} %get-tuple-element.8.refs_0_, f32[192,256]{1,0:T(8,128)} %copy-done, f32[192,256]{1,0:T(8,128)} %collective-permute-done.1.refs_2_, f32[192,256]{1,0:T(8,128)} %collective-permute-done.2.refs_3_), custom_call_target="tpu_custom_call" | custom-call | flops 603979776 | bytes 1835012 | tf_op jit(solution)/shard_map/basis/basis/pallas_call | solution.py:87
  113.1 12.8 %all-to-all-done.5.parts = f32[128,2,128]{2,1,0:T(2,128)S(1)} async-done(((f32[128,2,128]{2,1,0:T(2,128)}), f32[128,2,128]{2,1,0:T(2,128)S(1)}, u32[]{:S(2)}, u32[]{:S(2)}) %all-to-all-start.5) | async-done | bytes 131104 | tf_op jit(solution)/shard_map/reduced/all_to_all | solution.py:25
  125.9 0.6 last.1
  (1 shorter events, 0.0 us)
Async XLA Ops:
  18.2 20.8 %all-to-all-start.1 = ((f32[32,4,384]{2,1,0:T(4,128)}), f32[32,4,384]{2,1,0:T(4,128)S(1)}, u32[]{:S(2)}, u32[]{:S(2)}) async-start(f32[32,4,384]{2,1,0:T(4,128)} %get-tuple-element.7), calls=%async_computation.1 | async-start | bytes 393216 | tf_op jit(solution)/shard_map/gram/all_to_all | solution.py:25
  28.2 26.3 %collective-permute-start = (f32[192,256]{1,0:T(8,128)}, f32[192,256]{1,0:T(8,128)S(1)}, u32[]{:S(2)}, u32[]{:S(2)}) collective-permute-start(f32[192,256]{1,0:T(8,128)} %get-tuple-element.8.refs_0_), channel_id=1, source_target_pairs={{0,1},{1,2},{2,3},{3,0},{4,5},{5,6},{6,7},{7,4},{8,9},{9,10},{10,1... | collective-permute-start | bytes 589832 | tf_op jit(solution)/shard_map/gather/ppermute | solution.py:30
  31.5 23.1 %collective-permute-start.1 = (f32[192,256]{1,0:T(8,128)}, f32[192,256]{1,0:T(8,128)}, u32[]{:S(2)}, u32[]{:S(2)}) collective-permute-start(f32[192,256]{1,0:T(8,128)} %get-tuple-element.8.refs_0_), channel_id=1, source_target_pairs={{0,2},{1,3},{2,0},{3,1},{4,6},{5,7},{6,4},{7,5},{8,10},{9,11},{10,... | collective-permute-start | bytes 589832 | tf_op jit(solution)/shard_map/gather/ppermute | solution.py:30
  35.8 18.8 %collective-permute-start.2 = (f32[192,256]{1,0:T(8,128)}, f32[192,256]{1,0:T(8,128)}, u32[]{:S(2)}, u32[]{:S(2)}) collective-permute-start(f32[192,256]{1,0:T(8,128)} %get-tuple-element.8.refs_0_), channel_id=1, source_target_pairs={{0,3},{1,0},{2,1},{3,2},{4,7},{5,4},{6,5},{7,6},{8,11},{9,8},{10,9... | collective-permute-start | bytes 589832 | tf_op jit(solution)/shard_map/gather/ppermute | solution.py:30
  39.6 26.8 %all-to-all-start.2 = ((f32[16,4,384]{2,1,0:T(4,128)}), f32[16,4,384]{2,1,0:T(4,128)S(1)}, u32[]{:S(2)}, u32[]{:S(2)}) async-start(f32[16,4,384]{2,1,0:T(4,128)} %tile.2), calls=%async_computation.2 | async-start | bytes 196608 | tf_op jit(solution)/shard_map/gram/all_to_all | solution.py:25
  54.6 0.7 copy-start
  58.1 16.3 %collective-permute-start.3 = (f32[8,256,128]{2,1,0:T(8,128)}, f32[8,256,128]{2,1,0:T(8,128)}, u32[]{:S(2)}, u32[]{:S(2)}) collective-permute-start(f32[8,256,128]{2,1,0:T(8,128)} %moment.2), channel_id=1, source_target_pairs={{0,4},{4,0},{1,5},{5,1},{2,6},{6,2},{3,7},{7,3},{8,12},{12,8},{9,1... | collective-permute-start | bytes 3145736 | tf_op jit(solution)/shard_map/moment/ppermute | solution.py:297
  67.1 15.4 %all-to-all-start.3 = ((f32[32,4,384]{2,1,0:T(4,128)}), f32[32,4,384]{2,1,0:T(4,128)S(1)}, u32[]{:S(2)}, u32[]{:S(2)}) async-start(f32[32,4,384]{2,1,0:T(4,128)} %tile.3), calls=%async_computation.3 | async-start | bytes 393216 | tf_op jit(solution)/shard_map/gram/all_to_all | solution.py:25
  82.5 18.5 %all-to-all-start.4 = ((f32[8,256,128]{2,1,0:T(8,128)}), f32[8,256,128]{2,1,0:T(8,128)S(1)}, u32[]{:S(2)}, u32[]{:S(2)}) async-start(f32[8,256,128]{2,1,0:T(8,128)} %moment.3), calls=%async_computation.4 | async-start | bytes 2097152 | tf_op jit(solution)/shard_map/moment/all_to_all | solution.py:25
  102.1 23.8 %all-to-all-start.5 = ((f32[128,2,128]{2,1,0:T(2,128)}), f32[128,2,128]{2,1,0:T(2,128)S(1)}, u32[]{:S(2)}, u32[]{:S(2)}) async-start(f32[128,2,128]{2,1,0:T(2,128)} %solve.1), calls=%async_computation.5 | async-start | bytes 262144 | tf_op jit(solution)/shard_map/reduced/all_to_all | solution.py:25

commit v10 on v9

--- a/solution.py
+++ b/solution.py
@@ -14,10 +14,11 @@
 DEEP = ("far", "pair")
 CROSS = ("pair", "x")
 NEAR = ("x", "core", "y")
+FIRST = ("pair", *NEAR)
 GROUPS = 4
 PIECES = 4
 PANEL = 8
-SHORT = 3 * 10**10
+LONG = 3 * 10**10
 VMEM_LIMIT = 8 * 1024 * 1024
 
 
@@ -111,13 +112,24 @@
     left = dot(total, total[:, :n], ((0,), (0,)))
     right = dot(total[:, n:], total[:, n:], ((0,), (0,)))
     packed = jnp.concatenate([left[:n], left[n:], right], 1)
-    gram[...] = packed.reshape(gram.shape)
+    pairs, near, size, wide = gram.shape
+    packed = packed.reshape(near, pairs * size, wide)
+    for i in range(pairs):
+        gram[i] = packed[:, i * size : (i + 1) * size]
 
 
 def tile_kernel(parts, tiles):
     total = jnp.sum(parts[...], 0)
     for i in range(tiles.shape[0]):
         tiles[i] = total
+
+
+def join_kernel(parts, tiles):
+    total = jnp.sum(parts[...], 0)
+    pairs, size, _ = total.shape
+    for i in range(tiles.shape[0]):
+        for j in range(pairs):
+            tiles[i, j * size : (j + 1) * size] = total[j]
 
 
 def factor_kernel(shares, out, packed):
@@ -256,7 +268,7 @@
     scale = float(rows * members_of_rows) ** 0.5
     core = lax.axis_index("core").astype(jnp.int32)
     mine = lax.axis_index("y").astype(jnp.int32)
-    share = (rank // 2 // near, 3 * rank // 2)
+    size, wide = rank // 2 // (pairs * near), 3 * rank // 2
     width = feats // (cores * pairs * xs)
 
     with jax.named_scope("sketch"):
@@ -268,13 +280,16 @@
             gram_kernel,
             "gram",
             12 * rows // GROUPS * rank**2,
-            [far(rows // GROUPS, rank), far(near, *share)],
+            [far(rows // GROUPS, rank), far(pairs, near, size, wide)],
             parts,
         )
-        shares = exchange(shares, NEAR)
-        (shares,) = call(tile_kernel, "tile", SHORT, [far(deep, *share)], shares)
-        shares = exchange(shares, DEEP)
-        (shares,) = call(tile_kernel, "tile", SHORT, [far(near, *share)], shares)
+        shares = shares.reshape(pairs * near, size, wide)
+        shares = exchange(shares, FIRST)
+        (shares,) = call(tile_kernel, "tile", LONG, [far(deep, size, wide)], shares)
+        shares = exchange(shares, DEEP).reshape(-1, pairs, size, wide)
+        (shares,) = call(
+            join_kernel, "join", LONG, [far(near, pairs * size, wide)], shares
+        )
         shares = exchange(shares, NEAR)
 
     with jax.named_scope("factor"):
@@ -293,7 +308,7 @@
 
     with jax.named_scope("moment"):
         count = pairs * xs
-        away = moment_blocks(jnp.stack([1 - core, mine]), held, blocks, count, SHORT)
+        away = moment_blocks(jnp.stack([1 - core, mine]), held, blocks, count, LONG)
         away = lax.ppermute(away, "core", [(0, 1), (1, 0)])
         moment = moment_blocks(
             jnp.stack([core, mine]), held, blocks, count, 10**9, away

time: 127 us -> 128 us (level)
  starting transfers between devices: 57.4 us -> 59 us
    all_to_all x5, starting transfers between devices: 43.4 us -> 44.9 us  [exchange(): return lax.all_to_all(blocks, axes, 0, 0)]
where the time goes in v10:
time: 128 us
  starting transfers between devices  59 us (46%)
  waiting for transfers between devices  28.2 us (22%)
  Pallas kernels  25.9 us (20%)
  blocking collectives  13.2 us (10%)
    all_to_all x5, starting transfers between devices, exchange(): return lax.all_to_all(blocks, axes, 0, 0)  44.9 us
    all_to_all x5, waiting for transfers between devices, exchange(): return lax.all_to_all(blocks, axes, 0, 0)  28.2 us
    pallas_call x7, Pallas kernels, call(): pl.pallas_call(kernel, out_shape=outs, in_specs=[smem if a.ndim == 1 else...  16.6 us
    all_to_all x1, blocking collectives, exchange(): return lax.all_to_all(blocks, axes, 0, 0)  13.2 us
    ppermute x3, starting transfers between devices, shifted(): lax.ppermute(value, axis, [(i, (i + by) % count) for i in range(count)])  10.7 us
    pallas_call x2, Pallas kernels, moment_blocks(): pl.pallas_call(moment_kernel, out_shape=far(count, rank, width), in_specs...  6.14 us
    ppermute x1, starting transfers between devices, on_device(): away = lax.ppermute(away, 'core', [(0, 1), (1, 0)])  3.37 us
    pallas_call x1, Pallas kernels, sketch_blocks(): pl.pallas_call(sketch_kernel, out_shape=[f32(blocks, rows // blocks, rank...  3.18 us
  transfers between devices with their start and end apart: 9, of which 4 were waited for; matrix products, arithmetic and copies ran while one was open for 0% of the time, Pallas kernels for 16%

profile of v10, /device:TPU:1, one launch (start us, length us, event | category | flops | bytes accessed | tf_op | source)
XLA Modules:
  0.0 127.8 jit_solution(6677278445528519580)
XLA Ops:
  0.6 3.2 %sketch.1 = (f32[4,192,256]{2,1,0:T(8,128)S(1)}, bf16[768,2048]{1,0:T(8,128)(2,1)S(1)}) custom-call(bf16[768,2048]{1,0:T(8,128)(2,1)} %gradients.1, bf16[2048,256]{1,0:T(8,128)(2,1)} %projection.1), custom_call_target="tpu_custom_call" | custom-call | flops 805306368 | bytes 4194304 | tf_op jit(solution)/shard_map/sketch/sketch/pallas_call | solution.py:194
  3.8 13.2 %all_to_all.30.parts = f32[4,192,256]{2,1,0:T(8,128)S(1)} all-to-all(f32[4,192,256]{2,1,0:T(8,128)S(1)} %get-tuple-element.6), channel_id=1, replica_groups=mesh['far'=8,'pair'=2,'x'=4,'core'=2,'y'=4] {'y'}, dimensions={0} | all-to-all | bytes 1572864 | tf_op jit(solution)/shard_map/sketch/all_to_all | solution.py:26
  17.0 1.2 gram.1
  18.2 11.7 %all-to-all-start.1 = ((f32[64,2,384]{2,1,0:T(2,128)}), f32[64,2,384]{2,1,0:T(2,128)S(1)}, u32[]{:S(2)}, u32[]{:S(2)}) async-start(f32[64,2,384]{2,1,0:T(2,128)} %bitcast.6), calls=%async_computation.1 | async-start | bytes 393216 | tf_op jit(solution)/shard_map/gram/all_to_all | solution.py:26
  29.9 0.1 pad_add_fusion.1.place
  30.0 3.3 %collective-permute-start = (f32[192,256]{1,0:T(8,128)}, f32[192,256]{1,0:T(8,128)S(1)}, u32[]{:S(2)}, u32[]{:S(2)}) collective-permute-start(f32[192,256]{1,0:T(8,128)} %get-tuple-element.8.refs_0_), channel_id=1, source_target_pairs={{0,1},{1,2},{2,3},{3,0},{4,5},{5,6},{6,7},{7,4},{8,9},{9,10},{10,1... | collective-permute-start | bytes 589832 | tf_op jit(solution)/shard_map/gather/ppermute | solution.py:31
  33.3 4.3 %collective-permute-start.1 = (f32[192,256]{1,0:T(8,128)}, f32[192,256]{1,0:T(8,128)}, u32[]{:S(2)}, u32[]{:S(2)}) collective-permute-start(f32[192,256]{1,0:T(8,128)} %get-tuple-element.8.refs_0_), channel_id=1, source_target_pairs={{0,2},{1,3},{2,0},{3,1},{4,6},{5,7},{6,4},{7,5},{8,10},{9,11},{10,... | collective-permute-start | bytes 589832 | tf_op jit(solution)/shard_map/gather/ppermute | solution.py:31
  37.6 3.1 %collective-permute-start.2 = (f32[192,256]{1,0:T(8,128)}, f32[192,256]{1,0:T(8,128)}, u32[]{:S(2)}, u32[]{:S(2)}) collective-permute-start(f32[192,256]{1,0:T(8,128)} %get-tuple-element.8.refs_0_), channel_id=1, source_target_pairs={{0,3},{1,0},{2,1},{3,2},{4,7},{5,4},{6,5},{7,6},{8,11},{9,8},{10,9... | collective-permute-start | bytes 589832 | tf_op jit(solution)/shard_map/gather/ppermute | solution.py:31
  40.7 0.0 all-to-all-done.1.parts
  40.7 0.7 tile.1
  41.4 14.1 %all-to-all-start.2 = ((f32[16,2,384]{2,1,0:T(2,128)}), f32[16,2,384]{2,1,0:T(2,128)S(1)}, u32[]{:S(2)}, u32[]{:S(2)}) async-start(f32[16,2,384]{2,1,0:T(2,128)} %tile.1), calls=%async_computation.2 | async-start | bytes 98304 | tf_op jit(solution)/shard_map/gram/all_to_all | solution.py:26
  55.6 0.0 collective-permute-done.refs_1_
  55.6 0.0 collective-permute-done.1.refs_2_
  55.6 0.0 collective-permute-done.2.refs_3_
  55.6 0.6 copy-done
  56.2 2.9 %moment.2 = f32[8,256,128]{2,1,0:T(8,128)} custom-call(s32[2]{0:T(128)S(1)} %pad_add_fusion.1.place, bf16[768,2048]{1,0:T(8,128)(2,1)S(1)} %get-tuple-element.9.gradients, f32[192,256]{1,0:T(8,128)} %get-tuple-element.8.refs_0_, f32[192,256]{1,0:T(8,128)} %copy-done, f32[192,256]{1,0:T(8,128)} %collective-permute-done.1.refs_2_, ...), custom_call_target="tpu_custom_call" | custom-call | flops 30000001024 | bytes 2621440 | tf_op jit(solution)/shard_map/moment/moment/pallas_call | solution.py:243
  59.1 3.4 %collective-permute-start.3 = (f32[8,256,128]{2,1,0:T(8,128)}, f32[8,256,128]{2,1,0:T(8,128)}, u32[]{:S(2)}, u32[]{:S(2)}) collective-permute-start(f32[8,256,128]{2,1,0:T(8,128)} %moment.2), channel_id=1, source_target_pairs={{0,4},{4,0},{1,5},{5,1},{2,6},{6,2},{3,7},{7,3},{8,12},{12,8},{9,1... | collective-permute-start | bytes 3145736 | tf_op jit(solution)/shard_map/moment/ppermute | solution.py:312
  62.5 4.6 %all-to-all-done.2 = f32[16,2,384]{2,1,0:T(2,128)S(1)} async-done(((f32[16,2,384]{2,1,0:T(2,128)}), f32[16,2,384]{2,1,0:T(2,128)S(1)}, u32[]{:S(2)}, u32[]{:S(2)}) %all-to-all-start.2) | async-done | bytes 49184 | tf_op jit(solution)/shard_map/gram/all_to_all | solution.py:26
  67.1 0.7 join.1
  67.9 7.1 %all-to-all-start.3 = ((f32[32,4,384]{2,1,0:T(4,128)}), f32[32,4,384]{2,1,0:T(4,128)S(1)}, u32[]{:S(2)}, u32[]{:S(2)}) async-start(f32[32,4,384]{2,1,0:T(4,128)} %join.1), calls=%async_computation.3 | async-start | bytes 393216 | tf_op jit(solution)/shard_map/gram/all_to_all | solution.py:26
  75.0 0.1 pad_add_fusion.place
  75.1 0.0 collective-permute-done.3.refs_4_
  75.1 3.3 %moment.3 = f32[8,256,128]{2,1,0:T(8,128)} custom-call(s32[2]{0:T(128)S(1)} %pad_add_fusion.place, bf16[768,2048]{1,0:T(8,128)(2,1)S(1)} %get-tuple-element.9.gradients, f32[192,256]{1,0:T(8,128)} %get-tuple-element.8.refs_0_, f32[192,256]{1,0:T(8,128)} %copy-done, f32[192,256]{1,0:T(8,128)} %collective-permute-done.1.refs_2_, ...), custom_call_target="tpu_custom_call" | custom-call | flops 1000000000 | bytes 2621440 | tf_op jit(solution)/shard_map/moment/moment/pallas_call | solution.py:243
  78.3 4.9 %all-to-all-done.3.shares = f32[32,4,384]{2,1,0:T(4,128)S(1)} async-done(((f32[32,4,384]{2,1,0:T(4,128)}), f32[32,4,384]{2,1,0:T(4,128)S(1)}, u32[]{:S(2)}, u32[]{:S(2)}) %all-to-all-start.3) | async-done | bytes 196640 | tf_op jit(solution)/shard_map/gram/all_to_all | solution.py:26
  83.2 3.6 %all-to-all-start.4 = ((f32[8,256,128]{2,1,0:T(8,128)}), f32[8,256,128]{2,1,0:T(8,128)S(1)}, u32[]{:S(2)}, u32[]{:S(2)}) async-start(f32[8,256,128]{2,1,0:T(8,128)} %moment.3), calls=%async_computation.4 | async-start | bytes 2097152 | tf_op jit(solution)/shard_map/moment/all_to_all | solution.py:26
  86.7 9.0 %factor.1.inverse = f32[256,256]{1,0:T(8,128)S(1)} custom-call(f32[32,4,384]{2,1,0:T(4,128)S(1)} %all-to-all-done.3.shares), custom_call_target="tpu_custom_call" | custom-call | flops 10000000000 | bytes 458752 | tf_op jit(solution)/shard_map/factor/factor/pallas_call | solution.py:88
  95.7 5.9 %all-to-all-done.4.parts = f32[8,256,128]{2,1,0:T(8,128)S(1)} async-done(((f32[8,256,128]{2,1,0:T(8,128)}), f32[8,256,128]{2,1,0:T(8,128)S(1)}, u32[]{:S(2)}, u32[]{:S(2)}) %all-to-all-start.4) | async-done | bytes 1048608 | tf_op jit(solution)/shard_map/moment/all_to_all | solution.py:26
  101.6 1.1 solve.1
  102.7 8.4 %all-to-all-start.5 = ((f32[128,2,128]{2,1,0:T(2,128)}), f32[128,2,128]{2,1,0:T(2,128)S(1)}, u32[]{:S(2)}, u32[]{:S(2)}) async-start(f32[128,2,128]{2,1,0:T(2,128)} %solve.1), calls=%async_computation.5 | async-start | bytes 262144 | tf_op jit(solution)/shard_map/reduced/all_to_all | solution.py:26
  111.1 3.3 %basis.1 = f32[768,256]{1,0:T(8,128)} custom-call(s32[1]{0:T(128)} %bitcast.place, f32[256,256]{1,0:T(8,128)S(1)} %factor.1.inverse, f32[192,256]{1,0:T(8,128)} %get-tuple-element.8.refs_0_, f32[192,256]{1,0:T(8,128)} %copy-done, f32[192,256]{1,0:T(8,128)} %collective-permute-done.1.refs_2_, f32[192,256]{1,0:T(8,128)} %collective-permute-done.2.refs_3_), custom_call_target="tpu_custom_call" | custom-call | flops 603979776 | bytes 1835012 | tf_op jit(solution)/shard_map/basis/basis/pallas_call | solution.py:88
  114.4 12.8 %all-to-all-done.5.parts = f32[128,2,128]{2,1,0:T(2,128)S(1)} async-done(((f32[128,2,128]{2,1,0:T(2,128)}), f32[128,2,128]{2,1,0:T(2,128)S(1)}, u32[]{:S(2)}, u32[]{:S(2)}) %all-to-all-start.5) | async-done | bytes 131104 | tf_op jit(solution)/shard_map/reduced/all_to_all | solution.py:26
  127.2 0.6 last.1
  (1 shorter events, 0.0 us)
Async XLA Ops:
  18.2 22.5 %all-to-all-start.1 = ((f32[64,2,384]{2,1,0:T(2,128)}), f32[64,2,384]{2,1,0:T(2,128)S(1)}, u32[]{:S(2)}, u32[]{:S(2)}) async-start(f32[64,2,384]{2,1,0:T(2,128)} %bitcast.6), calls=%async_computation.1 | async-start | bytes 393216 | tf_op jit(solution)/shard_map/gram/all_to_all | solution.py:26
  30.0 25.6 %collective-permute-start = (f32[192,256]{1,0:T(8,128)}, f32[192,256]{1,0:T(8,128)S(1)}, u32[]{:S(2)}, u32[]{:S(2)}) collective-permute-start(f32[192,256]{1,0:T(8,128)} %get-tuple-element.8.refs_0_), channel_id=1, source_target_pairs={{0,1},{1,2},{2,3},{3,0},{4,5},{5,6},{6,7},{7,4},{8,9},{9,10},{10,1... | collective-permute-start | bytes 589832 | tf_op jit(solution)/shard_map/gather/ppermute | solution.py:31
  33.3 22.3 %collective-permute-start.1 = (f32[192,256]{1,0:T(8,128)}, f32[192,256]{1,0:T(8,128)}, u32[]{:S(2)}, u32[]{:S(2)}) collective-permute-start(f32[192,256]{1,0:T(8,128)} %get-tuple-element.8.refs_0_), channel_id=1, source_target_pairs={{0,2},{1,3},{2,0},{3,1},{4,6},{5,7},{6,4},{7,5},{8,10},{9,11},{10,... | collective-permute-start | bytes 589832 | tf_op jit(solution)/shard_map/gather/ppermute | solution.py:31
  37.6 18.0 %collective-permute-start.2 = (f32[192,256]{1,0:T(8,128)}, f32[192,256]{1,0:T(8,128)}, u32[]{:S(2)}, u32[]{:S(2)}) collective-permute-start(f32[192,256]{1,0:T(8,128)} %get-tuple-element.8.refs_0_), channel_id=1, source_target_pairs={{0,3},{1,0},{2,1},{3,2},{4,7},{5,4},{6,5},{7,6},{8,11},{9,8},{10,9... | collective-permute-start | bytes 589832 | tf_op jit(solution)/shard_map/gather/ppermute | solution.py:31
  41.4 25.7 %all-to-all-start.2 = ((f32[16,2,384]{2,1,0:T(2,128)}), f32[16,2,384]{2,1,0:T(2,128)S(1)}, u32[]{:S(2)}, u32[]{:S(2)}) async-start(f32[16,2,384]{2,1,0:T(2,128)} %tile.1), calls=%async_computation.2 | async-start | bytes 98304 | tf_op jit(solution)/shard_map/gram/all_to_all | solution.py:26
  55.6 0.7 copy-start
  59.1 15.9 %collective-permute-start.3 = (f32[8,256,128]{2,1,0:T(8,128)}, f32[8,256,128]{2,1,0:T(8,128)}, u32[]{:S(2)}, u32[]{:S(2)}) collective-permute-start(f32[8,256,128]{2,1,0:T(8,128)} %moment.2), channel_id=1, source_target_pairs={{0,4},{4,0},{1,5},{5,1},{2,6},{6,2},{3,7},{7,3},{8,12},{12,8},{9,1... | collective-permute-start | bytes 3145736 | tf_op jit(solution)/shard_map/moment/ppermute | solution.py:312
  67.9 15.3 %all-to-all-start.3 = ((f32[32,4,384]{2,1,0:T(4,128)}), f32[32,4,384]{2,1,0:T(4,128)S(1)}, u32[]{:S(2)}, u32[]{:S(2)}) async-start(f32[32,4,384]{2,1,0:T(4,128)} %join.1), calls=%async_computation.3 | async-start | bytes 393216 | tf_op jit(solution)/shard_map/gram/all_to_all | solution.py:26
  83.2 18.5 %all-to-all-start.4 = ((f32[8,256,128]{2,1,0:T(8,128)}), f32[8,256,128]{2,1,0:T(8,128)S(1)}, u32[]{:S(2)}, u32[]{:S(2)}) async-start(f32[8,256,128]{2,1,0:T(8,128)} %moment.3), calls=%async_computation.4 | async-start | bytes 2097152 | tf_op jit(solution)/shard_map/moment/all_to_all | solution.py:26
  102.7 24.5 %all-to-all-start.5 = ((f32[128,2,128]{2,1,0:T(2,128)}), f32[128,2,128]{2,1,0:T(2,128)S(1)}, u32[]{:S(2)}, u32[]{:S(2)}) async-start(f32[128,2,128]{2,1,0:T(2,128)} %solve.1), calls=%async_computation.5 | async-start | bytes 262144 | tf_op jit(solution)/shard_map/reduced/all_to_all | solution.py:26

commit v11 on v9

--- a/solution.py
+++ b/solution.py
@@ -17,7 +17,7 @@
 GROUPS = 4
 PIECES = 4
 PANEL = 8
-SHORT = 3 * 10**10
+LONG = 3 * 10**10
 VMEM_LIMIT = 8 * 1024 * 1024
 
 
@@ -186,7 +186,7 @@
             jax.ShapeDtypeStruct(gradients.shape, gradients.dtype),
         ],
         in_specs=[pl.BlockSpec(memory_space=pltpu.HBM)] * 2,
-        out_specs=[pl.BlockSpec(), pl.BlockSpec(memory_space=pltpu.VMEM)],
+        out_specs=[pl.BlockSpec(memory_space=pltpu.VMEM)] * 2,
         scratch_shapes=[
             pltpu.VMEM(projection.shape, projection.dtype),
             pltpu.SemaphoreType.DMA((PIECES + 1,)),
@@ -272,9 +272,9 @@
             parts,
         )
         shares = exchange(shares, NEAR)
-        (shares,) = call(tile_kernel, "tile", SHORT, [far(deep, *share)], shares)
+        (shares,) = call(tile_kernel, "tile", LONG, [far(deep, *share)], shares)
         shares = exchange(shares, DEEP)
-        (shares,) = call(tile_kernel, "tile", SHORT, [far(near, *share)], shares)
+        (shares,) = call(tile_kernel, "tile", LONG, [far(near, *share)], shares)
         shares = exchange(shares, NEAR)
 
     with jax.named_scope("factor"):
@@ -289,11 +289,10 @@
 
     with jax.named_scope("gather"):
         blocks = [own] + [shifted(own, "y", k) for k in range(1, GROUPS)]
-        blocks = [pltpu.with_memory_space_constraint(b, pltpu.HBM) for b in blocks]
 
     with jax.named_scope("moment"):
         count = pairs * xs
-        away = moment_blocks(jnp.stack([1 - core, mine]), held, blocks, count, SHORT)
+        away = moment_blocks(jnp.stack([1 - core, mine]), held, blocks, count, LONG)
         away = lax.ppermute(away, "core", [(0, 1), (1, 0)])
         moment = moment_blocks(
             jnp.stack([core, mine]), held, blocks, count, 10**9, away

time: 127 us -> 129 us (1.016)
  Pallas kernels: 25.9 us -> 28.1 us
    pallas_call x7, Pallas kernels: 16.6 us -> 19.2 us  [call(): pl.pallas_call(kernel, out_shape=outs, in_specs=[smem if a.ndim == 1 else...]
  transfers between devices with their start and end apart: 9 -> 9, of which waited for: 4 -> 4; matrix products, arithmetic and copies ran while one was open for 0% -> 0% of each run, Pallas kernels for 16% -> 17%
where the time goes in v11:
time: 129 us; the launch traced here: 128 us
  starting transfers between devices  57.1 us (44%)
  waiting for transfers between devices  28.8 us (22%)
  Pallas kernels  28.1 us (22%)
  blocking collectives  13.2 us (10%)
    all_to_all x5, starting transfers between devices, exchange(): return lax.all_to_all(blocks, axes, 0, 0)  43 us
    all_to_all x5, waiting for transfers between devices, exchange(): return lax.all_to_all(blocks, axes, 0, 0)  28.8 us
    pallas_call x7, Pallas kernels, call(): pl.pallas_call(kernel, out_shape=outs, in_specs=[smem if a.ndim == 1 else...  19.2 us
    all_to_all x1, blocking collectives, exchange(): return lax.all_to_all(blocks, axes, 0, 0)  13.2 us
    ppermute x3, starting transfers between devices, shifted(): lax.ppermute(value, axis, [(i, (i + by) % count) for i in range(count)])  10.8 us
    pallas_call x2, Pallas kernels, moment_blocks(): pl.pallas_call(moment_kernel, out_shape=far(count, rank, width), in_specs...  5.79 us
    ppermute x1, starting transfers between devices, on_device(): away = lax.ppermute(away, 'core', [(0, 1), (1, 0)])  3.37 us
    pallas_call x1, Pallas kernels, sketch_blocks(): pl.pallas_call(sketch_kernel, out_shape=[f32(blocks, rows // blocks, rank...  3.18 us
  transfers between devices with their start and end apart: 9, of which 4 were waited for; matrix products, arithmetic and copies ran while one was open for 0% of the time, Pallas kernels for 17%

profile of v11, /device:TPU:1, one launch (start us, length us, event | category | flops | bytes accessed | tf_op | source)
XLA Modules:
  0.0 128.2 jit_solution(5717113003461057121)
XLA Ops:
  0.6 3.2 %sketch.1 = (f32[4,192,256]{2,1,0:T(8,128)S(1)}, bf16[768,2048]{1,0:T(8,128)(2,1)S(1)}) custom-call(bf16[768,2048]{1,0:T(8,128)(2,1)} %gradients.1, bf16[2048,256]{1,0:T(8,128)(2,1)} %projection.1), custom_call_target="tpu_custom_call" | custom-call | flops 805306368 | bytes 4194304 | tf_op jit(solution)/shard_map/sketch/sketch/pallas_call | solution.py:182
  3.8 13.2 %all_to_all.30.parts = f32[4,192,256]{2,1,0:T(8,128)S(1)} all-to-all(f32[4,192,256]{2,1,0:T(8,128)S(1)} %get-tuple-element.6), channel_id=1, replica_groups=mesh['far'=8,'pair'=2,'x'=4,'core'=2,'y'=4] {'y'}, dimensions={0} | all-to-all | bytes 1572864 | tf_op jit(solution)/shard_map/sketch/all_to_all | solution.py:25
  17.0 1.2 gram.1
  18.2 10.0 %all-to-all-start.1 = ((f32[32,4,384]{2,1,0:T(4,128)}), f32[32,4,384]{2,1,0:T(4,128)}, u32[]{:S(2)}, u32[]{:S(2)}) async-start(f32[32,4,384]{2,1,0:T(4,128)} %get-tuple-element.7), calls=%async_computation.1 | async-start | bytes 393216 | tf_op jit(solution)/shard_map/gram/all_to_all | solution.py:25
  28.2 0.1 pad_add_fusion.1.place
  28.3 3.4 %collective-permute-start = (f32[192,256]{1,0:T(8,128)}, f32[192,256]{1,0:T(8,128)S(1)}, u32[]{:S(2)}, u32[]{:S(2)}) collective-permute-start(f32[192,256]{1,0:T(8,128)} %get-tuple-element.8.refs_0_), channel_id=1, source_target_pairs={{0,1},{1,2},{2,3},{3,0},{4,5},{5,6},{6,7},{7,4},{8,9},{9,10},{10,1... | collective-permute-start | bytes 589832 | tf_op jit(solution)/shard_map/gather/ppermute | solution.py:30
  31.7 4.3 %collective-permute-start.1 = (f32[192,256]{1,0:T(8,128)}, f32[192,256]{1,0:T(8,128)}, u32[]{:S(2)}, u32[]{:S(2)}) collective-permute-start(f32[192,256]{1,0:T(8,128)} %get-tuple-element.8.refs_0_), channel_id=1, source_target_pairs={{0,2},{1,3},{2,0},{3,1},{4,6},{5,7},{6,4},{7,5},{8,10},{9,11},{10,... | collective-permute-start | bytes 589832 | tf_op jit(solution)/shard_map/gather/ppermute | solution.py:30
  36.0 3.1 %collective-permute-start.2 = (f32[192,256]{1,0:T(8,128)}, f32[192,256]{1,0:T(8,128)}, u32[]{:S(2)}, u32[]{:S(2)}) collective-permute-start(f32[192,256]{1,0:T(8,128)} %get-tuple-element.8.refs_0_), channel_id=1, source_target_pairs={{0,3},{1,0},{2,1},{3,2},{4,7},{5,4},{6,5},{7,6},{8,11},{9,8},{10,9... | collective-permute-start | bytes 589832 | tf_op jit(solution)/shard_map/gather/ppermute | solution.py:30
  39.1 0.0 all-to-all-done.1.parts
  39.2 1.6 %tile.2 = f32[16,4,384]{2,1,0:T(4,128)} custom-call(f32[32,4,384]{2,1,0:T(4,128)} %all-to-all-done.1.parts), custom_call_target="tpu_custom_call" | custom-call | flops 30000001024 | bytes 294912 | tf_op jit(solution)/shard_map/gram/tile/pallas_call | solution.py:87
  40.8 15.0 %all-to-all-start.2 = ((f32[16,4,384]{2,1,0:T(4,128)}), f32[16,4,384]{2,1,0:T(4,128)}, u32[]{:S(2)}, u32[]{:S(2)}) async-start(f32[16,4,384]{2,1,0:T(4,128)} %tile.2), calls=%async_computation.2 | async-start | bytes 196608 | tf_op jit(solution)/shard_map/gram/all_to_all | solution.py:25
  55.7 0.0 collective-permute-done.refs_1_
  55.8 0.0 collective-permute-done.1.refs_2_
  55.8 0.0 collective-permute-done.2.refs_3_
  55.8 0.0 copy-done
  55.8 2.7 %moment.2 = f32[8,256,128]{2,1,0:T(8,128)} custom-call(s32[2]{0:T(128)S(1)} %pad_add_fusion.1.place, bf16[768,2048]{1,0:T(8,128)(2,1)S(1)} %get-tuple-element.9.gradients, f32[192,256]{1,0:T(8,128)S(1)} %copy-done, f32[192,256]{1,0:T(8,128)S(1)} %collective-permute-done.refs_1_, f32[192,256]{1,0:T(8,128)} %collective-permute-done.1.refs_2_, ...), custom_call_target="tpu_custom_call" | custom-call | flops 30000001024 | bytes 2621440 | tf_op jit(solution)/shard_map/moment/moment/pallas_call | solution.py:231
  58.5 3.4 %collective-permute-start.3 = (f32[8,256,128]{2,1,0:T(8,128)}, f32[8,256,128]{2,1,0:T(8,128)}, u32[]{:S(2)}, u32[]{:S(2)}) collective-permute-start(f32[8,256,128]{2,1,0:T(8,128)} %moment.2), channel_id=1, source_target_pairs={{0,4},{4,0},{1,5},{5,1},{2,6},{6,2},{3,7},{7,3},{8,12},{12,8},{9,1... | collective-permute-start | bytes 3145736 | tf_op jit(solution)/shard_map/moment/ppermute | solution.py:296
  61.9 5.8 %all-to-all-done.2.parts = f32[16,4,384]{2,1,0:T(4,128)} async-done(((f32[16,4,384]{2,1,0:T(4,128)}), f32[16,4,384]{2,1,0:T(4,128)}, u32[]{:S(2)}, u32[]{:S(2)}) %all-to-all-start.2) | async-done | bytes 98336 | tf_op jit(solution)/shard_map/gram/all_to_all | solution.py:25
  67.6 1.6 %tile.3 = f32[32,4,384]{2,1,0:T(4,128)} custom-call(f32[16,4,384]{2,1,0:T(4,128)} %all-to-all-done.2.parts), custom_call_target="tpu_custom_call" | custom-call | flops 30000001024 | bytes 294912 | tf_op jit(solution)/shard_map/gram/tile/pallas_call | solution.py:87
  69.2 7.3 %all-to-all-start.3 = ((f32[32,4,384]{2,1,0:T(4,128)}), f32[32,4,384]{2,1,0:T(4,128)}, u32[]{:S(2)}, u32[]{:S(2)}) async-start(f32[32,4,384]{2,1,0:T(4,128)} %tile.3), calls=%async_computation.3 | async-start | bytes 393216 | tf_op jit(solution)/shard_map/gram/all_to_all | solution.py:25
  76.5 0.1 pad_add_fusion.place
  76.6 0.0 collective-permute-done.3.refs_4_
  76.6 3.1 %moment.3 = f32[8,256,128]{2,1,0:T(8,128)} custom-call(s32[2]{0:T(128)S(1)} %pad_add_fusion.place, bf16[768,2048]{1,0:T(8,128)(2,1)S(1)} %get-tuple-element.9.gradients, f32[192,256]{1,0:T(8,128)S(1)} %copy-done, f32[192,256]{1,0:T(8,128)S(1)} %collective-permute-done.refs_1_, f32[192,256]{1,0:T(8,128)} %collective-permute-done.1.refs_2_, ...), custom_call_target="tpu_custom_call" | custom-call | flops 1000000000 | bytes 2621440 | tf_op jit(solution)/shard_map/moment/moment/pallas_call | solution.py:231
  79.7 5.1 %all-to-all-done.3.shares = f32[32,4,384]{2,1,0:T(4,128)} async-done(((f32[32,4,384]{2,1,0:T(4,128)}), f32[32,4,384]{2,1,0:T(4,128)}, u32[]{:S(2)}, u32[]{:S(2)}) %all-to-all-start.3) | async-done | bytes 196640 | tf_op jit(solution)/shard_map/gram/all_to_all | solution.py:25
  84.8 3.6 %all-to-all-start.4 = ((f32[8,256,128]{2,1,0:T(8,128)}), f32[8,256,128]{2,1,0:T(8,128)S(1)}, u32[]{:S(2)}, u32[]{:S(2)}) async-start(f32[8,256,128]{2,1,0:T(8,128)} %moment.3), calls=%async_computation.4 | async-start | bytes 2097152 | tf_op jit(solution)/shard_map/moment/all_to_all | solution.py:25
  88.3 9.9 %factor.1.inverse = f32[256,256]{1,0:T(8,128)S(1)} custom-call(f32[32,4,384]{2,1,0:T(4,128)} %all-to-all-done.3.shares), custom_call_target="tpu_custom_call" | custom-call | flops 10000000000 | bytes 458752 | tf_op jit(solution)/shard_map/factor/factor/pallas_call | solution.py:87
  98.2 5.0 %all-to-all-done.4.parts = f32[8,256,128]{2,1,0:T(8,128)S(1)} async-done(((f32[8,256,128]{2,1,0:T(8,128)}), f32[8,256,128]{2,1,0:T(8,128)S(1)}, u32[]{:S(2)}, u32[]{:S(2)}) %all-to-all-start.4) | async-done | bytes 1048608 | tf_op jit(solution)/shard_map/moment/all_to_all | solution.py:25
  103.2 1.1 solve.1
  104.3 7.2 %all-to-all-start.5 = ((f32[128,2,128]{2,1,0:T(2,128)}), f32[128,2,128]{2,1,0:T(2,128)S(1)}, u32[]{:S(2)}, u32[]{:S(2)}) async-start(f32[128,2,128]{2,1,0:T(2,128)} %solve.1), calls=%async_computation.5 | async-start | bytes 262144 | tf_op jit(solution)/shard_map/reduced/all_to_all | solution.py:25
  111.5 3.1 %basis.1 = f32[768,256]{1,0:T(8,128)} custom-call(s32[1]{0:T(128)} %bitcast.place, f32[256,256]{1,0:T(8,128)S(1)} %factor.1.inverse, f32[192,256]{1,0:T(8,128)S(1)} %copy-done, f32[192,256]{1,0:T(8,128)S(1)} %collective-permute-done.refs_1_, f32[192,256]{1,0:T(8,128)} %collective-permute-done.1.refs_2_, f32[192,256]{1,0:T(8,128)} %collective-permute-done.2.refs_3_), custom_call_target="tpu_custom_call" | custom-call | flops 603979776 | bytes 1835012 | tf_op jit(solution)/shard_map/basis/basis/pallas_call | solution.py:87
  114.6 13.0 %all-to-all-done.5.parts = f32[128,2,128]{2,1,0:T(2,128)S(1)} async-done(((f32[128,2,128]{2,1,0:T(2,128)}), f32[128,2,128]{2,1,0:T(2,128)S(1)}, u32[]{:S(2)}, u32[]{:S(2)}) %all-to-all-start.5) | async-done | bytes 131104 | tf_op jit(solution)/shard_map/reduced/all_to_all | solution.py:25
  127.5 0.6 last.1
  (1 shorter events, 0.0 us)
Async XLA Ops:
  18.2 20.9 %all-to-all-start.1 = ((f32[32,4,384]{2,1,0:T(4,128)}), f32[32,4,384]{2,1,0:T(4,128)}, u32[]{:S(2)}, u32[]{:S(2)}) async-start(f32[32,4,384]{2,1,0:T(4,128)} %get-tuple-element.7), calls=%async_computation.1 | async-start | bytes 393216 | tf_op jit(solution)/shard_map/gram/all_to_all | solution.py:25
  28.3 27.5 %copy-start = (f32[192,256]{1,0:T(8,128)S(1)}, f32[192,256]{1,0:T(8,128)}, u32[]{:S(2)}) copy-start(f32[192,256]{1,0:T(8,128)} %get-tuple-element.8.refs_0_) | copy-start | bytes 589828
  28.3 27.4 %collective-permute-start = (f32[192,256]{1,0:T(8,128)}, f32[192,256]{1,0:T(8,128)S(1)}, u32[]{:S(2)}, u32[]{:S(2)}) collective-permute-start(f32[192,256]{1,0:T(8,128)} %get-tuple-element.8.refs_0_), channel_id=1, source_target_pairs={{0,1},{1,2},{2,3},{3,0},{4,5},{5,6},{6,7},{7,4},{8,9},{9,10},{10,1... | collective-permute-start | bytes 589832 | tf_op jit(solution)/shard_map/gather/ppermute | solution.py:30
  31.7 24.0 %collective-permute-start.1 = (f32[192,256]{1,0:T(8,128)}, f32[192,256]{1,0:T(8,128)}, u32[]{:S(2)}, u32[]{:S(2)}) collective-permute-start(f32[192,256]{1,0:T(8,128)} %get-tuple-element.8.refs_0_), channel_id=1, source_target_pairs={{0,2},{1,3},{2,0},{3,1},{4,6},{5,7},{6,4},{7,5},{8,10},{9,11},{10,... | collective-permute-start | bytes 589832 | tf_op jit(solution)/shard_map/gather/ppermute | solution.py:30
  36.0 19.7 %collective-permute-start.2 = (f32[192,256]{1,0:T(8,128)}, f32[192,256]{1,0:T(8,128)}, u32[]{:S(2)}, u32[]{:S(2)}) collective-permute-start(f32[192,256]{1,0:T(8,128)} %get-tuple-element.8.refs_0_), channel_id=1, source_target_pairs={{0,3},{1,0},{2,1},{3,2},{4,7},{5,4},{6,5},{7,6},{8,11},{9,8},{10,9... | collective-permute-start | bytes 589832 | tf_op jit(solution)/shard_map/gather/ppermute | solution.py:30
  40.8 26.9 %all-to-all-start.2 = ((f32[16,4,384]{2,1,0:T(4,128)}), f32[16,4,384]{2,1,0:T(4,128)}, u32[]{:S(2)}, u32[]{:S(2)}) async-start(f32[16,4,384]{2,1,0:T(4,128)} %tile.2), calls=%async_computation.2 | async-start | bytes 196608 | tf_op jit(solution)/shard_map/gram/all_to_all | solution.py:25
  58.5 18.1 %collective-permute-start.3 = (f32[8,256,128]{2,1,0:T(8,128)}, f32[8,256,128]{2,1,0:T(8,128)}, u32[]{:S(2)}, u32[]{:S(2)}) collective-permute-start(f32[8,256,128]{2,1,0:T(8,128)} %moment.2), channel_id=1, source_target_pairs={{0,4},{4,0},{1,5},{5,1},{2,6},{6,2},{3,7},{7,3},{8,12},{12,8},{9,1... | collective-permute-start | bytes 3145736 | tf_op jit(solution)/shard_map/moment/ppermute | solution.py:296
  69.2 15.5 %all-to-all-start.3 = ((f32[32,4,384]{2,1,0:T(4,128)}), f32[32,4,384]{2,1,0:T(4,128)}, u32[]{:S(2)}, u32[]{:S(2)}) async-start(f32[32,4,384]{2,1,0:T(4,128)} %tile.3), calls=%async_computation.3 | async-start | bytes 393216 | tf_op jit(solution)/shard_map/gram/all_to_all | solution.py:25
  84.8 18.5 %all-to-all-start.4 = ((f32[8,256,128]{2,1,0:T(8,128)}), f32[8,256,128]{2,1,0:T(8,128)S(1)}, u32[]{:S(2)}, u32[]{:S(2)}) async-start(f32[8,256,128]{2,1,0:T(8,128)} %moment.3), calls=%async_computation.4 | async-start | bytes 2097152 | tf_op jit(solution)/shard_map/moment/all_to_all | solution.py:25
  104.3 23.2 %all-to-all-start.5 = ((f32[128,2,128]{2,1,0:T(2,128)}), f32[128,2,128]{2,1,0:T(2,128)S(1)}, u32[]{:S(2)}, u32[]{:S(2)}) async-start(f32[128,2,128]{2,1,0:T(2,128)} %solve.1), calls=%async_computation.5 | async-start | bytes 262144 | tf_op jit(solution)/shard_map/reduced/all_to_all | solution.py:25

commit v12 on v11

--- a/solution.py
+++ b/solution.py
@@ -289,6 +289,7 @@
 
     with jax.named_scope("gather"):
         blocks = [own] + [shifted(own, "y", k) for k in range(1, GROUPS)]
+        blocks = [pltpu.with_memory_space_constraint(b, pltpu.HBM) for b in blocks]
 
     with jax.named_scope("moment"):
         count = pairs * xs

time: 129 us -> 127 us (0.984)
  Pallas kernels: 28.1 us -> 25.9 us
    pallas_call x7, Pallas kernels: 19.2 us -> 16.6 us  [call(): pl.pallas_call(kernel, out_shape=outs, in_specs=[smem if a.ndim == 1 else...]
  transfers between devices with their start and end apart: 9 -> 9, of which waited for: 4 -> 4; matrix products, arithmetic and copies ran while one was open for 0% -> 0% of each run, Pallas kernels for 17% -> 16%
where the time goes in v12:
time: 127 us
  starting transfers between devices  57.4 us (45%)
  waiting for transfers between devices  28.4 us (22%)
  Pallas kernels  25.9 us (20%)
  blocking collectives  13.2 us (10%)
    all_to_all x5, starting transfers between devices, exchange(): return lax.all_to_all(blocks, axes, 0, 0)  43.4 us
    all_to_all x5, waiting for transfers between devices, exchange(): return lax.all_to_all(blocks, axes, 0, 0)  28.4 us
    pallas_call x7, Pallas kernels, call(): pl.pallas_call(kernel, out_shape=outs, in_specs=[smem if a.ndim == 1 else...  16.6 us
    all_to_all x1, blocking collectives, exchange(): return lax.all_to_all(blocks, axes, 0, 0)  13.2 us
    ppermute x3, starting transfers between devices, shifted(): lax.ppermute(value, axis, [(i, (i + by) % count) for i in range(count)])  10.7 us
    pallas_call x2, Pallas kernels, moment_blocks(): pl.pallas_call(moment_kernel, out_shape=far(count, rank, width), in_specs...  6.14 us
    ppermute x1, starting transfers between devices, on_device(): away = lax.ppermute(away, 'core', [(0, 1), (1, 0)])  3.37 us
    pallas_call x1, Pallas kernels, sketch_blocks(): pl.pallas_call(sketch_kernel, out_shape=[f32(blocks, rows // blocks, rank...  3.18 us
  transfers between devices with their start and end apart: 9, of which 4 were waited for; matrix products, arithmetic and copies ran while one was open for 0% of the time, Pallas kernels for 16%

profile of v12, /device:TPU:1, one launch (start us, length us, event | category | flops | bytes accessed | tf_op | source)
XLA Modules:
  0.0 126.5 jit_solution(11929678606259752773)
XLA Ops:
  0.6 3.2 %sketch.1 = (f32[4,192,256]{2,1,0:T(8,128)S(1)}, bf16[768,2048]{1,0:T(8,128)(2,1)S(1)}) custom-call(bf16[768,2048]{1,0:T(8,128)(2,1)} %gradients.1, bf16[2048,256]{1,0:T(8,128)(2,1)} %projection.1), custom_call_target="tpu_custom_call" | custom-call | flops 805306368 | bytes 4194304 | tf_op jit(solution)/shard_map/sketch/sketch/pallas_call | solution.py:182
  3.8 13.2 %all_to_all.30.parts = f32[4,192,256]{2,1,0:T(8,128)S(1)} all-to-all(f32[4,192,256]{2,1,0:T(8,128)S(1)} %get-tuple-element.6), channel_id=1, replica_groups=mesh['far'=8,'pair'=2,'x'=4,'core'=2,'y'=4] {'y'}, dimensions={0} | all-to-all | bytes 1572864 | tf_op jit(solution)/shard_map/sketch/all_to_all | solution.py:25
  17.0 1.2 gram.1
  18.2 10.0 %all-to-all-start.1 = ((f32[32,4,384]{2,1,0:T(4,128)}), f32[32,4,384]{2,1,0:T(4,128)S(1)}, u32[]{:S(2)}, u32[]{:S(2)}) async-start(f32[32,4,384]{2,1,0:T(4,128)} %get-tuple-element.7), calls=%async_computation.1 | async-start | bytes 393216 | tf_op jit(solution)/shard_map/gram/all_to_all | solution.py:25
  28.2 0.1 pad_add_fusion.1.place
  28.2 3.3 %collective-permute-start = (f32[192,256]{1,0:T(8,128)}, f32[192,256]{1,0:T(8,128)S(1)}, u32[]{:S(2)}, u32[]{:S(2)}) collective-permute-start(f32[192,256]{1,0:T(8,128)} %get-tuple-element.8.refs_0_), channel_id=1, source_target_pairs={{0,1},{1,2},{2,3},{3,0},{4,5},{5,6},{6,7},{7,4},{8,9},{9,10},{10,1... | collective-permute-start | bytes 589832 | tf_op jit(solution)/shard_map/gather/ppermute | solution.py:30
  31.5 4.3 %collective-permute-start.1 = (f32[192,256]{1,0:T(8,128)}, f32[192,256]{1,0:T(8,128)}, u32[]{:S(2)}, u32[]{:S(2)}) collective-permute-start(f32[192,256]{1,0:T(8,128)} %get-tuple-element.8.refs_0_), channel_id=1, source_target_pairs={{0,2},{1,3},{2,0},{3,1},{4,6},{5,7},{6,4},{7,5},{8,10},{9,11},{10,... | collective-permute-start | bytes 589832 | tf_op jit(solution)/shard_map/gather/ppermute | solution.py:30
  35.8 3.1 %collective-permute-start.2 = (f32[192,256]{1,0:T(8,128)}, f32[192,256]{1,0:T(8,128)}, u32[]{:S(2)}, u32[]{:S(2)}) collective-permute-start(f32[192,256]{1,0:T(8,128)} %get-tuple-element.8.refs_0_), channel_id=1, source_target_pairs={{0,3},{1,0},{2,1},{3,2},{4,7},{5,4},{6,5},{7,6},{8,11},{9,8},{10,9... | collective-permute-start | bytes 589832 | tf_op jit(solution)/shard_map/gather/ppermute | solution.py:30
  38.9 0.0 all-to-all-done.1.parts
  38.9 0.7 tile.2
  39.6 14.9 %all-to-all-start.2 = ((f32[16,4,384]{2,1,0:T(4,128)}), f32[16,4,384]{2,1,0:T(4,128)S(1)}, u32[]{:S(2)}, u32[]{:S(2)}) async-start(f32[16,4,384]{2,1,0:T(4,128)} %tile.2), calls=%async_computation.2 | async-start | bytes 196608 | tf_op jit(solution)/shard_map/gram/all_to_all | solution.py:25
  54.6 0.0 collective-permute-done.refs_1_
  54.6 0.0 collective-permute-done.1.refs_2_
  54.6 0.0 collective-permute-done.2.refs_3_
  54.6 0.6 copy-done
  55.2 2.9 %moment.2 = f32[8,256,128]{2,1,0:T(8,128)} custom-call(s32[2]{0:T(128)S(1)} %pad_add_fusion.1.place, bf16[768,2048]{1,0:T(8,128)(2,1)S(1)} %get-tuple-element.9.gradients, f32[192,256]{1,0:T(8,128)} %get-tuple-element.8.refs_0_, f32[192,256]{1,0:T(8,128)} %copy-done, f32[192,256]{1,0:T(8,128)} %collective-permute-done.1.refs_2_, ...), custom_call_target="tpu_custom_call" | custom-call | flops 30000001024 | bytes 2621440 | tf_op jit(solution)/shard_map/moment/moment/pallas_call | solution.py:231
  58.1 3.4 %collective-permute-start.3 = (f32[8,256,128]{2,1,0:T(8,128)}, f32[8,256,128]{2,1,0:T(8,128)}, u32[]{:S(2)}, u32[]{:S(2)}) collective-permute-start(f32[8,256,128]{2,1,0:T(8,128)} %moment.2), channel_id=1, source_target_pairs={{0,4},{4,0},{1,5},{5,1},{2,6},{6,2},{3,7},{7,3},{8,12},{12,8},{9,1... | collective-permute-start | bytes 3145736 | tf_op jit(solution)/shard_map/moment/ppermute | solution.py:297
  61.5 4.9 %all-to-all-done.2.parts = f32[16,4,384]{2,1,0:T(4,128)S(1)} async-done(((f32[16,4,384]{2,1,0:T(4,128)}), f32[16,4,384]{2,1,0:T(4,128)S(1)}, u32[]{:S(2)}, u32[]{:S(2)}) %all-to-all-start.2) | async-done | bytes 98336 | tf_op jit(solution)/shard_map/gram/all_to_all | solution.py:25
  66.4 0.7 tile.3
  67.1 7.2 %all-to-all-start.3 = ((f32[32,4,384]{2,1,0:T(4,128)}), f32[32,4,384]{2,1,0:T(4,128)S(1)}, u32[]{:S(2)}, u32[]{:S(2)}) async-start(f32[32,4,384]{2,1,0:T(4,128)} %tile.3), calls=%async_computation.3 | async-start | bytes 393216 | tf_op jit(solution)/shard_map/gram/all_to_all | solution.py:25
  74.4 0.1 pad_add_fusion.place
  74.4 0.0 collective-permute-done.3.refs_4_
  74.4 3.3 %moment.3 = f32[8,256,128]{2,1,0:T(8,128)} custom-call(s32[2]{0:T(128)S(1)} %pad_add_fusion.place, bf16[768,2048]{1,0:T(8,128)(2,1)S(1)} %get-tuple-element.9.gradients, f32[192,256]{1,0:T(8,128)} %get-tuple-element.8.refs_0_, f32[192,256]{1,0:T(8,128)} %copy-done, f32[192,256]{1,0:T(8,128)} %collective-permute-done.1.refs_2_, ...), custom_call_target="tpu_custom_call" | custom-call | flops 1000000000 | bytes 2621440 | tf_op jit(solution)/shard_map/moment/moment/pallas_call | solution.py:231
  77.7 4.8 %all-to-all-done.3.shares = f32[32,4,384]{2,1,0:T(4,128)S(1)} async-done(((f32[32,4,384]{2,1,0:T(4,128)}), f32[32,4,384]{2,1,0:T(4,128)S(1)}, u32[]{:S(2)}, u32[]{:S(2)}) %all-to-all-start.3) | async-done | bytes 196640 | tf_op jit(solution)/shard_map/gram/all_to_all | solution.py:25
  82.5 3.6 %all-to-all-start.4 = ((f32[8,256,128]{2,1,0:T(8,128)}), f32[8,256,128]{2,1,0:T(8,128)S(1)}, u32[]{:S(2)}, u32[]{:S(2)}) async-start(f32[8,256,128]{2,1,0:T(8,128)} %moment.3), calls=%async_computation.4 | async-start | bytes 2097152 | tf_op jit(solution)/shard_map/moment/all_to_all | solution.py:25
  86.1 9.0 %factor.1.inverse = f32[256,256]{1,0:T(8,128)S(1)} custom-call(f32[32,4,384]{2,1,0:T(4,128)S(1)} %all-to-all-done.3.shares), custom_call_target="tpu_custom_call" | custom-call | flops 10000000000 | bytes 458752 | tf_op jit(solution)/shard_map/factor/factor/pallas_call | solution.py:87
  95.1 5.9 %all-to-all-done.4.parts = f32[8,256,128]{2,1,0:T(8,128)S(1)} async-done(((f32[8,256,128]{2,1,0:T(8,128)}), f32[8,256,128]{2,1,0:T(8,128)S(1)}, u32[]{:S(2)}, u32[]{:S(2)}) %all-to-all-start.4) | async-done | bytes 1048608 | tf_op jit(solution)/shard_map/moment/all_to_all | solution.py:25
  101.0 1.1 solve.1
  102.1 7.7 %all-to-all-start.5 = ((f32[128,2,128]{2,1,0:T(2,128)}), f32[128,2,128]{2,1,0:T(2,128)S(1)}, u32[]{:S(2)}, u32[]{:S(2)}) async-start(f32[128,2,128]{2,1,0:T(2,128)} %solve.1), calls=%async_computation.5 | async-start | bytes 262144 | tf_op jit(solution)/shard_map/reduced/all_to_all | solution.py:25
  109.8 3.3 %basis.1 = f32[768,256]{1,0:T(8,128)} custom-call(s32[1]{0:T(128)} %bitcast.place, f32[256,256]{1,0:T(8,128)S(1)} %factor.1.inverse, f32[192,256]{1,0:T(8,128)} %get-tuple-element.8.refs_0_, f32[192,256]{1,0:T(8,128)} %copy-done, f32[192,256]{1,0:T(8,128)} %collective-permute-done.1.refs_2_, f32[192,256]{1,0:T(8,128)} %collective-permute-done.2.refs_3_), custom_call_target="tpu_custom_call" | custom-call | flops 603979776 | bytes 1835012 | tf_op jit(solution)/shard_map/basis/basis/pallas_call | solution.py:87
  113.1 12.8 %all-to-all-done.5.parts = f32[128,2,128]{2,1,0:T(2,128)S(1)} async-done(((f32[128,2,128]{2,1,0:T(2,128)}), f32[128,2,128]{2,1,0:T(2,128)S(1)}, u32[]{:S(2)}, u32[]{:S(2)}) %all-to-all-start.5) | async-done | bytes 131104 | tf_op jit(solution)/shard_map/reduced/all_to_all | solution.py:25
  125.9 0.6 last.1
  (1 shorter events, 0.0 us)
Async XLA Ops:
  18.2 20.8 %all-to-all-start.1 = ((f32[32,4,384]{2,1,0:T(4,128)}), f32[32,4,384]{2,1,0:T(4,128)S(1)}, u32[]{:S(2)}, u32[]{:S(2)}) async-start(f32[32,4,384]{2,1,0:T(4,128)} %get-tuple-element.7), calls=%async_computation.1 | async-start | bytes 393216 | tf_op jit(solution)/shard_map/gram/all_to_all | solution.py:25
  28.2 26.3 %collective-permute-start = (f32[192,256]{1,0:T(8,128)}, f32[192,256]{1,0:T(8,128)S(1)}, u32[]{:S(2)}, u32[]{:S(2)}) collective-permute-start(f32[192,256]{1,0:T(8,128)} %get-tuple-element.8.refs_0_), channel_id=1, source_target_pairs={{0,1},{1,2},{2,3},{3,0},{4,5},{5,6},{6,7},{7,4},{8,9},{9,10},{10,1... | collective-permute-start | bytes 589832 | tf_op jit(solution)/shard_map/gather/ppermute | solution.py:30
  31.5 23.1 %collective-permute-start.1 = (f32[192,256]{1,0:T(8,128)}, f32[192,256]{1,0:T(8,128)}, u32[]{:S(2)}, u32[]{:S(2)}) collective-permute-start(f32[192,256]{1,0:T(8,128)} %get-tuple-element.8.refs_0_), channel_id=1, source_target_pairs={{0,2},{1,3},{2,0},{3,1},{4,6},{5,7},{6,4},{7,5},{8,10},{9,11},{10,... | collective-permute-start | bytes 589832 | tf_op jit(solution)/shard_map/gather/ppermute | solution.py:30
  35.8 18.8 %collective-permute-start.2 = (f32[192,256]{1,0:T(8,128)}, f32[192,256]{1,0:T(8,128)}, u32[]{:S(2)}, u32[]{:S(2)}) collective-permute-start(f32[192,256]{1,0:T(8,128)} %get-tuple-element.8.refs_0_), channel_id=1, source_target_pairs={{0,3},{1,0},{2,1},{3,2},{4,7},{5,4},{6,5},{7,6},{8,11},{9,8},{10,9... | collective-permute-start | bytes 589832 | tf_op jit(solution)/shard_map/gather/ppermute | solution.py:30
  39.6 26.8 %all-to-all-start.2 = ((f32[16,4,384]{2,1,0:T(4,128)}), f32[16,4,384]{2,1,0:T(4,128)S(1)}, u32[]{:S(2)}, u32[]{:S(2)}) async-start(f32[16,4,384]{2,1,0:T(4,128)} %tile.2), calls=%async_computation.2 | async-start | bytes 196608 | tf_op jit(solution)/shard_map/gram/all_to_all | solution.py:25
  54.6 0.7 copy-start
  58.1 16.3 %collective-permute-start.3 = (f32[8,256,128]{2,1,0:T(8,128)}, f32[8,256,128]{2,1,0:T(8,128)}, u32[]{:S(2)}, u32[]{:S(2)}) collective-permute-start(f32[8,256,128]{2,1,0:T(8,128)} %moment.2), channel_id=1, source_target_pairs={{0,4},{4,0},{1,5},{5,1},{2,6},{6,2},{3,7},{7,3},{8,12},{12,8},{9,1... | collective-permute-start | bytes 3145736 | tf_op jit(solution)/shard_map/moment/ppermute | solution.py:297
  67.1 15.4 %all-to-all-start.3 = ((f32[32,4,384]{2,1,0:T(4,128)}), f32[32,4,384]{2,1,0:T(4,128)S(1)}, u32[]{:S(2)}, u32[]{:S(2)}) async-start(f32[32,4,384]{2,1,0:T(4,128)} %tile.3), calls=%async_computation.3 | async-start | bytes 393216 | tf_op jit(solution)/shard_map/gram/all_to_all | solution.py:25
  82.5 18.5 %all-to-all-start.4 = ((f32[8,256,128]{2,1,0:T(8,128)}), f32[8,256,128]{2,1,0:T(8,128)S(1)}, u32[]{:S(2)}, u32[]{:S(2)}) async-start(f32[8,256,128]{2,1,0:T(8,128)} %moment.3), calls=%async_computation.4 | async-start | bytes 2097152 | tf_op jit(solution)/shard_map/moment/all_to_all | solution.py:25
  102.1 23.8 %all-to-all-start.5 = ((f32[128,2,128]{2,1,0:T(2,128)}), f32[128,2,128]{2,1,0:T(2,128)S(1)}, u32[]{:S(2)}, u32[]{:S(2)}) async-start(f32[128,2,128]{2,1,0:T(2,128)} %solve.1), calls=%async_computation.5 | async-start | bytes 262144 | tf_op jit(solution)/shard_map/reduced/all_to_all | solution.py:25

commit v13 on v7

--- a/solution.py
+++ b/solution.py
@@ -15,7 +15,7 @@
 CROSS = ("pair", "x")
 NEAR = ("x", "core", "y")
 GROUPS = 4
-PIECES = 4
+PIECES = 8
 PANEL = 8
 SHORT = 3 * 10**10
 VMEM_LIMIT = 8 * 1024 * 1024

time: 127 us -> 127 us (level)
  no operation moved by 1% of the time
where the time goes in v13:
time: 127 us
  starting transfers between devices  57.5 us (45%)
  waiting for transfers between devices  28.4 us (22%)
  Pallas kernels  25.3 us (20%)
  blocking collectives  13.2 us (10%)
  local copies, waits for them, and re-layouts  1.29 us (1%)
    all_to_all x5, starting transfers between devices, exchange(): return lax.all_to_all(blocks, axes, 0, 0)  43.4 us
    all_to_all x5, waiting for transfers between devices, exchange(): return lax.all_to_all(blocks, axes, 0, 0)  28.4 us
    pallas_call x6, Pallas kernels, call(): pl.pallas_call(kernel, out_shape=outs, in_specs=[smem if a.ndim == 1 else...  15.9 us
    all_to_all x1, blocking collectives, exchange(): return lax.all_to_all(blocks, axes, 0, 0)  13.2 us
    ppermute x3, starting transfers between devices, shifted(): lax.ppermute(value, axis, [(i, (i + by) % count) for i in range(count)])  10.7 us
    pallas_call x2, Pallas kernels, moment_blocks(): pl.pallas_call(moment_kernel, out_shape=far(count, rank, width), in_specs...  6.15 us
    ppermute x1, starting transfers between devices, on_device(): away = lax.ppermute(away, 'core', [(0, 1), (1, 0)])  3.38 us
    pallas_call x1, Pallas kernels, sketch_blocks(): pl.pallas_call(sketch_kernel, out_shape=[f32(blocks, rows // blocks, rank...  3.2 us
  transfers between devices with their start and end apart: 9, of which 4 were waited for; matrix products, arithmetic and copies ran while one was open for 0% of the time, Pallas kernels for 16%

profile of v13, /device:TPU:1, one launch (start us, length us, event | category | flops | bytes accessed | tf_op | source)
XLA Modules:
  0.0 126.6 jit_solution(13110147712738961652)
XLA Ops:
  0.6 3.2 %sketch.1 = (f32[4,192,256]{2,1,0:T(8,128)S(1)}, bf16[768,2048]{1,0:T(8,128)(2,1)S(1)}) custom-call(bf16[768,2048]{1,0:T(8,128)(2,1)} %gradients.1, bf16[2048,256]{1,0:T(8,128)(2,1)} %projection.1), custom_call_target="tpu_custom_call" | custom-call | flops 805306368 | bytes 4194304 | tf_op jit(solution)/shard_map/sketch/sketch/pallas_call | solution.py:172
  3.8 13.2 %all_to_all.30.parts = f32[4,192,256]{2,1,0:T(8,128)S(1)} all-to-all(f32[4,192,256]{2,1,0:T(8,128)S(1)} %get-tuple-element.6), channel_id=1, replica_groups=mesh['far'=8,'pair'=2,'x'=4,'core'=2,'y'=4] {'y'}, dimensions={0} | all-to-all | bytes 1572864 | tf_op jit(solution)/shard_map/sketch/all_to_all | solution.py:25
  17.0 1.2 gram.1
  18.2 10.0 %all-to-all-start.1 = ((f32[32,4,384]{2,1,0:T(4,128)}), f32[32,4,384]{2,1,0:T(4,128)S(1)}, u32[]{:S(2)}, u32[]{:S(2)}) async-start(f32[32,4,384]{2,1,0:T(4,128)} %get-tuple-element.7), calls=%async_computation.1 | async-start | bytes 393216 | tf_op jit(solution)/shard_map/gram/all_to_all | solution.py:25
  28.2 0.1 pad_add_fusion.1.place
  28.3 3.3 %collective-permute-start = (f32[192,256]{1,0:T(8,128)}, f32[192,256]{1,0:T(8,128)S(1)}, u32[]{:S(2)}, u32[]{:S(2)}) collective-permute-start(f32[192,256]{1,0:T(8,128)} %get-tuple-element.8.refs_0_), channel_id=1, source_target_pairs={{0,1},{1,2},{2,3},{3,0},{4,5},{5,6},{6,7},{7,4},{8,9},{9,10},{10,1... | collective-permute-start | bytes 589832 | tf_op jit(solution)/shard_map/gather/ppermute | solution.py:30
  31.5 4.3 %collective-permute-start.1 = (f32[192,256]{1,0:T(8,128)}, f32[192,256]{1,0:T(8,128)}, u32[]{:S(2)}, u32[]{:S(2)}) collective-permute-start(f32[192,256]{1,0:T(8,128)} %get-tuple-element.8.refs_0_), channel_id=1, source_target_pairs={{0,2},{1,3},{2,0},{3,1},{4,6},{5,7},{6,4},{7,5},{8,10},{9,11},{10,... | collective-permute-start | bytes 589832 | tf_op jit(solution)/shard_map/gather/ppermute | solution.py:30
  35.9 3.1 %collective-permute-start.2 = (f32[192,256]{1,0:T(8,128)}, f32[192,256]{1,0:T(8,128)}, u32[]{:S(2)}, u32[]{:S(2)}) collective-permute-start(f32[192,256]{1,0:T(8,128)} %get-tuple-element.8.refs_0_), channel_id=1, source_target_pairs={{0,3},{1,0},{2,1},{3,2},{4,7},{5,4},{6,5},{7,6},{8,11},{9,8},{10,9... | collective-permute-start | bytes 589832 | tf_op jit(solution)/shard_map/gather/ppermute | solution.py:30
  39.0 0.0 all-to-all-done.1.parts
  39.0 0.7 tile.2
  39.7 14.9 %all-to-all-start.2 = ((f32[16,4,384]{2,1,0:T(4,128)}), f32[16,4,384]{2,1,0:T(4,128)S(1)}, u32[]{:S(2)}, u32[]{:S(2)}) async-start(f32[16,4,384]{2,1,0:T(4,128)} %tile.2), calls=%async_computation.2 | async-start | bytes 196608 | tf_op jit(solution)/shard_map/gram/all_to_all | solution.py:25
  54.6 0.0 collective-permute-done.refs_1_
  54.6 0.0 collective-permute-done.1.refs_2_
  54.6 0.0 collective-permute-done.2.refs_3_
  54.6 0.7 copy-done
  55.3 2.9 %moment.2 = f32[8,256,128]{2,1,0:T(8,128)} custom-call(s32[2]{0:T(128)S(1)} %pad_add_fusion.1.place, bf16[768,2048]{1,0:T(8,128)(2,1)S(1)} %get-tuple-element.9.gradients, f32[192,256]{1,0:T(8,128)} %get-tuple-element.8.refs_0_, f32[192,256]{1,0:T(8,128)} %copy-done, f32[192,256]{1,0:T(8,128)} %collective-permute-done.1.refs_2_, ...), custom_call_target="tpu_custom_call" | custom-call | flops 30000001024 | bytes 2621440 | tf_op jit(solution)/shard_map/moment/moment/pallas_call | solution.py:221
  58.2 3.4 %collective-permute-start.3 = (f32[8,256,128]{2,1,0:T(8,128)}, f32[8,256,128]{2,1,0:T(8,128)}, u32[]{:S(2)}, u32[]{:S(2)}) collective-permute-start(f32[8,256,128]{2,1,0:T(8,128)} %moment.2), channel_id=1, source_target_pairs={{0,4},{4,0},{1,5},{5,1},{2,6},{6,2},{3,7},{7,3},{8,12},{12,8},{9,1... | collective-permute-start | bytes 3145736 | tf_op jit(solution)/shard_map/moment/ppermute | solution.py:287
  61.6 4.9 %all-to-all-done.2.parts = f32[16,4,384]{2,1,0:T(4,128)S(1)} async-done(((f32[16,4,384]{2,1,0:T(4,128)}), f32[16,4,384]{2,1,0:T(4,128)S(1)}, u32[]{:S(2)}, u32[]{:S(2)}) %all-to-all-start.2) | async-done | bytes 98336 | tf_op jit(solution)/shard_map/gram/all_to_all | solution.py:25
  66.4 0.7 tile.3
  67.1 7.2 %all-to-all-start.3 = ((f32[32,4,384]{2,1,0:T(4,128)}), f32[32,4,384]{2,1,0:T(4,128)S(1)}, u32[]{:S(2)}, u32[]{:S(2)}) async-start(f32[32,4,384]{2,1,0:T(4,128)} %tile.3), calls=%async_computation.3 | async-start | bytes 393216 | tf_op jit(solution)/shard_map/gram/all_to_all | solution.py:25
  74.4 0.1 pad_add_fusion.place
  74.4 0.0 collective-permute-done.3.refs_4_
  74.4 3.3 %moment.3 = f32[8,256,128]{2,1,0:T(8,128)} custom-call(s32[2]{0:T(128)S(1)} %pad_add_fusion.place, bf16[768,2048]{1,0:T(8,128)(2,1)S(1)} %get-tuple-element.9.gradients, f32[192,256]{1,0:T(8,128)} %get-tuple-element.8.refs_0_, f32[192,256]{1,0:T(8,128)} %copy-done, f32[192,256]{1,0:T(8,128)} %collective-permute-done.1.refs_2_, ...), custom_call_target="tpu_custom_call" | custom-call | flops 1000000000 | bytes 2621440 | tf_op jit(solution)/shard_map/moment/moment/pallas_call | solution.py:221
  77.7 4.8 %all-to-all-done.3.shares = f32[32,4,384]{2,1,0:T(4,128)S(1)} async-done(((f32[32,4,384]{2,1,0:T(4,128)}), f32[32,4,384]{2,1,0:T(4,128)S(1)}, u32[]{:S(2)}, u32[]{:S(2)}) %all-to-all-start.3) | async-done | bytes 196640 | tf_op jit(solution)/shard_map/gram/all_to_all | solution.py:25
  82.6 3.6 %all-to-all-start.4 = ((f32[8,256,128]{2,1,0:T(8,128)}), f32[8,256,128]{2,1,0:T(8,128)S(1)}, u32[]{:S(2)}, u32[]{:S(2)}) async-start(f32[8,256,128]{2,1,0:T(8,128)} %moment.3), calls=%async_computation.4 | async-start | bytes 2097152 | tf_op jit(solution)/shard_map/moment/all_to_all | solution.py:25
  86.1 9.0 %factor.1.inverse = f32[256,256]{1,0:T(8,128)S(1)} custom-call(f32[32,4,384]{2,1,0:T(4,128)S(1)} %all-to-all-done.3.shares), custom_call_target="tpu_custom_call" | custom-call | flops 10000000000 | bytes 458752 | tf_op jit(solution)/shard_map/factor/factor/pallas_call | solution.py:86
  95.1 5.9 %all-to-all-done.4.parts = f32[8,256,128]{2,1,0:T(8,128)S(1)} async-done(((f32[8,256,128]{2,1,0:T(8,128)}), f32[8,256,128]{2,1,0:T(8,128)S(1)}, u32[]{:S(2)}, u32[]{:S(2)}) %all-to-all-start.4) | async-done | bytes 1048608 | tf_op jit(solution)/shard_map/moment/all_to_all | solution.py:25
  101.0 1.0 solve.1
  102.1 7.8 %all-to-all-start.5 = ((f32[128,2,128]{2,1,0:T(2,128)}), f32[128,2,128]{2,1,0:T(2,128)S(1)}, u32[]{:S(2)}, u32[]{:S(2)}) async-start(f32[128,2,128]{2,1,0:T(2,128)} %solve.1), calls=%async_computation.5 | async-start | bytes 262144 | tf_op jit(solution)/shard_map/reduced/all_to_all | solution.py:25
  109.8 3.3 %basis.1 = f32[768,256]{1,0:T(8,128)} custom-call(s32[1]{0:T(128)} %bitcast.place, f32[256,256]{1,0:T(8,128)S(1)} %factor.1.inverse, f32[192,256]{1,0:T(8,128)} %get-tuple-element.8.refs_0_, f32[192,256]{1,0:T(8,128)} %copy-done, f32[192,256]{1,0:T(8,128)} %collective-permute-done.1.refs_2_, f32[192,256]{1,0:T(8,128)} %collective-permute-done.2.refs_3_), custom_call_target="tpu_custom_call" | custom-call | flops 603979776 | bytes 1835012 | tf_op jit(solution)/shard_map/basis/basis/pallas_call | solution.py:86
  113.1 12.8 %all-to-all-done.5 = f32[128,2,128]{2,1,0:T(2,128)S(1)} async-done(((f32[128,2,128]{2,1,0:T(2,128)}), f32[128,2,128]{2,1,0:T(2,128)S(1)}, u32[]{:S(2)}, u32[]{:S(2)}) %all-to-all-start.5) | async-done | bytes 131104 | tf_op jit(solution)/shard_map/reduced/all_to_all | solution.py:25
  126.0 0.6 reshape.11
  (3 shorter events, 0.1 us)
Async XLA Ops:
  18.2 20.8 %all-to-all-start.1 = ((f32[32,4,384]{2,1,0:T(4,128)}), f32[32,4,384]{2,1,0:T(4,128)S(1)}, u32[]{:S(2)}, u32[]{:S(2)}) async-start(f32[32,4,384]{2,1,0:T(4,128)} %get-tuple-element.7), calls=%async_computation.1 | async-start | bytes 393216 | tf_op jit(solution)/shard_map/gram/all_to_all | solution.py:25
  28.3 26.3 %collective-permute-start = (f32[192,256]{1,0:T(8,128)}, f32[192,256]{1,0:T(8,128)S(1)}, u32[]{:S(2)}, u32[]{:S(2)}) collective-permute-start(f32[192,256]{1,0:T(8,128)} %get-tuple-element.8.refs_0_), channel_id=1, source_target_pairs={{0,1},{1,2},{2,3},{3,0},{4,5},{5,6},{6,7},{7,4},{8,9},{9,10},{10,1... | collective-permute-start | bytes 589832 | tf_op jit(solution)/shard_map/gather/ppermute | solution.py:30
  31.5 23.1 %collective-permute-start.1 = (f32[192,256]{1,0:T(8,128)}, f32[192,256]{1,0:T(8,128)}, u32[]{:S(2)}, u32[]{:S(2)}) collective-permute-start(f32[192,256]{1,0:T(8,128)} %get-tuple-element.8.refs_0_), channel_id=1, source_target_pairs={{0,2},{1,3},{2,0},{3,1},{4,6},{5,7},{6,4},{7,5},{8,10},{9,11},{10,... | collective-permute-start | bytes 589832 | tf_op jit(solution)/shard_map/gather/ppermute | solution.py:30
  35.9 18.8 %collective-permute-start.2 = (f32[192,256]{1,0:T(8,128)}, f32[192,256]{1,0:T(8,128)}, u32[]{:S(2)}, u32[]{:S(2)}) collective-permute-start(f32[192,256]{1,0:T(8,128)} %get-tuple-element.8.refs_0_), channel_id=1, source_target_pairs={{0,3},{1,0},{2,1},{3,2},{4,7},{5,4},{6,5},{7,6},{8,11},{9,8},{10,9... | collective-permute-start | bytes 589832 | tf_op jit(solution)/shard_map/gather/ppermute | solution.py:30
  39.7 26.8 %all-to-all-start.2 = ((f32[16,4,384]{2,1,0:T(4,128)}), f32[16,4,384]{2,1,0:T(4,128)S(1)}, u32[]{:S(2)}, u32[]{:S(2)}) async-start(f32[16,4,384]{2,1,0:T(4,128)} %tile.2), calls=%async_computation.2 | async-start | bytes 196608 | tf_op jit(solution)/shard_map/gram/all_to_all | solution.py:25
  54.6 0.7 copy-start
  58.2 16.3 %collective-permute-start.3 = (f32[8,256,128]{2,1,0:T(8,128)}, f32[8,256,128]{2,1,0:T(8,128)}, u32[]{:S(2)}, u32[]{:S(2)}) collective-permute-start(f32[8,256,128]{2,1,0:T(8,128)} %moment.2), channel_id=1, source_target_pairs={{0,4},{4,0},{1,5},{5,1},{2,6},{6,2},{3,7},{7,3},{8,12},{12,8},{9,1... | collective-permute-start | bytes 3145736 | tf_op jit(solution)/shard_map/moment/ppermute | solution.py:287
  67.1 15.4 %all-to-all-start.3 = ((f32[32,4,384]{2,1,0:T(4,128)}), f32[32,4,384]{2,1,0:T(4,128)S(1)}, u32[]{:S(2)}, u32[]{:S(2)}) async-start(f32[32,4,384]{2,1,0:T(4,128)} %tile.3), calls=%async_computation.3 | async-start | bytes 393216 | tf_op jit(solution)/shard_map/gram/all_to_all | solution.py:25
  82.6 18.5 %all-to-all-start.4 = ((f32[8,256,128]{2,1,0:T(8,128)}), f32[8,256,128]{2,1,0:T(8,128)S(1)}, u32[]{:S(2)}, u32[]{:S(2)}) async-start(f32[8,256,128]{2,1,0:T(8,128)} %moment.3), calls=%async_computation.4 | async-start | bytes 2097152 | tf_op jit(solution)/shard_map/moment/all_to_all | solution.py:25
  102.1 23.8 %all-to-all-start.5 = ((f32[128,2,128]{2,1,0:T(2,128)}), f32[128,2,128]{2,1,0:T(2,128)S(1)}, u32[]{:S(2)}, u32[]{:S(2)}) async-start(f32[128,2,128]{2,1,0:T(2,128)} %solve.1), calls=%async_computation.5 | async-start | bytes 262144 | tf_op jit(solution)/shard_map/reduced/all_to_all | solution.py:25
